TPU v7x, 32 devices: a whole 2x2x4 slice. The times are simulated.
32 devices in a mesh: groups: 2 (over y), expert: 4 (over z), dp: 4 (over x, core).
Axes of the slice: x: 2, y: 2, z: 4, core: 2. Of those that a mesh axis runs over, the one named last changes fastest.
Arguments:
- tokens: bfloat16 [4096, 2048], P(('groups', 'expert', 'dp')), parts along dimension 0, may hold values from -6 to 6
- out_grad: bfloat16 [4096, 2048], P(('groups', 'expert', 'dp')), parts along dimension 0, may hold values from -18 to 18
- route_weight: bfloat16 [4096, 1], P(('groups', 'expert', 'dp')), parts along dimension 0, may hold values from 0.049804688 to 0.5
- expert_ids: int32 [4096, 1], P(('groups', 'expert', 'dp')), parts along dimension 0, may hold values from 0 to 63; in each aligned block of 128 rows (0 to 127, 128 to 255, ...) at most 4 rows name the same one
- gate_weight: bfloat16 [64, 2048, 768], P('expert', None, 'dp'), may hold values from -0.125 to 0.125
- up_weight: bfloat16 [64, 2048, 768], P('expert', None, 'dp'), may hold values from -0.125 to 0.125
- down_weight: bfloat16 [64, 768, 2048], P('expert', 'dp'), may hold values from -0.21875 to 0.21875
Outputs:
- token_grad: bfloat16 [4096, 2048], P(('groups', 'expert', 'dp')), parts along dimension 0
- route_grad: bfloat16 [4096, 1], P(('groups', 'expert', 'dp')), parts along dimension 0
- down_grad: bfloat16 [128, 768, 2048], P(('groups', 'expert'), 'dp'), parts along dimension 0
There are 2 independent parts, one for each index of `groups`. A program takes and returns all parts, laid end to end along the dimension named above; an argument that names none is the same for every part. Nothing has to cross between parts.
Inputs may be any that keep to these rules, and one draw needn't show every extreme that they name: `expert_ids`: each row names 1 different experts; in the rows of one device no expert is named more than 4 times.
All inputs are finite; a program needn't handle non-finite values.
Results may differ from a plain program's by a relative error of at most 0.013.
Values may be sent and summed in bfloat16 or wider, within the bound.
No kernel may reach another device: no remote copies, remote signals or barrier semaphores. Data moves between devices by JAX's collectives and lax.ppermute only.
A program may use at most 576 MiB of HBM per device.

v0:
```python
import jax
import jax.numpy as jnp
from jax import lax
from jax.sharding import PartitionSpec as P

BLOCK = 128
MOST = 4


def silu_pair(pre_act):
    sigma_val = jax.nn.sigmoid(pre_act)
    return (pre_act * sigma_val, sigma_val * (1.0 + pre_act * (1.0 - sigma_val)))


def expert_block(x_block, cot_block, wgt_block, gate_c, up_c, down_c):
    gate_pre = jnp.dot(x_block, gate_c, preferred_element_type=jnp.float32)
    up_pre = jnp.dot(x_block, up_c, preferred_element_type=jnp.float32)
    act_val, act_slope = silu_pair(gate_pre)
    hidden = (act_val * up_pre).astype(jnp.bfloat16)
    out_part = jnp.dot(hidden, down_c, preferred_element_type=jnp.float32)
    weight_part = jnp.sum(cot_block.astype(jnp.float32) * out_part, axis=1)
    scaled = (wgt_block.astype(jnp.float32)[:, None] * cot_block.astype(jnp.float32)).astype(
        jnp.bfloat16
    )
    hidden_grad = lax.dot_general(
        scaled, down_c, (((1,), (1,)), ((), ())), preferred_element_type=jnp.float32
    )
    down_part = lax.dot_general(
        hidden, scaled, (((0,), (0,)), ((), ())), preferred_element_type=jnp.float32
    )
    gate_back = (hidden_grad * up_pre * act_slope).astype(jnp.bfloat16)
    up_back = (hidden_grad * act_val).astype(jnp.bfloat16)
    input_part = lax.dot_general(
        gate_back, gate_c, (((1,), (1,)), ((), ())), preferred_element_type=jnp.float32
    )
    input_part = input_part + lax.dot_general(
        up_back, up_c, (((1,), (1,)), ((), ())), preferred_element_type=jnp.float32
    )
    return (input_part, weight_part, down_part)


def earlier_count(onehot):
    before = jnp.cumsum(onehot, axis=0) - onehot
    return jnp.sum(before * onehot, axis=1)


def place_routes(ids_block, replicate, n_devices, per_device):
    flat_ids = ids_block.reshape(-1)
    experts = n_devices * per_device
    onehot_exp = (flat_ids[:, None] == jnp.arange(experts, dtype=jnp.int32)[None, :]).astype(
        jnp.int32
    )
    rank_exp = earlier_count(onehot_exp)
    to_helper = jnp.sum(onehot_exp * replicate[None, :], axis=1) * (rank_exp % 2)
    target = (flat_ids // per_device + to_helper * (n_devices // 2)) % n_devices
    copy_index = flat_ids % per_device + to_helper * per_device
    onehot_dev = (target[:, None] == jnp.arange(n_devices, dtype=jnp.int32)[None, :]).astype(
        jnp.int32
    )
    return (target, earlier_count(onehot_dev), copy_index)


def fill_slots(position, tok_flat, cot_flat, wgt_flat, copy_flat, size_rows, top_count):
    n_routes = position.shape[0]
    filler = (
        jnp.full((size_rows,), n_routes, jnp.int32)
        .at[position]
        .set(jnp.arange(n_routes, dtype=jnp.int32))
    )
    token_at = filler // top_count
    zero_row = jnp.zeros((1, tok_flat.shape[1]), jnp.bfloat16)
    tok_rows = jnp.concatenate([tok_flat, zero_row])[token_at]
    cot_rows = jnp.concatenate([cot_flat, zero_row])[token_at]
    wgt_rows = jnp.concatenate([wgt_flat, jnp.zeros((1,), jnp.bfloat16)])[filler]
    tag_rows = jnp.concatenate([copy_flat + 1, jnp.zeros((1,), jnp.int32)])[filler].astype(
        jnp.bfloat16
    )
    return (tok_rows, cot_rows, wgt_rows, tag_rows)


def run_copies(x_rows, cot_rows, wgt_rows, tag_rows, gate_all, up_all, down_all):
    row_count, model_width = x_rows.shape
    copies = gate_all.shape[0]
    block_rows = BLOCK
    onehot_copy = (tag_rows[:, None] == jnp.arange(1, copies + 1, dtype=jnp.int32)[None, :]).astype(
        jnp.int32
    )
    counts = jnp.sum(onehot_copy, axis=0)
    padded = (counts + block_rows - 1) // block_rows * block_rows
    offsets = jnp.cumsum(padded) - padded
    copy_ends = offsets + padded
    rank_copy = earlier_count(onehot_copy)
    total_blocks = (row_count + block_rows - 1) // block_rows + copies
    capacity = total_blocks * block_rows
    packed_at = jnp.sum(onehot_copy * (offsets[None, :] + rank_copy[:, None]), axis=1)
    packed_at = jnp.where(tag_rows > 0, packed_at, capacity)
    source = (
        jnp.full((capacity + 1,), row_count, jnp.int32)
        .at[packed_at]
        .set(jnp.arange(row_count, dtype=jnp.int32))[:capacity]
    )
    zero_row = jnp.zeros((1, model_width), jnp.bfloat16)
    x_pack = jnp.concatenate([x_rows, zero_row])[source]
    cot_pack = jnp.concatenate([cot_rows, zero_row])[source]
    wgt_pack = jnp.concatenate([wgt_rows, jnp.zeros((1,), jnp.bfloat16)])[source]
    n_blocks = jnp.sum(padded) // block_rows
    hidden_width = down_all.shape[1]

    def one_block(carry, block_index):
        row_start = block_index * block_rows
        copy_pick = jnp.sum((copy_ends <= row_start).astype(jnp.int32))

        def working(operand):
            gate_c = lax.dynamic_index_in_dim(gate_all, copy_pick, 0, keepdims=False)
            up_c = lax.dynamic_index_in_dim(up_all, copy_pick, 0, keepdims=False)
            down_c = lax.dynamic_index_in_dim(down_all, copy_pick, 0, keepdims=False)
            x_block = lax.dynamic_slice_in_dim(x_pack, row_start, block_rows)
            cot_block = lax.dynamic_slice_in_dim(cot_pack, row_start, block_rows)
            wgt_block = lax.dynamic_slice_in_dim(wgt_pack, row_start, block_rows)
            return expert_block(x_block, cot_block, wgt_block, gate_c, up_c, down_c)

        def skipped(operand):
            return (
                jnp.zeros((block_rows, model_width), jnp.float32),
                jnp.zeros((block_rows,), jnp.float32),
                jnp.zeros((hidden_width, model_width), jnp.float32),
            )

        parts = lax.cond(block_index < n_blocks, working, skipped, 0)
        return (carry, (parts[0], parts[1], parts[2], copy_pick))

    unused, stacked = lax.scan(
        one_block, jnp.zeros((), jnp.int32), jnp.arange(total_blocks, dtype=jnp.int32)
    )
    input_blocks, weight_blocks, down_blocks, picks = stacked
    input_acc = input_blocks.reshape(capacity, model_width)
    weight_acc = weight_blocks.reshape(capacity)
    pick_table = (picks[:, None] == jnp.arange(copies, dtype=jnp.int32)[None, :]).astype(
        jnp.float32
    )
    down_acc = jnp.einsum("bc,bfd->cfd", pick_table, down_blocks, precision=lax.Precision.HIGHEST)
    input_rows = jnp.concatenate([input_acc, jnp.zeros((1, model_width), jnp.float32)])[packed_at]
    weight_rows = jnp.concatenate([weight_acc, jnp.zeros((1,), jnp.float32)])[packed_at]
    return (input_rows, weight_rows, down_acc)


def shards(tokens, out_grad, route_weight, expert_ids, gate_weight, up_weight, down_weight):
    n_devices = lax.axis_size("expert")
    n_data = lax.axis_size("dp")
    per_device = gate_weight.shape[0]
    tok_dev, top_count = expert_ids.shape
    model_width = tokens.shape[1]
    n_routes = tok_dev * top_count
    experts = n_devices * per_device
    replicate = jnp.zeros((experts,), jnp.int32)
    slot_rows = min(n_routes, per_device * MOST)
    gate_all, up_all, down_all = (gate_weight, up_weight, down_weight)
    target, place_in, copy_index = place_routes(expert_ids, replicate, n_devices, per_device)
    home_spot = target * slot_rows + place_in
    send_x, send_cot, send_wgt, send_tag = fill_slots(
        home_spot,
        tokens,
        out_grad,
        route_weight.reshape(-1),
        copy_index,
        n_devices * slot_rows,
        top_count,
    )
    part_shape = (n_devices, slot_rows, model_width)
    arrived_x, arrived_cot, arrived_wgt, arrived_tag = (
        lax.all_to_all(
            send_x.reshape(part_shape), "expert", split_axis=0, concat_axis=0, tiled=True
        ),
        lax.all_to_all(
            send_cot.reshape(part_shape), "expert", split_axis=0, concat_axis=0, tiled=True
        ),
        lax.all_to_all(
            send_wgt.reshape(part_shape[:2]), "expert", split_axis=0, concat_axis=0, tiled=True
        ),
        lax.all_to_all(
            send_tag.reshape(part_shape[:2]), "expert", split_axis=0, concat_axis=0, tiled=True
        ),
    )
    got_x, got_cot, got_wgt, got_tag = (
        lax.all_gather(arrived_x[None], "dp", axis=0, tiled=True),
        lax.all_gather(arrived_cot[None], "dp", axis=0, tiled=True),
        lax.all_gather(arrived_wgt[None], "dp", axis=0, tiled=True),
        lax.all_gather(arrived_tag[None], "dp", axis=0, tiled=True),
    )
    lay_shape = (n_data, n_devices, slot_rows, model_width)
    input_rows, weight_rows, down_acc = run_copies(
        got_x.reshape(-1, model_width),
        got_cot.reshape(-1, model_width),
        got_wgt.reshape(-1),
        got_tag.reshape(-1).astype(jnp.int32),
        gate_all,
        up_all,
        down_all,
    )
    summed, summed_w = (
        lax.psum_scatter(
            input_rows.reshape(lay_shape).astype(jnp.bfloat16),
            "dp",
            scatter_dimension=0,
            tiled=True,
        ).astype(jnp.float32),
        lax.psum_scatter(
            weight_rows.reshape(lay_shape[:3]).astype(jnp.bfloat16),
            "dp",
            scatter_dimension=0,
            tiled=True,
        ).astype(jnp.float32),
    )
    back_rows = summed.reshape(n_devices, slot_rows, model_width).astype(jnp.bfloat16)
    back_w = summed_w.reshape(n_devices, slot_rows).astype(jnp.bfloat16)
    home_rows, home_w = (
        lax.all_to_all(back_rows, "expert", split_axis=0, concat_axis=0, tiled=True),
        lax.all_to_all(back_w, "expert", split_axis=0, concat_axis=0, tiled=True),
    )
    route_rows = home_rows.reshape(-1, model_width)[home_spot].astype(jnp.float32)
    token_grad = jnp.sum(route_rows.reshape(tok_dev, top_count, model_width), axis=1).astype(
        jnp.bfloat16
    )
    route_grad = home_w.reshape(-1)[home_spot].reshape(tok_dev, top_count)
    return (token_grad, route_grad, down_acc.astype(jnp.bfloat16))


def solution(mesh):
    in_specs = (
        P(("groups", "expert", "dp"), None),
        P(("groups", "expert", "dp"), None),
        P(("groups", "expert", "dp"), None),
        P(("groups", "expert", "dp"), None),
        P("expert", None, "dp"),
        P("expert", None, "dp"),
        P("expert", "dp", None),
    )
    out_specs = (
        P(("groups", "expert", "dp"), None),
        P(("groups", "expert", "dp"), None),
        P(("groups", "expert"), "dp", None),
    )
    return jax.shard_map(shards, mesh=mesh, in_specs=in_specs, out_specs=out_specs, check_vma=False)
```

profile of v0, /device:TPU:0, one launch (start us, length us, event | category | flops | bytes accessed | tf_op | source)
XLA Modules:
  0.0 1495.9 jit_solution(2625032202233827775)
XLA Ops:
  12.6 31.9 %all_to_all.37 = bf16[4,64,2048]{2,1,0:T(8,128)(2,1)} all-to-all(bf16[4,64,2048]{2,1,0:T(8,128)(2,1)S(1)} %bitcast.84), channel_id=1, replica_groups=mesh['groups'=2,'expert'=4,'dp'=4] {'expert'}, dimensions={0} | all-to-all | bytes 2097152 | tf_op jit(solution)/shard_map/all_to_all | solution.py:174
  46.0 28.0 %all_to_all.38 = bf16[4,64,2048]{2,1,0:T(8,128)(2,1)} all-to-all(bf16[4,64,2048]{2,1,0:T(8,128)(2,1)S(1)} %bitcast.85), channel_id=1, replica_groups=mesh['groups'=2,'expert'=4,'dp'=4] {'expert'}, dimensions={0} | all-to-all | bytes 2097152 | tf_op jit(solution)/shard_map/all_to_all | solution.py:171
  82.6 20.9 %copy.38 = bf16[16,2048,192]{2,1,0:T(8,128)(2,1)} copy(bf16[16,2048,192]{1,2,0:T(8,128)(2,1)} %param.16) | data formatting | bytes 25165824 | tf_op jit(solution)/shard_map/while | solution.py:132
  103.5 20.6 %copy.39 = bf16[16,2048,192]{2,1,0:T(8,128)(2,1)} copy(bf16[16,2048,192]{1,2,0:T(8,128)(2,1)} %param.15) | data formatting | bytes 25165824 | tf_op jit(solution)/shard_map/while | solution.py:132
  153.3 19.4 %gather_fusion.2 = bf16[3072]{0:T(1024)(128)(2,1)S(1)} fusion(bf16[1025]{0:T(1024)(128)(2,1)S(1)} %pad_maximum_fusion.1, s32[3072]{0:T(1024)S(1)} %fusion.41), kind=kCustom, calls=%fused_computation.2 | custom fusion | bytes 24576 | tf_op jit(solution)/shard_map/gather | solution.py:105
  177.5 26.6 %gather_fusion.4 = bf16[3072,2048]{1,0:T(8,128)(2,1)} fusion(bf16[1025,2048]{1,0:T(8,128)(2,1)} %concatenate.31, s32[3072]{0:T(1024)S(1)} %fusion.41), kind=kCustom, calls=%fused_computation.4 | custom fusion | bytes 25178112 | tf_op jit(solution)/shard_map/gather | solution.py:104
  208.8 26.6 %gather_fusion.6 = bf16[3072,2048]{1,0:T(8,128)(2,1)} fusion(bf16[1025,2048]{1,0:T(8,128)(2,1)} %concatenate.33, s32[3072]{0:T(1024)S(1)} %fusion.41), kind=kCustom, calls=%fused_computation.6 | custom fusion | bytes 25178112 | tf_op jit(solution)/shard_map/gather | solution.py:103
  235.4 1136.8 %while.16 = (s32[]{:T(128)}, bf16[24,128,2048]{2,1,0:T(8,128)(2,1)}, bf16[24,128]{1,0:T(8,128)(2,1)S(1)}, f32[24,192,2048]{2,0,1:T(8,128)}, s32[24]{0:T(128)S(1)...) while((s32[]{:T(128)}, ...), condition=%wide.region_16.17_spmd, body=%wide.region_11.16_spmd.sunk | while | flops 708067392 | bytes 23055880 | solution.py:132
  238.0 14.5 conditional.2
  254.9 29.9 %dynamic_update_slice.23 = f32[24,192,2048]{2,0,1:T(8,128)} dynamic-update-slice(f32[24,192,2048]{2,0,1:T(8,128)} %get-tuple-element.331, f32[1,192,2048]{2,0,1:T(1,128)S(1)} %copy.49, s32[]{:T(128)} %get-tuple-element.328, s32[]{:T(128)} %constant.154.clone.1..sunk, s32[]{:T(128)} %constant.154.clone.1..sunk) | dynamic-update-slice | bytes 3145732 | tf_op jit(solution)/shard_map/while/body/jit(dynamic_update_index_in_dim)/dynamic_update_slice | solution.py:132
  290.1 14.5 conditional.2
  307.0 29.9 %dynamic_update_slice.23 = f32[24,192,2048]{2,0,1:T(8,128)} dynamic-update-slice(f32[24,192,2048]{2,0,1:T(8,128)} %get-tuple-element.331, f32[1,192,2048]{2,0,1:T(1,128)S(1)} %copy.49, s32[]{:T(128)} %get-tuple-element.328, s32[]{:T(128)} %constant.154.clone.1..sunk, s32[]{:T(128)} %constant.154.clone.1..sunk) | dynamic-update-slice | bytes 3145732 | tf_op jit(solution)/shard_map/while/body/jit(dynamic_update_index_in_dim)/dynamic_update_slice | solution.py:132
  359.1 29.9 %dynamic_update_slice.23 = f32[24,192,2048]{2,0,1:T(8,128)} dynamic-update-slice(f32[24,192,2048]{2,0,1:T(8,128)} %get-tuple-element.331, f32[1,192,2048]{2,0,1:T(1,128)S(1)} %copy.49, s32[]{:T(128)} %get-tuple-element.328, s32[]{:T(128)} %constant.154.clone.1..sunk, s32[]{:T(128)} %constant.154.clone.1..sunk) | dynamic-update-slice | bytes 3145732 | tf_op jit(solution)/shard_map/while/body/jit(dynamic_update_index_in_dim)/dynamic_update_slice | solution.py:132
  394.3 14.5 conditional.2
  411.2 29.9 %dynamic_update_slice.23 = f32[24,192,2048]{2,0,1:T(8,128)} dynamic-update-slice(f32[24,192,2048]{2,0,1:T(8,128)} %get-tuple-element.331, f32[1,192,2048]{2,0,1:T(1,128)S(1)} %copy.49, s32[]{:T(128)} %get-tuple-element.328, s32[]{:T(128)} %constant.154.clone.1..sunk, s32[]{:T(128)} %constant.154.clone.1..sunk) | dynamic-update-slice | bytes 3145732 | tf_op jit(solution)/shard_map/while/body/jit(dynamic_update_index_in_dim)/dynamic_update_slice | solution.py:132
  463.3 29.9 %dynamic_update_slice.23 = f32[24,192,2048]{2,0,1:T(8,128)} dynamic-update-slice(f32[24,192,2048]{2,0,1:T(8,128)} %get-tuple-element.331, f32[1,192,2048]{2,0,1:T(1,128)S(1)} %copy.49, s32[]{:T(128)} %get-tuple-element.328, s32[]{:T(128)} %constant.154.clone.1..sunk, s32[]{:T(128)} %constant.154.clone.1..sunk) | dynamic-update-slice | bytes 3145732 | tf_op jit(solution)/shard_map/while/body/jit(dynamic_update_index_in_dim)/dynamic_update_slice | solution.py:132
  498.6 14.5 conditional.2
  515.5 29.9 %dynamic_update_slice.23 = f32[24,192,2048]{2,0,1:T(8,128)} dynamic-update-slice(f32[24,192,2048]{2,0,1:T(8,128)} %get-tuple-element.331, f32[1,192,2048]{2,0,1:T(1,128)S(1)} %copy.49, s32[]{:T(128)} %get-tuple-element.328, s32[]{:T(128)} %constant.154.clone.1..sunk, s32[]{:T(128)} %constant.154.clone.1..sunk) | dynamic-update-slice | bytes 3145732 | tf_op jit(solution)/shard_map/while/body/jit(dynamic_update_index_in_dim)/dynamic_update_slice | solution.py:132
  567.6 29.9 %dynamic_update_slice.23 = f32[24,192,2048]{2,0,1:T(8,128)} dynamic-update-slice(f32[24,192,2048]{2,0,1:T(8,128)} %get-tuple-element.331, f32[1,192,2048]{2,0,1:T(1,128)S(1)} %copy.49, s32[]{:T(128)} %get-tuple-element.328, s32[]{:T(128)} %constant.154.clone.1..sunk, s32[]{:T(128)} %constant.154.clone.1..sunk) | dynamic-update-slice | bytes 3145732 | tf_op jit(solution)/shard_map/while/body/jit(dynamic_update_index_in_dim)/dynamic_update_slice | solution.py:132
  602.8 14.5 conditional.2
  619.7 29.9 %dynamic_update_slice.23 = f32[24,192,2048]{2,0,1:T(8,128)} dynamic-update-slice(f32[24,192,2048]{2,0,1:T(8,128)} %get-tuple-element.331, f32[1,192,2048]{2,0,1:T(1,128)S(1)} %copy.49, s32[]{:T(128)} %get-tuple-element.328, s32[]{:T(128)} %constant.154.clone.1..sunk, s32[]{:T(128)} %constant.154.clone.1..sunk) | dynamic-update-slice | bytes 3145732 | tf_op jit(solution)/shard_map/while/body/jit(dynamic_update_index_in_dim)/dynamic_update_slice | solution.py:132
  671.8 29.9 %dynamic_update_slice.23 = f32[24,192,2048]{2,0,1:T(8,128)} dynamic-update-slice(f32[24,192,2048]{2,0,1:T(8,128)} %get-tuple-element.331, f32[1,192,2048]{2,0,1:T(1,128)S(1)} %copy.49, s32[]{:T(128)} %get-tuple-element.328, s32[]{:T(128)} %constant.154.clone.1..sunk, s32[]{:T(128)} %constant.154.clone.1..sunk) | dynamic-update-slice | bytes 3145732 | tf_op jit(solution)/shard_map/while/body/jit(dynamic_update_index_in_dim)/dynamic_update_slice | solution.py:132
  707.0 14.5 conditional.2
  723.9 29.9 %dynamic_update_slice.23 = f32[24,192,2048]{2,0,1:T(8,128)} dynamic-update-slice(f32[24,192,2048]{2,0,1:T(8,128)} %get-tuple-element.331, f32[1,192,2048]{2,0,1:T(1,128)S(1)} %copy.49, s32[]{:T(128)} %get-tuple-element.328, s32[]{:T(128)} %constant.154.clone.1..sunk, s32[]{:T(128)} %constant.154.clone.1..sunk) | dynamic-update-slice | bytes 3145732 | tf_op jit(solution)/shard_map/while/body/jit(dynamic_update_index_in_dim)/dynamic_update_slice | solution.py:132
  759.1 14.5 conditional.2
  776.0 29.9 %dynamic_update_slice.23 = f32[24,192,2048]{2,0,1:T(8,128)} dynamic-update-slice(f32[24,192,2048]{2,0,1:T(8,128)} %get-tuple-element.331, f32[1,192,2048]{2,0,1:T(1,128)S(1)} %copy.49, s32[]{:T(128)} %get-tuple-element.328, s32[]{:T(128)} %constant.154.clone.1..sunk, s32[]{:T(128)} %constant.154.clone.1..sunk) | dynamic-update-slice | bytes 3145732 | tf_op jit(solution)/shard_map/while/body/jit(dynamic_update_index_in_dim)/dynamic_update_slice | solution.py:132
  811.2 14.5 conditional.2
  828.1 29.9 %dynamic_update_slice.23 = f32[24,192,2048]{2,0,1:T(8,128)} dynamic-update-slice(f32[24,192,2048]{2,0,1:T(8,128)} %get-tuple-element.331, f32[1,192,2048]{2,0,1:T(1,128)S(1)} %copy.49, s32[]{:T(128)} %get-tuple-element.328, s32[]{:T(128)} %constant.154.clone.1..sunk, s32[]{:T(128)} %constant.154.clone.1..sunk) | dynamic-update-slice | bytes 3145732 | tf_op jit(solution)/shard_map/while/body/jit(dynamic_update_index_in_dim)/dynamic_update_slice | solution.py:132
  863.3 14.5 conditional.2
  880.2 29.9 %dynamic_update_slice.23 = f32[24,192,2048]{2,0,1:T(8,128)} dynamic-update-slice(f32[24,192,2048]{2,0,1:T(8,128)} %get-tuple-element.331, f32[1,192,2048]{2,0,1:T(1,128)S(1)} %copy.49, s32[]{:T(128)} %get-tuple-element.328, s32[]{:T(128)} %constant.154.clone.1..sunk, s32[]{:T(128)} %constant.154.clone.1..sunk) | dynamic-update-slice | bytes 3145732 | tf_op jit(solution)/shard_map/while/body/jit(dynamic_update_index_in_dim)/dynamic_update_slice | solution.py:132
  915.4 14.5 conditional.2
  932.3 29.9 %dynamic_update_slice.23 = f32[24,192,2048]{2,0,1:T(8,128)} dynamic-update-slice(f32[24,192,2048]{2,0,1:T(8,128)} %get-tuple-element.331, f32[1,192,2048]{2,0,1:T(1,128)S(1)} %copy.49, s32[]{:T(128)} %get-tuple-element.328, s32[]{:T(128)} %constant.154.clone.1..sunk, s32[]{:T(128)} %constant.154.clone.1..sunk) | dynamic-update-slice | bytes 3145732 | tf_op jit(solution)/shard_map/while/body/jit(dynamic_update_index_in_dim)/dynamic_update_slice | solution.py:132
  967.5 14.5 conditional.2
  984.4 29.9 %dynamic_update_slice.23 = f32[24,192,2048]{2,0,1:T(8,128)} dynamic-update-slice(f32[24,192,2048]{2,0,1:T(8,128)} %get-tuple-element.331, f32[1,192,2048]{2,0,1:T(1,128)S(1)} %copy.49, s32[]{:T(128)} %get-tuple-element.328, s32[]{:T(128)} %constant.154.clone.1..sunk, s32[]{:T(128)} %constant.154.clone.1..sunk) | dynamic-update-slice | bytes 3145732 | tf_op jit(solution)/shard_map/while/body/jit(dynamic_update_index_in_dim)/dynamic_update_slice | solution.py:132
  1019.6 14.5 conditional.2
  1036.5 29.9 %dynamic_update_slice.23 = f32[24,192,2048]{2,0,1:T(8,128)} dynamic-update-slice(f32[24,192,2048]{2,0,1:T(8,128)} %get-tuple-element.331, f32[1,192,2048]{2,0,1:T(1,128)S(1)} %copy.49, s32[]{:T(128)} %get-tuple-element.328, s32[]{:T(128)} %constant.154.clone.1..sunk, s32[]{:T(128)} %constant.154.clone.1..sunk) | dynamic-update-slice | bytes 3145732 | tf_op jit(solution)/shard_map/while/body/jit(dynamic_update_index_in_dim)/dynamic_update_slice | solution.py:132
  1074.4 29.9 %dynamic_update_slice.23 = f32[24,192,2048]{2,0,1:T(8,128)} dynamic-update-slice(f32[24,192,2048]{2,0,1:T(8,128)} %get-tuple-element.331, f32[1,192,2048]{2,0,1:T(1,128)S(1)} %copy.49, s32[]{:T(128)} %get-tuple-element.328, s32[]{:T(128)} %constant.154.clone.1..sunk, s32[]{:T(128)} %constant.154.clone.1..sunk) | dynamic-update-slice | bytes 3145732 | tf_op jit(solution)/shard_map/while/body/jit(dynamic_update_index_in_dim)/dynamic_update_slice | solution.py:132
  1112.3 29.9 %dynamic_update_slice.23 = f32[24,192,2048]{2,0,1:T(8,128)} dynamic-update-slice(f32[24,192,2048]{2,0,1:T(8,128)} %get-tuple-element.331, f32[1,192,2048]{2,0,1:T(1,128)S(1)} %copy.49, s32[]{:T(128)} %get-tuple-element.328, s32[]{:T(128)} %constant.154.clone.1..sunk, s32[]{:T(128)} %constant.154.clone.1..sunk) | dynamic-update-slice | bytes 3145732 | tf_op jit(solution)/shard_map/while/body/jit(dynamic_update_index_in_dim)/dynamic_update_slice | solution.py:132
  1150.2 29.9 %dynamic_update_slice.23 = f32[24,192,2048]{2,0,1:T(8,128)} dynamic-update-slice(f32[24,192,2048]{2,0,1:T(8,128)} %get-tuple-element.331, f32[1,192,2048]{2,0,1:T(1,128)S(1)} %copy.49, s32[]{:T(128)} %get-tuple-element.328, s32[]{:T(128)} %constant.154.clone.1..sunk, s32[]{:T(128)} %constant.154.clone.1..sunk) | dynamic-update-slice | bytes 3145732 | tf_op jit(solution)/shard_map/while/body/jit(dynamic_update_index_in_dim)/dynamic_update_slice | solution.py:132
  1188.1 29.9 %dynamic_update_slice.23 = f32[24,192,2048]{2,0,1:T(8,128)} dynamic-update-slice(f32[24,192,2048]{2,0,1:T(8,128)} %get-tuple-element.331, f32[1,192,2048]{2,0,1:T(1,128)S(1)} %copy.49, s32[]{:T(128)} %get-tuple-element.328, s32[]{:T(128)} %constant.154.clone.1..sunk, s32[]{:T(128)} %constant.154.clone.1..sunk) | dynamic-update-slice | bytes 3145732 | tf_op jit(solution)/shard_map/while/body/jit(dynamic_update_index_in_dim)/dynamic_update_slice | solution.py:132
  1225.9 29.9 %dynamic_update_slice.23 = f32[24,192,2048]{2,0,1:T(8,128)} dynamic-update-slice(f32[24,192,2048]{2,0,1:T(8,128)} %get-tuple-element.331, f32[1,192,2048]{2,0,1:T(1,128)S(1)} %copy.49, s32[]{:T(128)} %get-tuple-element.328, s32[]{:T(128)} %constant.154.clone.1..sunk, s32[]{:T(128)} %constant.154.clone.1..sunk) | dynamic-update-slice | bytes 3145732 | tf_op jit(solution)/shard_map/while/body/jit(dynamic_update_index_in_dim)/dynamic_update_slice | solution.py:132
  1263.8 29.9 %dynamic_update_slice.23 = f32[24,192,2048]{2,0,1:T(8,128)} dynamic-update-slice(f32[24,192,2048]{2,0,1:T(8,128)} %get-tuple-element.331, f32[1,192,2048]{2,0,1:T(1,128)S(1)} %copy.49, s32[]{:T(128)} %get-tuple-element.328, s32[]{:T(128)} %constant.154.clone.1..sunk, s32[]{:T(128)} %constant.154.clone.1..sunk) | dynamic-update-slice | bytes 3145732 | tf_op jit(solution)/shard_map/while/body/jit(dynamic_update_index_in_dim)/dynamic_update_slice | solution.py:132
  1301.7 29.9 %dynamic_update_slice.23 = f32[24,192,2048]{2,0,1:T(8,128)} dynamic-update-slice(f32[24,192,2048]{2,0,1:T(8,128)} %get-tuple-element.331, f32[1,192,2048]{2,0,1:T(1,128)S(1)} %copy.49, s32[]{:T(128)} %get-tuple-element.328, s32[]{:T(128)} %constant.154.clone.1..sunk, s32[]{:T(128)} %constant.154.clone.1..sunk) | dynamic-update-slice | bytes 3145732 | tf_op jit(solution)/shard_map/while/body/jit(dynamic_update_index_in_dim)/dynamic_update_slice | solution.py:132
  1339.6 29.9 %dynamic_update_slice.23 = f32[24,192,2048]{2,0,1:T(8,128)} dynamic-update-slice(f32[24,192,2048]{2,0,1:T(8,128)} %get-tuple-element.331, f32[1,192,2048]{2,0,1:T(1,128)S(1)} %copy.49, s32[]{:T(128)} %get-tuple-element.328, s32[]{:T(128)} %constant.154.clone.1..sunk, s32[]{:T(128)} %constant.154.clone.1..sunk) | dynamic-update-slice | bytes 3145732 | tf_op jit(solution)/shard_map/while/body/jit(dynamic_update_index_in_dim)/dynamic_update_slice | solution.py:132
  1382.8 15.3 %gather_fusion.7 = bf16[1024,2048]{1,0:T(8,128)(2,1)} fusion(bf16[3073,2048]{1,0:T(8,128)(2,1)} %concatenate.34, s32[1024]{0:T(1024)S(1)} %broadcast_clamp_fusion), kind=kCustom, calls=%fused_computation.7 | custom fusion | bytes 8392704 | tf_op jit(solution)/shard_map/gather | solution.py:142
  1423.7 20.5 %reduce-scatter.2.cloned.1.call-done = bf16[1,4,64,2048]{3,2,1,0:T(8,128)(2,1)} async-done(((bf16[4,4,64,2048]{3,2,1,0:T(8,128)(2,1)}), bf16[1,4,64,2048]{3,2,1,0:T(8,128)(2,1)}) %reduce-scatter.2.cloned.1.call-update) | async-done | bytes 1048592 | tf_op jit(solution)/shard_map/reduce_scatter | solution.py:201
  1448.9 22.4 %convolution_convert_fusion = bf16[16,192,2048]{2,0,1:T(8,128)(2,1)} fusion(f32[24,192,2048]{2,0,1:T(8,128)} %get-tuple-element.111, s32[24]{0:T(128)S(1)} %get-tuple-element.110), kind=kOutput, calls=%fused_computation.57 | convolution fusion | flops 1818231168 | bytes 50331744 | tf_op jit(solution)/shard_map/bc,bfd->cfd/dot_general | solution.py:141
  1471.3 14.5 copy.42
  (453 shorter events, 508.4 us)
Async XLA Ops:
  7.2 37.4 %copy-start.1 = (bf16[128,2048]{1,0:T(8,128)(2,1)S(1)}, bf16[128,2048]{1,0:T(8,128)(2,1)}, u32[]{:S(2)}) copy-start(bf16[128,2048]{1,0:T(8,128)(2,1)} %param.11) | copy-start | bytes 1572868
  7.2 165.6 %all-gather.7.cloned.1.call-start = ((), (), s32[]{:S(2)}) async-start(), calls=%async_computation.8 | async-start | bytes 5242880 | tf_op jit(solution)/shard_map/all_gather | solution.py:186
  11.2 62.9 %copy-start.2 = (s32[128,1]{0,1:T(1,128)S(1)}, s32[128,1]{0,1:T(1,128)}, u32[]{:S(2)}) copy-start(s32[128,1]{0,1:T(1,128)} %param.14) | copy-start | bytes 1540
  11.2 68.8 %copy-start.3 = (bf16[128,1]{0,1:T(2,128)(2,1)S(1)}, bf16[128,1]{0,1:T(2,128)(2,1)}, u32[]{:S(2)}) copy-start(bf16[128,1]{0,1:T(2,128)(2,1)} %param.13) | copy-start | bytes 772
  44.5 159.5 %all-gather.9.cloned.1.call-start = ((), (), s32[]{:S(2)}) async-start(), calls=%async_computation.9 | async-start | bytes 5242880 | tf_op jit(solution)/shard_map/all_gather | solution.py:185
  76.7 47.4 %all-to-all-start = ((bf16[4,1,64]{2,1,0:T(2,128)(2,1)}), bf16[4,1,64]{2,1,0:T(2,128)(2,1)S(1)}, u32[]{:S(2)}, u32[]{:S(2)}) async-start(bf16[4,1,64]{2,1,0:T(2,128)(2,1)} %convert_element_type.134), calls=%async_computation | async-start | bytes 4096 | tf_op jit(solution)/shard_map/all_to_all | solution.py:180
  124.1 19.3 %all-to-all-start.1 = ((bf16[4,1,64]{2,1,0:T(2,128)(2,1)}), bf16[4,1,64]{2,1,0:T(2,128)(2,1)S(1)}, u32[]{:S(2)}, u32[]{:S(2)}) async-start(bf16[4,1,64]{2,1,0:T(2,128)(2,1)} %all_to_all.30), calls=%async_computation.1 | async-start | bytes 4096 | tf_op jit(solution)/shard_map/all_to_all | solution.py:177
  129.2 1315.1 %reduce-scatter.2.cloned.1.call-start = ((), (), s32[]{:S(2)}) async-start(), calls=%async_computation.7 | async-start | bytes 5242880 | tf_op jit(solution)/shard_map/reduce_scatter | solution.py:201
  252.5 0.8 copy-start
  304.6 0.8 copy-start
  356.7 0.8 copy-start
  408.8 0.8 copy-start
  460.9 0.8 copy-start
  513.0 0.8 copy-start
  565.2 0.8 copy-start
  617.3 0.8 copy-start
  669.4 0.8 copy-start
  721.5 0.8 copy-start
  773.6 0.8 copy-start
  825.7 0.8 copy-start
  877.8 0.8 copy-start
  929.9 0.8 copy-start
  982.0 0.8 copy-start
  1034.1 0.8 copy-start
  1072.0 0.8 copy-start
  1109.9 0.8 copy-start
  1147.8 0.8 copy-start
  1185.6 0.8 copy-start
  1223.5 0.8 copy-start
  1261.4 0.8 copy-start
  1299.3 0.8 copy-start
  1337.1 0.8 copy-start
  1382.8 15.3 %copy-start.4 = (u32[32]{0:T(128)S(1)}, u32[32]{0:T(128)}, u32[]{:S(2)}) copy-start(u32[32]{0:T(128)} %constant.188) | copy-start | bytes 388
  1444.3 43.3 %all-to-all-start.4 = ((bf16[4,64,2048]{2,1,0:T(8,128)(2,1)}), bf16[4,64,2048]{2,1,0:T(8,128)(2,1)S(1)}, u32[]{:S(2)}, u32[]{:S(2)}) async-start(bf16[4,64,2048]{2,1,0:T(8,128)(2,1)} %bitcast.88), calls=%async_computation.5 | async-start | bytes 2097152 | tf_op jit(solution)/shard_map/all_to_all | solution.py:217
Sparse Core Ops, SparseCore 0:
  44.7 33.5 all-gather.6
  79.8 34.4 all-gather.8
  1398.2 46.0 reduce-scatter.1
where the time goes:
time: 1520 us; the launch traced here: 1500 us
  local copies, waits for them, and re-layouts  1050 us (69%)
  matrix products  218 us (14%)
  blocking collectives  87.8 us (6%)
  loops' own time  66.2 us (4%)
  other arithmetic  26.4 us (2%)
  waiting for transfers between devices  20.6 us (1%)
  between operations  16.7 us (1%)
    dynamic_update_slice x120, local copies, waits for them, and re-layouts, run_copies(): lax.scan(one_block, jnp.zeros((), jnp.int32), jnp.arange(total_blocks, dt...  821 us
    while x2, local copies, waits for them, and re-layouts, run_copies(): lax.scan(one_block, jnp.zeros((), jnp.int32), jnp.arange(total_blocks, dt...  41.5 us
    another operation x24, loops' own time, one_block(): parts = lax.cond(block_index < n_blocks, working, skipped, 0)  34.5 us
    all_to_all x1, blocking collectives, shards(): lax.all_to_all(send_cot.reshape(part_shape), 'expert', split_axis=0, conc...  31.9 us
    another operation x1, loops' own time, run_copies(): lax.scan(one_block, jnp.zeros((), jnp.int32), jnp.arange(total_blocks, dt...  31.8 us
    dot_general x16, matrix products, expert_block(): up_pre = jnp.dot(x_block, up_c, preferred_element_type=jnp.float32)  30.5 us
  transfers between devices with their start and end apart: 6, of which 1 were waited for; matrix products, arithmetic and copies ran while one was open for 10% of the time, Pallas kernels for 0%

commit v1 on v0

v1 whole, which is shorter than its diff:
```python
import functools

import jax
import jax.numpy as jnp
from jax import lax
from jax.experimental import pallas as pl
from jax.experimental.pallas import tpu as pltpu
from jax.sharding import PartitionSpec as P

MOST = 4
META = 128
BF = jnp.bfloat16
F32 = jnp.float32
VMEM_BYTES = 48 * 1024 * 1024


def dot_nn(a, b):
    return jnp.dot(a, b, preferred_element_type=F32)


def dot_nt(a, b):
    return lax.dot_general(a, b, (((1,), (1,)), ((), ())), preferred_element_type=F32)


def dot_tn(a, b):
    return lax.dot_general(a, b, (((0,), (0,)), ((), ())), preferred_element_type=F32)


def params():
    return pltpu.CompilerParams(vmem_limit_bytes=VMEM_BYTES)


def cost(flops, moved):
    return pl.CostEstimate(flops=int(flops), bytes_accessed=int(moved), transcendentals=0)


def whole(array):
    zeros = (0,) * array.ndim
    return pl.BlockSpec(array.shape, lambda *_: zeros)


def route_columns(ids, per_device):
    count = ids.shape[0]
    across = jnp.broadcast_to(ids.astype(F32), (count, count))
    down = jnp.transpose(across)
    row = lax.broadcasted_iota(jnp.int32, (count, count), 0)
    col = lax.broadcasted_iota(jnp.int32, (count, count), 1)
    earlier = col < row
    inv = 1.0 / per_device
    same_expert = jnp.where((across == down) & earlier, 1.0, 0.0)
    same_shard = jnp.where(
        (jnp.floor((across + 0.5) * inv) == jnp.floor((down + 0.5) * inv)) & earlier, 1.0, 0.0
    )
    rank = jnp.sum(same_expert, axis=1, keepdims=True)
    place = jnp.sum(same_shard, axis=1, keepdims=True)
    shard = jnp.floor((ids.astype(F32) + 0.5) * inv)
    local = ids.astype(F32) - shard * per_device
    return shard, local, rank, place


def slot_table(ids, per_device, room, n_shards):
    shard, local, rank, place = route_columns(ids, per_device)
    slot = jnp.where(place < room, shard * room + place, -1.0).astype(jnp.int32)
    lanes = lax.broadcasted_iota(jnp.int32, (ids.shape[0], n_shards * room), 1)
    return jnp.where(lanes == slot, 1.0, 0.0).astype(BF), local * MOST + rank + 1.0


def pack_kernel(per_device, room, n_shards, ids_ref, tok_ref, cot_ref, wgt_ref, x_ref, c_ref):
    table, tag = slot_table(ids_ref[...], per_device, room, n_shards)
    width = tok_ref.shape[1]
    x_ref[:, :width] = dot_tn(table, tok_ref[...]).astype(BF)
    lane = lax.broadcasted_iota(jnp.int32, (tag.shape[0], META), 1)
    info = jnp.where(lane == 0, tag, jnp.where(lane == 1, wgt_ref[...].astype(F32), 0.0))
    x_ref[:, width:] = dot_tn(table, info.astype(BF)).astype(BF)
    c_ref[...] = dot_tn(table, cot_ref[...]).astype(BF)


def pack_rows(ids, tokens, out_grad, wgt, per_device, room, n_shards):
    rows, width = n_shards * room, tokens.shape[1]
    args = (ids, tokens, out_grad, wgt)
    return pl.pallas_call(
        functools.partial(pack_kernel, per_device, room, n_shards),
        grid=(1,),
        in_specs=[whole(a) for a in args],
        out_specs=[
            pl.BlockSpec((rows, width + META), lambda i: (0, 0)),
            pl.BlockSpec((rows, width), lambda i: (0, 0)),
        ],
        out_shape=[
            jax.ShapeDtypeStruct((rows, width + META), BF),
            jax.ShapeDtypeStruct((rows, width), BF),
        ],
        compiler_params=params(),
        cost_estimate=cost(4e8, 4e6),
        name="pack_rows",
    )(*args)


def sorted_table(meta, room, n_shards, n_sorted):
    tag = meta[:, 0:1].astype(F32).astype(jnp.int32)
    rows = lax.broadcasted_iota(jnp.int32, tag.shape, 0)
    source = jnp.floor((rows.astype(F32) + 0.5) * (1.0 / room)).astype(jnp.int32)
    at = tag - 1
    local = at // MOST
    dest = local * (n_shards * MOST) + source * MOST + (at - local * MOST)
    dest = jnp.where(tag > 0, dest, -1)
    lanes = lax.broadcasted_iota(jnp.int32, (meta.shape[0], n_sorted), 1)
    return jnp.where(lanes == dest, 1.0, 0.0).astype(BF)


def spread(table, rows_ref, width, out_ref, member, chunk=512):
    experts, _, _ = out_ref.shape
    per_expert = table.shape[1] // experts
    turned = jnp.transpose(table)
    low = member * per_expert
    for c in range(0, width, chunk):
        part = dot_nn(turned, rows_ref[:, c : c + chunk]).astype(BF)
        out_ref[:, low : low + per_expert, c : c + chunk] = part.reshape(
            experts, per_expert, chunk
        )


def first_kernel(n_dp, room, n_shards, *refs):
    x_refs = refs[:n_dp]
    gate_ref, up_ref, g_ref, u_ref, xs = refs[n_dp:]
    experts, expert_rows, width = xs.shape
    n_sorted = experts * expert_rows // n_dp

    @pl.when(pl.program_id(0) == 0)
    def _():
        for d in range(n_dp):
            table = sorted_table(x_refs[d][:, width : width + META], room, n_shards, n_sorted)
            spread(table, x_refs[d], width, xs, d)

    x_block = xs[pl.program_id(0)]
    g_ref[0] = dot_nt(x_block, gate_ref[0])
    u_ref[0] = dot_nt(x_block, up_ref[0])


def first_layer(x_list, gate, up, room, n_shards):
    n_dp = len(x_list)
    experts, hidden, width = gate.shape
    expert_rows = n_dp * n_shards * MOST
    by_expert = lambda e: (e, 0, 0)
    shape = jax.ShapeDtypeStruct((experts, expert_rows, hidden), F32)
    return pl.pallas_call(
        functools.partial(first_kernel, n_dp, room, n_shards),
        grid=(experts,),
        in_specs=[whole(x) for x in x_list]
        + [pl.BlockSpec((1, hidden, width), by_expert)] * 2,
        out_specs=[pl.BlockSpec((1, expert_rows, hidden), by_expert)] * 2,
        out_shape=[shape, shape],
        scratch_shapes=[pltpu.VMEM((experts, expert_rows, width), BF)],
        compiler_params=params(),
        cost_estimate=cost(2e9, 3e7),
        name="gate_up",
    )(*x_list, gate, up)


def second_kernel(n_dp, room, n_shards, *refs):
    m_refs, c_refs = refs[:n_dp], refs[n_dp : 2 * n_dp]
    g_ref, u_ref, down_ref, dg_ref, du_ref, hw_ref, cs_ref, r_ref, cs, ms = refs[2 * n_dp :]
    experts, expert_rows, width = cs.shape
    n_sorted = experts * expert_rows // n_dp

    @pl.when(pl.program_id(0) == 0)
    def _():
        for d in range(n_dp):
            meta = m_refs[d][...]
            table = sorted_table(meta, room, n_shards, n_sorted)
            spread(table, c_refs[d], width, cs, d)
            spread(table, m_refs[d], META, ms, d, META)

    at = pl.program_id(0)
    c_block = cs[at]
    cs_ref[0] = c_block
    weight = ms[at][:, 1:2].astype(F32)
    back = dot_nt(c_block, down_ref[0])
    g, u = g_ref[0], u_ref[0]
    sig = jax.nn.sigmoid(g)
    act = g * sig
    hidden = act * u
    router = jnp.sum(hidden.astype(BF).astype(F32) * back, axis=1, keepdims=True)
    r_ref[0] = jnp.broadcast_to(router, (expert_rows, META)).astype(BF)
    hw_ref[0] = (hidden * weight).astype(BF)
    scaled = back * weight
    dg_ref[0] = (scaled * u * (sig * (1.0 + g * (1.0 - sig)))).astype(BF)
    du_ref[0] = (scaled * act).astype(BF)


def second_layer(x_list, c_list, g, u, down, room, n_shards):
    n_dp = len(c_list)
    experts, hidden, width = down.shape
    expert_rows = g.shape[1]
    slots = c_list[0].shape[0]
    by_expert = lambda e: (e, 0, 0)
    small = jax.ShapeDtypeStruct((experts, expert_rows, hidden), BF)
    small_spec = pl.BlockSpec((1, expert_rows, hidden), by_expert)
    return pl.pallas_call(
        functools.partial(second_kernel, n_dp, room, n_shards),
        grid=(experts,),
        in_specs=[pl.BlockSpec((slots, META), lambda e: (0, width // META))] * n_dp
        + [whole(c) for c in c_list]
        + [small_spec] * 2
        + [pl.BlockSpec((1, hidden, width), by_expert)],
        out_specs=[small_spec] * 3
        + [
            pl.BlockSpec((1, expert_rows, width), by_expert),
            pl.BlockSpec((1, expert_rows, META), by_expert),
        ],
        out_shape=[small] * 3
        + [
            jax.ShapeDtypeStruct((experts, expert_rows, width), BF),
            jax.ShapeDtypeStruct((experts, expert_rows, META), BF),
        ],
        scratch_shapes=[
            pltpu.VMEM((experts, expert_rows, width), BF),
            pltpu.VMEM((experts, expert_rows, META), BF),
        ],
        compiler_params=params(),
        cost_estimate=cost(2e9, 2e7),
        name="hidden_grads",
    )(*x_list, *c_list, g, u, down)


def third_kernel(n_dp, room, n_shards, with_router, *refs):
    m_refs = refs[:n_dp]
    rest = refs[n_dp:]
    dg_ref, du_ref, gate_ref, up_ref = rest[:4]
    rest = rest[4:]
    if with_router:
        r_ref, rest = rest[0], rest[1:]
    out_refs, acc = rest[:n_dp], rest[n_dp]
    experts, expert_rows = pl.num_programs(0), dg_ref.shape[1]
    _, _, per_expert, width = acc.shape
    part = gate_ref.shape[2]
    at = pl.program_id(0)
    grad = dot_nn(dg_ref[0], gate_ref[0]) + dot_nn(du_ref[0], up_ref[0])
    grad = grad.astype(BF)
    for d in range(n_dp):
        low = d * per_expert
        acc[d, at, :, :part] = grad[low : low + per_expert]
        if with_router:
            acc[d, at, :, part:] = r_ref[0, low : low + per_expert]

    @pl.when(at == acc.shape[1] - 1)
    def _():
        for d in range(n_dp):
            table = sorted_table(m_refs[d][...], room, n_shards, acc.shape[1] * per_expert)
            rows = acc[d].reshape(acc.shape[1] * per_expert, width)
            out_refs[d][...] = dot_nn(table, rows).astype(BF)


def third_layer(x_list, dg, du, gate, up, router, half, n_half, room, n_shards):
    n_dp = len(x_list)
    experts, hidden, full = gate.shape
    expert_rows = dg.shape[1]
    slots = x_list[0].shape[0]
    part = full // n_half
    width = part + (0 if router is None else META)
    by_expert = lambda e: (e, 0, 0)
    small_spec = pl.BlockSpec((1, expert_rows, hidden), by_expert)
    weight_spec = pl.BlockSpec((1, hidden, part), lambda e: (e, 0, half))
    args = [*x_list, dg, du, gate, up]
    specs = [pl.BlockSpec((slots, META), lambda e: (0, full // META))] * n_dp
    specs += [small_spec] * 2 + [weight_spec] * 2
    if router is not None:
        args.append(router)
        specs.append(pl.BlockSpec((1, expert_rows, META), by_expert))
    return pl.pallas_call(
        functools.partial(third_kernel, n_dp, room, n_shards, router is not None),
        grid=(experts,),
        in_specs=specs,
        out_specs=[pl.BlockSpec((slots, width), lambda e: (0, 0))] * n_dp,
        out_shape=[jax.ShapeDtypeStruct((slots, width), BF)] * n_dp,
        scratch_shapes=[pltpu.VMEM((n_dp, experts, expert_rows // n_dp, width), BF)],
        compiler_params=params(),
        cost_estimate=cost(1e9, 1.5e7),
        name="input_grads",
    )(*args)


def down_kernel(hw_ref, cs_ref, out_ref):
    out_ref[0] = dot_tn(hw_ref[0], cs_ref[0]).astype(BF)


def down_layer(hw, cs):
    experts, rows, hidden = hw.shape
    width = cs.shape[2]
    by_expert = lambda e: (e, 0, 0)
    return pl.pallas_call(
        down_kernel,
        grid=(experts,),
        in_specs=[
            pl.BlockSpec((1, rows, hidden), by_expert),
            pl.BlockSpec((1, rows, width), by_expert),
        ],
        out_specs=pl.BlockSpec((1, hidden, width), by_expert),
        out_shape=jax.ShapeDtypeStruct((experts, hidden, width), BF),
        compiler_params=params(),
        cost_estimate=cost(1e9, 1.8e7),
        name="down_grads",
    )(hw, cs)


def home_kernel(per_device, room, n_shards, n_half, n_blocks, ids_ref, *refs):
    table, _ = slot_table(ids_ref[...], per_device, room, n_shards)
    blocks, (tok_ref, route_ref) = refs[:-2], refs[-2:]
    part = tok_ref.shape[1] // n_half
    size = n_shards * room // n_blocks
    for h in range(n_half):
        total = None
        for k in range(n_blocks):
            term = dot_nn(table[:, k * size : (k + 1) * size], blocks[h * n_blocks + k][...])
            total = term if total is None else total + term
        tok_ref[:, h * part : (h + 1) * part] = total[:, :part].astype(BF)
        if h == n_half - 1:
            route_ref[...] = total[:, part : part + META].astype(BF)


def home_rows(ids, halves, width, per_device, room, n_shards):
    n_half, n_blocks = len(halves), len(halves[0])
    count = ids.shape[0]
    blocks = [b for half in halves for b in half]
    return pl.pallas_call(
        functools.partial(home_kernel, per_device, room, n_shards, n_half, n_blocks),
        grid=(1,),
        in_specs=[whole(ids)] + [whole(b) for b in blocks],
        out_specs=[
            pl.BlockSpec((count, width), lambda i: (0, 0)),
            pl.BlockSpec((count, META), lambda i: (0, 0)),
        ],
        out_shape=[
            jax.ShapeDtypeStruct((count, width), BF),
            jax.ShapeDtypeStruct((count, META), BF),
        ],
        compiler_params=params(),
        cost_estimate=cost(2e8, 2e6),
        name="home_rows",
    )(ids, *blocks)


def shifted(value, axis, step):
    n = lax.axis_size(axis)
    return lax.ppermute(value, axis, [(i, (i + step) % n) for i in range(n)])


def swapped(value, axis, bit):
    n = lax.axis_size(axis)
    return lax.ppermute(value, axis, [(i, i ^ bit) for i in range(n)])


def direct(n_shards):
    return n_shards <= 4


def to_shards(rows, room, n_shards):
    if not direct(n_shards):
        shaped = rows.reshape(n_shards, room, rows.shape[1])
        return lax.all_to_all(shaped, "expert", 0, 0, tiled=True).reshape(rows.shape)
    parts = [rows[:room]]
    for k in range(1, n_shards):
        parts.append(shifted(rows[k * room : (k + 1) * room], "expert", k))
    return jnp.concatenate(parts)


def from_shards(rows, room, n_shards):
    if not direct(n_shards):
        return [to_shards(rows, room, n_shards)]
    parts = [rows[:room]]
    for k in range(1, n_shards):
        parts.append(shifted(rows[k * room : (k + 1) * room], "expert", -k))
    return parts


def dp_bits(n_dp):
    bits, bit = [], 1
    while bit < n_dp:
        bits.append(bit)
        bit *= 2
    return bits


def gather_dp(rows, n_dp):
    got = {0: rows}
    for bit in reversed(dp_bits(n_dp)):
        for k in list(got):
            got[k ^ bit] = swapped(got[k], "dp", bit)
    return [got[k] for k in range(n_dp)]


def scatter_dp(parts, n_dp):
    have = dict(enumerate(parts))
    bits = dp_bits(n_dp)
    for bit in bits:
        left = {}
        for k in sorted(have, reverse=True):
            if k & bit == 0:
                moved = swapped(have[k ^ bit], "dp", bit)
                left[k] = (have[k].astype(F32) + moved.astype(F32)).astype(BF)
        have = left
    return have[0]


def run(room, ids, tokens, out_grad, route_weight, gate, up, down):
    n_shards, n_dp = lax.axis_size("expert"), lax.axis_size("dp")
    per_device, width = gate.shape[0], tokens.shape[1]
    gate, up = jnp.swapaxes(gate, 1, 2), jnp.swapaxes(up, 1, 2)
    send_x, send_c = pack_rows(ids, tokens, out_grad, route_weight, per_device, room, n_shards)
    x_list = gather_dp(to_shards(send_x, room, n_shards), n_dp)
    c_list = gather_dp(to_shards(send_c, room, n_shards), n_dp)
    g, u = first_layer(x_list, gate, up, room, n_shards)
    dg, du, hw, cs, router = second_layer(x_list, c_list, g, u, down, room, n_shards)
    n_half = 2
    halves = []
    for half in range(n_half):
        column = router if half == n_half - 1 else None
        parts = third_layer(
            x_list, dg, du, gate, up, column, half, n_half, room, n_shards
        )
        halves.append(from_shards(scatter_dp(parts, n_dp), room, n_shards))
    down_grad = down_layer(hw, cs)
    token_grad, route = home_rows(ids, halves, width, per_device, room, n_shards)
    return token_grad, route[:, :1], down_grad


def shards(tokens, out_grad, route_weight, expert_ids, gate, up, down):
    n_shards = lax.axis_size("expert")
    per_device = gate.shape[0]
    slot_rows = min(expert_ids.shape[0], per_device * MOST)
    ids = expert_ids
    if direct(n_shards):
        total = n_shards * per_device
        ids = (ids - lax.axis_index("expert") * per_device + total) % total
    return run(slot_rows, ids, tokens, out_grad, route_weight, gate, up, down)


def solution(mesh):
    rows = P(("groups", "expert", "dp"), None)
    in_specs = (
        rows,
        rows,
        rows,
        rows,
        P("expert", None, "dp"),
        P("expert", None, "dp"),
        P("expert", "dp", None),
    )
    out_specs = (rows, rows, P(("groups", "expert"), "dp", None))
    return jax.shard_map(shards, mesh=mesh, in_specs=in_specs, out_specs=out_specs, check_vma=False)
```

time: 1520 us -> 215 us (0.14); the launches traced: 1500 us -> 212 us
  local copies, waits for them, and re-layouts: 1050 us -> 7 us
  matrix products: 218 us -> 0 us
  blocking collectives: 87.8 us -> 0 us
  Pallas kernels: 0 us -> 76.4 us
  loops' own time: 66.2 us -> 0 us
  waiting for transfers between devices: 20.6 us -> 70.2 us
  starting transfers between devices: 13 us -> 55.4 us
  other arithmetic: 26.4 us -> 1.68 us
  between operations: 16.7 us -> 0.87 us
    dynamic_update_slice x120 -> x0, local copies, waits for them, and re-layouts: 821 us -> none  [run_copies(): lax.scan(one_block, jnp.zeros((), jnp.int32), jnp.arange(total_blocks, dt...]
    dot_general x113 -> x0, matrix products: 218 us -> none  [the longest x16 30.5 us: expert_block(): up_pre = jnp.dot(x_block, up_c, preferred_element_type=jnp.float32)]
    gather x11 -> x0, local copies, waits for them, and re-layouts: 105 us -> none  [the longest x1 26.6 us: run_copies(): cot_pack = jnp.concatenate([cot_rows, zero_row])[source]]
    pallas_call x0 -> x7, Pallas kernels: none -> 76.4 us  [the longest x2 26.3 us: third_layer(): pl.pallas_call(functools.partial(third_kernel, n_dp, room, n_shards, rout...]
    all_to_all x3 -> x0, blocking collectives: 70.4 us -> none  [the longest x1 31.9 us: shards(): lax.all_to_all(send_cot.reshape(part_shape), 'expert', split_axis=0, conc...]
    ppermute x0 -> x24, waiting for transfers between devices: none -> 70.2 us  [the longest x12 39.6 us: swapped(): return lax.ppermute(value, axis, [(i, i ^ bit) for i in range(n)])]
    another operation x25 -> x0, loops' own time: 66.2 us -> none  [the longest x24 34.5 us: one_block(): parts = lax.cond(block_index < n_blocks, working, skipped, 0)]
    while x50 -> x0, local copies, waits for them, and re-layouts: 60.5 us -> none  [the longest x2 41.5 us: run_copies(): lax.scan(one_block, jnp.zeros((), jnp.int32), jnp.arange(total_blocks, dt...]
  transfers between devices with their start and end apart: 6 -> 24, of which waited for: 1 -> 8; matrix products, arithmetic and copies ran while one was open for 10% -> 1% of each run, Pallas kernels for 0% -> 20%
where the time goes in v1:
time: 215 us; the launch traced here: 212 us
  Pallas kernels  76.4 us (36%)
  waiting for transfers between devices  70.2 us (33%)
  starting transfers between devices  55.4 us (26%)
  local copies, waits for them, and re-layouts  7 us (3%)
    ppermute x12, starting transfers between devices, shifted(): return lax.ppermute(value, axis, [(i, (i + step) % n) for i in range(n)])  47.8 us
    ppermute x12, waiting for transfers between devices, swapped(): return lax.ppermute(value, axis, [(i, i ^ bit) for i in range(n)])  39.6 us
    ppermute x12, waiting for transfers between devices, shifted(): return lax.ppermute(value, axis, [(i, (i + step) % n) for i in range(n)])  30.7 us
    pallas_call x2, Pallas kernels, third_layer(): pl.pallas_call(functools.partial(third_kernel, n_dp, room, n_shards, rout...  26.3 us
    pallas_call x1, Pallas kernels, first_layer(): pl.pallas_call(functools.partial(first_kernel, n_dp, room, n_shards), gri...  19.4 us
    pallas_call x1, Pallas kernels, second_layer(): pl.pallas_call(functools.partial(second_kernel, n_dp, room, n_shards), gr...  17.3 us
    pallas_call x1, Pallas kernels, down_layer(): pl.pallas_call(down_kernel, grid=(experts,), in_specs=[pl.BlockSpec((1, r...  10.5 us
    ppermute x12, starting transfers between devices, swapped(): return lax.ppermute(value, axis, [(i, i ^ bit) for i in range(n)])  7.6 us
  transfers between devices with their start and end apart: 24, of which 8 were waited for; matrix products, arithmetic and copies ran while one was open for 1% of the time, Pallas kernels for 20%

profile of v1, /device:TPU:0, one launch (start us, length us, event | category | flops | bytes accessed | tf_op | source)
XLA Modules:
  0.0 211.6 jit_solution(10333729724187342531)
XLA Ops:
  0.6 0.7 broadcast_compare_fusion
  1.3 0.1 copy.24
  1.4 0.8 copy.25.wgt_ref
  2.2 0.1 copy.21
  2.4 1.0 copy-done.8
  3.4 1.0 copy-done.9
  4.5 1.1 pack_rows.1
  5.6 5.1 %collective-permute-start.2 = (bf16[64,2176]{1,0:T(8,128)(2,1)S(1)}, bf16[64,2176]{1,0:T(8,128)(2,1)S(1)}, u32[]{:S(2)}, u32[]{:S(2)}) collective-permute-start(bf16[64,2176]{1,0:T(8,128)(2,1)S(1)} %get-tuple-element.50), channel_id=1, source_target_pairs={{0,12},{4,0},{8,4},{12,8},{1,13},{5,1},{9,5},{13,9},{2,14},{6,2},{... | collective-permute-start | bytes 835592 | tf_op jit(solution)/shard_map/ppermute | solution.py:345
  10.7 1.0 collective-permute-start
  11.8 2.9 %collective-permute-start.8 = (bf16[64,2048]{1,0:T(8,128)(2,1)S(1)}, bf16[64,2048]{1,0:T(8,128)(2,1)S(1)}, u32[]{:S(2)}, u32[]{:S(2)}) collective-permute-start(bf16[64,2048]{1,0:T(8,128)(2,1)S(1)} %get-tuple-element.54), channel_id=1, source_target_pairs={{0,12},{4,0},{8,4},{12,8},{1,13},{5,1},{9,5},{13,9},{2,14},{6,2},{... | collective-permute-start | bytes 786440 | tf_op jit(solution)/shard_map/ppermute | solution.py:345
  14.7 1.1 collective-permute-start.7
  15.8 2.0 collective-permute-done.2
  17.8 11.3 %collective-permute-start.6 = (bf16[64,2048]{1,0:T(8,128)(2,1)S(1)}, bf16[64,2048]{1,0:T(8,128)(2,1)S(1)}, u32[]{:S(2)}, u32[]{:S(2)}) collective-permute-start(bf16[64,2048]{1,0:T(8,128)(2,1)S(1)} %get-tuple-element.56), channel_id=1, source_target_pairs={{0,4},{4,8},{8,12},{12,0},{1,5},{5,9},{9,13},{13,1},{2,6},{6,10},{... | collective-permute-start | bytes 786440 | tf_op jit(solution)/shard_map/ppermute | solution.py:345
  29.1 17.7 %collective-permute-done.1 = bf16[64,2176]{1,0:T(8,128)(2,1)S(1)} collective-permute-done((bf16[64,2176]{1,0:T(8,128)(2,1)S(1)}, bf16[64,2176]{1,0:T(8,128)(2,1)S(1)}, u32[]{:S(2)}, u32[]{:S(2)}) %collective-permute-start.1) | collective-permute-done | bytes 278560 | tf_op jit(solution)/shard_map/ppermute | solution.py:345
  46.9 1.6 collective-permute-start.4
  48.5 8.4 %collective-permute-done.7 = bf16[64,2048]{1,0:T(8,128)(2,1)S(1)} collective-permute-done((bf16[64,2048]{1,0:T(8,128)(2,1)S(1)}, bf16[64,2048]{1,0:T(8,128)(2,1)S(1)}, u32[]{:S(2)}, u32[]{:S(2)}) %collective-permute-start.7) | collective-permute-done | bytes 262176 | tf_op jit(solution)/shard_map/ppermute | solution.py:345
  56.9 0.1 pad_maximum_fusion.1.refs_4_
  57.0 1.6 collective-permute-start.10
  58.6 7.7 %collective-permute-done.4.refs_2_ = bf16[256,2176]{1,0:T(8,128)(2,1)S(1)} collective-permute-done((bf16[256,2176]{1,0:T(8,128)(2,1)S(1)}, bf16[256,2176]{1,0:T(8,128)(2,1)S(1)}, u32[]{:S(2)}, u32[]{:S(2)}) %collective-permute-start.4) | collective-permute-done | bytes 1114144 | tf_op jit(solution)/shard_map/ppermute | solution.py:350
  66.3 0.5 collective-permute-start.9
  66.8 18.2 %collective-permute-done.10.refs_6_ = bf16[256,2048]{1,0:T(8,128)(2,1)S(1)} collective-permute-done((bf16[256,2048]{1,0:T(8,128)(2,1)S(1)}, bf16[256,2048]{1,0:T(8,128)(2,1)S(1)}, u32[]{:S(2)}, u32[]{:S(2)}) %collective-permute-start.10) | collective-permute-done | bytes 1048608 | tf_op jit(solution)/shard_map/ppermute | solution.py:350
  85.0 1.0 copy-done.10
  86.0 19.4 %gate_up.1 = (f32[16,64,192]{2,1,0:T(8,128)S(1)}, f32[16,64,192]{2,1,0:T(8,128)S(1)}) custom-call(bf16[256,2176]{1,0:T(8,128)(2,1)S(1)} %pad_maximum_fusion.refs_0_, bf16[256,2176]{1,0:T(8,128)(2,1)S(1)} %collective-permute-done.3.refs_1_, bf16[256,2176]{1,0:T(8,128)(2,1)S(1)} %collective-permute-done.4.refs_2_, bf16[256,2176]{1,0:T(8,128)(2,1)} %copy-done.10, ...), custom_call_target="tpu_custom_call" | custom-call | flops 2000000000 | bytes 30000000 | tf_op jit(solution)/shard_map/gate_up/pallas_call | solution.py:146
  105.4 1.0 copy-done.6
  106.4 1.0 copy-done.7
  107.5 17.3 %hidden_grads.1 = (bf16[16,64,192]{2,1,0:T(8,128)(2,1)S(1)}, bf16[16,64,192]{2,1,0:T(8,128)(2,1)S(1)}, bf16[16,64,192]{2,1,0:T(8,128)(2,1)S(1)}, bf16[16,64,2048]{2,1,0:T(8,128)(2,1)}, bf16[16,64,128]{2,1,0:T(8,128)(2,1)S(1)}) custom-call(bf16[256,2176]{1,0:T(8,128)(2,1)} %copy-done, bf16[256,2176]{1,0:T(8,128)(2,1)} %copy-done.3, ...), custom_call_target="tpu_custom_call" | custom-call | flops 2000000000 | bytes 20000000 | tf_op jit(solution)/shard_map/hidden_grads/pallas_call | solution.py:199
  124.8 13.1 %input_grads.2 = (bf16[256,1024]{1,0:T(8,128)(2,1)S(1)}, bf16[256,1024]{1,0:T(8,128)(2,1)S(1)}, bf16[256,1024]{1,0:T(8,128)(2,1)S(1)}, bf16[256,1024]{1,0:T(8,128)(2,1)S(1)}) custom-call(bf16[256,2176]{1,0:T(8,128)(2,1)S(1)} %copy-done.1, bf16[256,2176]{1,0:T(8,128)(2,1)S(1)} %copy-done.4, bf16[256,2176]{1,0:T(8,128)(2,1)} %copy-done.2, ...), custom_call_target="tpu_custom_call" | custom-call | flops 1000000000 | bytes 15000000 | tf_op jit(solution)/shard_map/input_grads/pallas_call | solution.py:270
  137.9 0.6 collective-permute-start.13
  138.4 13.2 %input_grads.3 = (bf16[256,1152]{1,0:T(8,128)(2,1)S(1)}, bf16[256,1152]{1,0:T(8,128)(2,1)S(1)}, bf16[256,1152]{1,0:T(8,128)(2,1)S(1)}, bf16[256,1152]{1,0:T(8,128)(2,1)S(1)}) custom-call(bf16[256,2176]{1,0:T(8,128)(2,1)S(1)} %copy-done.1, bf16[256,2176]{1,0:T(8,128)(2,1)S(1)} %copy-done.4, bf16[256,2176]{1,0:T(8,128)(2,1)} %copy-done.2, ...), custom_call_target="tpu_custom_call" | custom-call | flops 1000000000 | bytes 15000000 | tf_op jit(solution)/shard_map/input_grads/pallas_call | solution.py:270
  151.6 0.1 collective-permute-start.19
  151.7 0.5 collective-permute-start.12
  152.3 0.2 add_convert_fusion.4
  152.5 1.5 collective-permute-start.14
  154.0 0.1 add_convert_fusion.1
  154.2 1.2 collective-permute-start.20
  155.4 11.9 %collective-permute-done.14 = bf16[256,1024]{1,0:T(8,128)(2,1)S(1)} collective-permute-done((bf16[256,1024]{1,0:T(8,128)(2,1)S(1)}, bf16[256,1024]{1,0:T(8,128)(2,1)S(1)}, u32[]{:S(2)}, u32[]{:S(2)}) %collective-permute-start.14) | collective-permute-done | bytes 524320 | tf_op jit(solution)/shard_map/ppermute | solution.py:350
  167.3 0.3 add_convert_fusion.3
  167.6 10.0 %collective-permute-start.17 = (bf16[64,1024]{1,0:T(8,128)(2,1)S(1)}, bf16[64,1024]{1,0:T(8,128)(2,1)S(1)}, u32[]{:S(2)}, u32[]{:S(2)}) collective-permute-start(bf16[64,1024]{1,0:T(8,128)(2,1)S(1)} %get-tuple-element.61), channel_id=1, source_target_pairs={{0,4},{4,8},{8,12},{12,0},{1,5},{5,9},{9,13},{13,1},{2,6},{6,10},{... | collective-permute-start | bytes 393224 | tf_op jit(solution)/shard_map/ppermute | solution.py:345
  177.6 1.8 collective-permute-done.20
  179.5 0.2 add_convert_fusion
  179.7 10.0 %collective-permute-start.23 = (bf16[64,1152]{1,0:T(8,128)(2,1)S(1)}, bf16[64,1152]{1,0:T(8,128)(2,1)S(1)}, u32[]{:S(2)}, u32[]{:S(2)}) collective-permute-start(bf16[64,1152]{1,0:T(8,128)(2,1)S(1)} %get-tuple-element.57), channel_id=1, source_target_pairs={{0,4},{4,8},{8,12},{12,0},{1,5},{5,9},{9,13},{13,1},{2,6},{6,10},{... | collective-permute-start | bytes 442376 | tf_op jit(solution)/shard_map/ppermute | solution.py:345
  189.8 2.0 collective-permute-start.22
  191.8 2.9 %collective-permute-start.21 = (bf16[64,1152]{1,0:T(8,128)(2,1)S(1)}, bf16[64,1152]{1,0:T(8,128)(2,1)S(1)}, u32[]{:S(2)}, u32[]{:S(2)}) collective-permute-start(bf16[64,1152]{1,0:T(8,128)(2,1)S(1)} %get-tuple-element.59), channel_id=1, source_target_pairs={{0,12},{4,0},{8,4},{12,8},{1,13},{5,1},{9,5},{13,9},{2,14},{6,2},{... | collective-permute-start | bytes 442376 | tf_op jit(solution)/shard_map/ppermute | solution.py:345
  194.6 1.5 collective-permute-start.15
  196.2 10.5 %down_grads.1 = bf16[16,192,2048]{2,1,0:T(8,128)(2,1)} custom-call(bf16[16,64,192]{2,1,0:T(8,128)(2,1)S(1)} %get-tuple-element.39.hw_ref, bf16[16,64,2048]{2,1,0:T(8,128)(2,1)S(1)} %copy-done.5), custom_call_target="tpu_custom_call" | custom-call | flops 1000000000 | bytes 18000000 | tf_op jit(solution)/shard_map/down_grads/pallas_call | solution.py:291
  206.7 2.5 %collective-permute-done.16.refs_2_ = bf16[64,1024]{1,0:T(8,128)(2,1)S(1)} collective-permute-done((bf16[64,1024]{1,0:T(8,128)(2,1)S(1)}, bf16[64,1024]{1,0:T(8,128)(2,1)S(1)}, u32[]{:S(2)}, u32[]{:S(2)}) %collective-permute-start.16) | collective-permute-done | bytes 131104 | tf_op jit(solution)/shard_map/ppermute | solution.py:345
  209.2 1.9 home_rows.1
  211.0 0.6 copy.26
  (45 shorter events, 0.5 us)
Async XLA Ops:
  2.4 1.0 copy-start.8
  3.4 1.0 copy-start.9
  5.6 12.2 %collective-permute-start.2 = (bf16[64,2176]{1,0:T(8,128)(2,1)S(1)}, bf16[64,2176]{1,0:T(8,128)(2,1)S(1)}, u32[]{:S(2)}, u32[]{:S(2)}) collective-permute-start(bf16[64,2176]{1,0:T(8,128)(2,1)S(1)} %get-tuple-element.50), channel_id=1, source_target_pairs={{0,12},{4,0},{8,4},{12,8},{1,13},{5,1},{9,5},{13,9},{2,14},{6,2},{... | collective-permute-start | bytes 835592 | tf_op jit(solution)/shard_map/ppermute | solution.py:345
  10.7 36.1 %collective-permute-start.1 = (bf16[64,2176]{1,0:T(8,128)(2,1)S(1)}, bf16[64,2176]{1,0:T(8,128)(2,1)S(1)}, u32[]{:S(2)}, u32[]{:S(2)}) collective-permute-start(bf16[64,2176]{1,0:T(8,128)(2,1)S(1)} %get-tuple-element.51), channel_id=1, source_target_pairs={{0,8},{4,12},{8,0},{12,4},{1,9},{5,13},{9,1},{13,5},{2,10},{6,14},... | collective-permute-start | bytes 835592 | tf_op jit(solution)/shard_map/ppermute | solution.py:345
  10.7 36.1 %collective-permute-start = (bf16[64,2176]{1,0:T(8,128)(2,1)S(1)}, bf16[64,2176]{1,0:T(8,128)(2,1)S(1)}, u32[]{:S(2)}, u32[]{:S(2)}) collective-permute-start(bf16[64,2176]{1,0:T(8,128)(2,1)S(1)} %get-tuple-element.52), channel_id=1, source_target_pairs={{0,4},{4,8},{8,12},{12,0},{1,5},{5,9},{9,13},{13,1},{2,6},{6,10},{... | collective-permute-start | bytes 835592 | tf_op jit(solution)/shard_map/ppermute | solution.py:345
  11.8 36.7 %collective-permute-start.8 = (bf16[64,2048]{1,0:T(8,128)(2,1)S(1)}, bf16[64,2048]{1,0:T(8,128)(2,1)S(1)}, u32[]{:S(2)}, u32[]{:S(2)}) collective-permute-start(bf16[64,2048]{1,0:T(8,128)(2,1)S(1)} %get-tuple-element.54), channel_id=1, source_target_pairs={{0,12},{4,0},{8,4},{12,8},{1,13},{5,1},{9,5},{13,9},{2,14},{6,2},{... | collective-permute-start | bytes 786440 | tf_op jit(solution)/shard_map/ppermute | solution.py:345
  14.7 42.2 %collective-permute-start.7 = (bf16[64,2048]{1,0:T(8,128)(2,1)S(1)}, bf16[64,2048]{1,0:T(8,128)(2,1)S(1)}, u32[]{:S(2)}, u32[]{:S(2)}) collective-permute-start(bf16[64,2048]{1,0:T(8,128)(2,1)S(1)} %get-tuple-element.55), channel_id=1, source_target_pairs={{0,8},{4,12},{8,0},{12,4},{1,9},{5,13},{9,1},{13,5},{2,10},{6,14},... | collective-permute-start | bytes 786440 | tf_op jit(solution)/shard_map/ppermute | solution.py:345
  17.8 39.1 %collective-permute-start.6 = (bf16[64,2048]{1,0:T(8,128)(2,1)S(1)}, bf16[64,2048]{1,0:T(8,128)(2,1)S(1)}, u32[]{:S(2)}, u32[]{:S(2)}) collective-permute-start(bf16[64,2048]{1,0:T(8,128)(2,1)S(1)} %get-tuple-element.56), channel_id=1, source_target_pairs={{0,4},{4,8},{8,12},{12,0},{1,5},{5,9},{9,13},{13,1},{2,6},{6,10},{... | collective-permute-start | bytes 786440 | tf_op jit(solution)/shard_map/ppermute | solution.py:345
  46.9 58.5 %copy-start = (bf16[256,2176]{1,0:T(8,128)(2,1)}, bf16[256,2176]{1,0:T(8,128)(2,1)S(1)}, u32[]{:S(2)}) copy-start(bf16[256,2176]{1,0:T(8,128)(2,1)S(1)} %pad_maximum_fusion.refs_0_) | copy-start | bytes 3342340
  46.9 19.3 %collective-permute-start.4 = (bf16[256,2176]{1,0:T(8,128)(2,1)S(1)}, bf16[256,2176]{1,0:T(8,128)(2,1)S(1)}, u32[]{:S(2)}, u32[]{:S(2)}) collective-permute-start(bf16[256,2176]{1,0:T(8,128)(2,1)S(1)} %pad_maximum_fusion.refs_0_), channel_id=1, source_target_pairs={{0,2},{1,3},{2,0},{3,1},{4,6},{5,7},{6,4},{7,5},{8,10},{9,11},{10,... | collective-permute-start | bytes 3342344 | tf_op jit(solution)/shard_map/ppermute | solution.py:350
  57.0 27.9 %collective-permute-start.10 = (bf16[256,2048]{1,0:T(8,128)(2,1)S(1)}, bf16[256,2048]{1,0:T(8,128)(2,1)S(1)}, u32[]{:S(2)}, u32[]{:S(2)}) collective-permute-start(bf16[256,2048]{1,0:T(8,128)(2,1)S(1)} %pad_maximum_fusion.1.refs_4_), channel_id=1, source_target_pairs={{0,2},{1,3},{2,0},{3,1},{4,6},{5,7},{6,4},{7,5},{8,10},{9,11},{10,... | collective-permute-start | bytes 3145736 | tf_op jit(solution)/shard_map/ppermute | solution.py:350
  58.6 26.4 %collective-permute-start.3 = (bf16[256,2176]{1,0:T(8,128)(2,1)S(1)}, bf16[256,2176]{1,0:T(8,128)(2,1)S(1)}, u32[]{:S(2)}, u32[]{:S(2)}) collective-permute-start(bf16[256,2176]{1,0:T(8,128)(2,1)S(1)} %pad_maximum_fusion.refs_0_), channel_id=1, source_target_pairs={{0,1},{1,0},{2,3},{3,2},{4,5},{5,4},{6,7},{7,6},{8,9},{9,8},{10,11... | collective-permute-start | bytes 3342344 | tf_op jit(solution)/shard_map/ppermute | solution.py:350
  66.3 39.1 %copy-start.2 = (bf16[256,2176]{1,0:T(8,128)(2,1)}, bf16[256,2176]{1,0:T(8,128)(2,1)S(1)}, u32[]{:S(2)}) copy-start(bf16[256,2176]{1,0:T(8,128)(2,1)S(1)} %collective-permute-done.4.refs_2_) | copy-start | bytes 3342340
  66.3 18.7 %collective-permute-start.5 = (bf16[256,2176]{1,0:T(8,128)(2,1)S(1)}, bf16[256,2176]{1,0:T(8,128)(2,1)S(1)}, u32[]{:S(2)}, u32[]{:S(2)}) collective-permute-start(bf16[256,2176]{1,0:T(8,128)(2,1)S(1)} %collective-permute-done.4.refs_2_), channel_id=1, source_target_pairs={{0,1},{1,0},{2,3},{3,2},{4,5},{5,4},{6,7},{7,6},{8,9},{9,8},{10,11... | collective-permute-start | bytes 3342344 | tf_op jit(solution)/shard_map/ppermute | solution.py:350
  66.3 41.2 %collective-permute-start.9 = (bf16[256,2048]{1,0:T(8,128)(2,1)S(1)}, bf16[256,2048]{1,0:T(8,128)(2,1)S(1)}, u32[]{:S(2)}, u32[]{:S(2)}) collective-permute-start(bf16[256,2048]{1,0:T(8,128)(2,1)S(1)} %pad_maximum_fusion.1.refs_4_), channel_id=1, source_target_pairs={{0,1},{1,0},{2,3},{3,2},{4,5},{5,4},{6,7},{7,6},{8,9},{9,8},{10,11... | collective-permute-start | bytes 3145736 | tf_op jit(solution)/shard_map/ppermute | solution.py:350
  85.0 22.5 %collective-permute-start.11 = (bf16[256,2048]{1,0:T(8,128)(2,1)S(1)}, bf16[256,2048]{1,0:T(8,128)(2,1)S(1)}, u32[]{:S(2)}, u32[]{:S(2)}) collective-permute-start(bf16[256,2048]{1,0:T(8,128)(2,1)S(1)} %collective-permute-done.10.refs_6_), channel_id=1, source_target_pairs={{0,1},{1,0},{2,3},{3,2},{4,5},{5,4},{6,7},{7,6},{8,9},{9,8},{10,11... | collective-permute-start | bytes 3145736 | tf_op jit(solution)/shard_map/ppermute | solution.py:350
  85.0 20.5 %copy-start.3 = (bf16[256,2176]{1,0:T(8,128)(2,1)}, bf16[256,2176]{1,0:T(8,128)(2,1)S(1)}, u32[]{:S(2)}) copy-start(bf16[256,2176]{1,0:T(8,128)(2,1)S(1)} %collective-permute-done.3.refs_1_) | copy-start | bytes 3342340
  85.0 1.0 copy-start.10
  105.4 1.0 copy-start.6
  106.4 1.0 copy-start.7
  107.4 17.3 %copy-start.1 = (bf16[256,2176]{1,0:T(8,128)(2,1)S(1)}, bf16[256,2176]{1,0:T(8,128)(2,1)}, u32[]{:S(2)}) copy-start(bf16[256,2176]{1,0:T(8,128)(2,1)} %copy-done) | copy-start | bytes 3342340
  107.4 17.3 %copy-start.4 = (bf16[256,2176]{1,0:T(8,128)(2,1)S(1)}, bf16[256,2176]{1,0:T(8,128)(2,1)}, u32[]{:S(2)}) copy-start(bf16[256,2176]{1,0:T(8,128)(2,1)} %copy-done.3) | copy-start | bytes 3342340
  137.9 14.4 %collective-permute-start.13 = (bf16[256,1024]{1,0:T(8,128)(2,1)S(1)}, bf16[256,1024]{1,0:T(8,128)(2,1)S(1)}, u32[]{:S(2)}, u32[]{:S(2)}) collective-permute-start(bf16[256,1024]{1,0:T(8,128)(2,1)S(1)} %get-tuple-element.31), channel_id=1, source_target_pairs={{0,1},{1,0},{2,3},{3,2},{4,5},{5,4},{6,7},{7,6},{8,9},{9,8},{10,11... | collective-permute-start | bytes 1572872 | tf_op jit(solution)/shard_map/ppermute | solution.py:350
  151.6 2.4 %collective-permute-start.19 = (bf16[256,1152]{1,0:T(8,128)(2,1)S(1)}, bf16[256,1152]{1,0:T(8,128)(2,1)S(1)}, u32[]{:S(2)}, u32[]{:S(2)}) collective-permute-start(bf16[256,1152]{1,0:T(8,128)(2,1)S(1)} %get-tuple-element.36), channel_id=1, source_target_pairs={{0,1},{1,0},{2,3},{3,2},{4,5},{5,4},{6,7},{7,6},{8,9},{9,8},{10,11... | collective-permute-start | bytes 1769480 | tf_op jit(solution)/shard_map/ppermute | solution.py:350
  151.7 3.7 %collective-permute-start.12 = (bf16[256,1024]{1,0:T(8,128)(2,1)S(1)}, bf16[256,1024]{1,0:T(8,128)(2,1)S(1)}, u32[]{:S(2)}, u32[]{:S(2)}) collective-permute-start(bf16[256,1024]{1,0:T(8,128)(2,1)S(1)} %get-tuple-element.29), channel_id=1, source_target_pairs={{0,1},{1,0},{2,3},{3,2},{4,5},{5,4},{6,7},{7,6},{8,9},{9,8},{10,11... | collective-permute-start | bytes 1572872 | tf_op jit(solution)/shard_map/ppermute | solution.py:350
  152.2 25.4 %collective-permute-start.18 = (bf16[256,1152]{1,0:T(8,128)(2,1)S(1)}, bf16[256,1152]{1,0:T(8,128)(2,1)S(1)}, u32[]{:S(2)}, u32[]{:S(2)}) collective-permute-start(bf16[256,1152]{1,0:T(8,128)(2,1)S(1)} %get-tuple-element.34), channel_id=1, source_target_pairs={{0,1},{1,0},{2,3},{3,2},{4,5},{5,4},{6,7},{7,6},{8,9},{9,8},{10,11... | collective-permute-start | bytes 1769480 | tf_op jit(solution)/shard_map/ppermute | solution.py:350
  152.5 14.8 %collective-permute-start.14 = (bf16[256,1024]{1,0:T(8,128)(2,1)S(1)}, bf16[256,1024]{1,0:T(8,128)(2,1)S(1)}, u32[]{:S(2)}, u32[]{:S(2)}) collective-permute-start(bf16[256,1024]{1,0:T(8,128)(2,1)S(1)} %add_convert_fusion.4), channel_id=1, source_target_pairs={{0,2},{1,3},{2,0},{3,1},{4,6},{5,7},{6,4},{7,5},{8,10},{9,11},{10,... | collective-permute-start | bytes 1572872 | tf_op jit(solution)/shard_map/ppermute | solution.py:350
  154.2 25.3 %collective-permute-start.20 = (bf16[256,1152]{1,0:T(8,128)(2,1)S(1)}, bf16[256,1152]{1,0:T(8,128)(2,1)S(1)}, u32[]{:S(2)}, u32[]{:S(2)}) collective-permute-start(bf16[256,1152]{1,0:T(8,128)(2,1)S(1)} %add_convert_fusion.1), channel_id=1, source_target_pairs={{0,2},{1,3},{2,0},{3,1},{4,6},{5,7},{6,4},{7,5},{8,10},{9,11},{10,... | collective-permute-start | bytes 1769480 | tf_op jit(solution)/shard_map/ppermute | solution.py:350
  167.5 28.6 %copy-start.5 = (bf16[16,64,2048]{2,1,0:T(8,128)(2,1)S(1)}, bf16[16,64,2048]{2,1,0:T(8,128)(2,1)}, u32[]{:S(2)}) copy-start(bf16[16,64,2048]{2,1,0:T(8,128)(2,1)} %get-tuple-element.40.cs_ref) | copy-start | bytes 12582916
  167.6 27.0 %collective-permute-start.17 = (bf16[64,1024]{1,0:T(8,128)(2,1)S(1)}, bf16[64,1024]{1,0:T(8,128)(2,1)S(1)}, u32[]{:S(2)}, u32[]{:S(2)}) collective-permute-start(bf16[64,1024]{1,0:T(8,128)(2,1)S(1)} %get-tuple-element.61), channel_id=1, source_target_pairs={{0,4},{4,8},{8,12},{12,0},{1,5},{5,9},{9,13},{13,1},{2,6},{6,10},{... | collective-permute-start | bytes 393224 | tf_op jit(solution)/shard_map/ppermute | solution.py:345
  179.7 29.4 %collective-permute-start.23 = (bf16[64,1152]{1,0:T(8,128)(2,1)S(1)}, bf16[64,1152]{1,0:T(8,128)(2,1)S(1)}, u32[]{:S(2)}, u32[]{:S(2)}) collective-permute-start(bf16[64,1152]{1,0:T(8,128)(2,1)S(1)} %get-tuple-element.57), channel_id=1, source_target_pairs={{0,4},{4,8},{8,12},{12,0},{1,5},{5,9},{9,13},{13,1},{2,6},{6,10},{... | collective-permute-start | bytes 442376 | tf_op jit(solution)/shard_map/ppermute | solution.py:345
  189.8 19.4 %collective-permute-start.22 = (bf16[64,1152]{1,0:T(8,128)(2,1)S(1)}, bf16[64,1152]{1,0:T(8,128)(2,1)S(1)}, u32[]{:S(2)}, u32[]{:S(2)}) collective-permute-start(bf16[64,1152]{1,0:T(8,128)(2,1)S(1)} %get-tuple-element.58), channel_id=1, source_target_pairs={{0,8},{4,12},{8,0},{12,4},{1,9},{5,13},{9,1},{13,5},{2,10},{6,14},... | collective-permute-start | bytes 442376 | tf_op jit(solution)/shard_map/ppermute | solution.py:345
  191.8 17.4 %collective-permute-start.21 = (bf16[64,1152]{1,0:T(8,128)(2,1)S(1)}, bf16[64,1152]{1,0:T(8,128)(2,1)S(1)}, u32[]{:S(2)}, u32[]{:S(2)}) collective-permute-start(bf16[64,1152]{1,0:T(8,128)(2,1)S(1)} %get-tuple-element.59), channel_id=1, source_target_pairs={{0,12},{4,0},{8,4},{12,8},{1,13},{5,1},{9,5},{13,9},{2,14},{6,2},{... | collective-permute-start | bytes 442376 | tf_op jit(solution)/shard_map/ppermute | solution.py:345
  194.6 14.5 %collective-permute-start.16 = (bf16[64,1024]{1,0:T(8,128)(2,1)S(1)}, bf16[64,1024]{1,0:T(8,128)(2,1)S(1)}, u32[]{:S(2)}, u32[]{:S(2)}) collective-permute-start(bf16[64,1024]{1,0:T(8,128)(2,1)S(1)} %get-tuple-element.62), channel_id=1, source_target_pairs={{0,8},{4,12},{8,0},{12,4},{1,9},{5,13},{9,1},{13,5},{2,10},{6,14},... | collective-permute-start | bytes 393224 | tf_op jit(solution)/shard_map/ppermute | solution.py:345
  194.6 14.5 %collective-permute-start.15 = (bf16[64,1024]{1,0:T(8,128)(2,1)S(1)}, bf16[64,1024]{1,0:T(8,128)(2,1)S(1)}, u32[]{:S(2)}, u32[]{:S(2)}) collective-permute-start(bf16[64,1024]{1,0:T(8,128)(2,1)S(1)} %get-tuple-element.63), channel_id=1, source_target_pairs={{0,12},{4,0},{8,4},{12,8},{1,13},{5,1},{9,5},{13,9},{2,14},{6,2},{... | collective-permute-start | bytes 393224 | tf_op jit(solution)/shard_map/ppermute | solution.py:345

commit v2 on v1

--- a/solution.py
+++ b/solution.py
@@ -9,6 +9,7 @@
 
 MOST = 4
 META = 128
+OVER = 2
 BF = jnp.bfloat16
 F32 = jnp.float32
 VMEM_BYTES = 48 * 1024 * 1024
@@ -32,6 +33,13 @@
 
 def cost(flops, moved):
     return pl.CostEstimate(flops=int(flops), bytes_accessed=int(moved), transcendentals=0)
+
+
+def step_of(experts, most):
+    step = 1
+    while step * 2 <= most and experts % (step * 2) == 0:
+        step *= 2
+    return step
 
 
 def whole(array):
@@ -62,16 +70,20 @@
     shard, local, rank, place = route_columns(ids, per_device)
     slot = jnp.where(place < room, shard * room + place, -1.0).astype(jnp.int32)
     lanes = lax.broadcasted_iota(jnp.int32, (ids.shape[0], n_shards * room), 1)
-    return jnp.where(lanes == slot, 1.0, 0.0).astype(BF), local * MOST + rank + 1.0
+    over = jnp.max(place, axis=0, keepdims=True) >= room
+    return jnp.where(lanes == slot, 1.0, 0.0).astype(BF), local * MOST + rank + 1.0, over
 
 
 def pack_kernel(per_device, room, n_shards, ids_ref, tok_ref, cot_ref, wgt_ref, x_ref, c_ref):
-    table, tag = slot_table(ids_ref[...], per_device, room, n_shards)
+    table, tag, over = slot_table(ids_ref[...], per_device, room, n_shards)
     width = tok_ref.shape[1]
     x_ref[:, :width] = dot_tn(table, tok_ref[...]).astype(BF)
     lane = lax.broadcasted_iota(jnp.int32, (tag.shape[0], META), 1)
     info = jnp.where(lane == 0, tag, jnp.where(lane == 1, wgt_ref[...].astype(F32), 0.0))
-    x_ref[:, width:] = dot_tn(table, info.astype(BF)).astype(BF)
+    packed = dot_tn(table, info.astype(BF))
+    lane = lax.broadcasted_iota(jnp.int32, packed.shape, 1)
+    flag = jnp.broadcast_to(jnp.where(over, 1.0, 0.0), packed.shape)
+    x_ref[:, width:] = jnp.where(lane == OVER, flag, packed).astype(BF)
     c_ref[...] = dot_tn(table, cot_ref[...]).astype(BF)
 
 
@@ -132,23 +144,26 @@
             table = sorted_table(x_refs[d][:, width : width + META], room, n_shards, n_sorted)
             spread(table, x_refs[d], width, xs, d)
 
-    x_block = xs[pl.program_id(0)]
-    g_ref[0] = dot_nt(x_block, gate_ref[0])
-    u_ref[0] = dot_nt(x_block, up_ref[0])
+    step = gate_ref.shape[0]
+    for i in range(step):
+        x_block = xs[pl.program_id(0) * step + i]
+        g_ref[i] = dot_nt(x_block, gate_ref[i])
+        u_ref[i] = dot_nt(x_block, up_ref[i])
 
 
 def first_layer(x_list, gate, up, room, n_shards):
     n_dp = len(x_list)
     experts, hidden, width = gate.shape
     expert_rows = n_dp * n_shards * MOST
+    step = step_of(experts, 4)
     by_expert = lambda e: (e, 0, 0)
     shape = jax.ShapeDtypeStruct((experts, expert_rows, hidden), F32)
     return pl.pallas_call(
         functools.partial(first_kernel, n_dp, room, n_shards),
-        grid=(experts,),
+        grid=(experts // step,),
         in_specs=[whole(x) for x in x_list]
-        + [pl.BlockSpec((1, hidden, width), by_expert)] * 2,
-        out_specs=[pl.BlockSpec((1, expert_rows, hidden), by_expert)] * 2,
+        + [pl.BlockSpec((step, hidden, width), by_expert)] * 2,
+        out_specs=[pl.BlockSpec((step, expert_rows, hidden), by_expert)] * 2,
         out_shape=[shape, shape],
         scratch_shapes=[pltpu.VMEM((experts, expert_rows, width), BF)],
         compiler_params=params(),
@@ -171,21 +186,23 @@
             spread(table, c_refs[d], width, cs, d)
             spread(table, m_refs[d], META, ms, d, META)
 
-    at = pl.program_id(0)
-    c_block = cs[at]
-    cs_ref[0] = c_block
-    weight = ms[at][:, 1:2].astype(F32)
-    back = dot_nt(c_block, down_ref[0])
-    g, u = g_ref[0], u_ref[0]
-    sig = jax.nn.sigmoid(g)
-    act = g * sig
-    hidden = act * u
-    router = jnp.sum(hidden.astype(BF).astype(F32) * back, axis=1, keepdims=True)
-    r_ref[0] = jnp.broadcast_to(router, (expert_rows, META)).astype(BF)
-    hw_ref[0] = (hidden * weight).astype(BF)
-    scaled = back * weight
-    dg_ref[0] = (scaled * u * (sig * (1.0 + g * (1.0 - sig)))).astype(BF)
-    du_ref[0] = (scaled * act).astype(BF)
+    step = g_ref.shape[0]
+    for i in range(step):
+        at = pl.program_id(0) * step + i
+        c_block = cs[at]
+        cs_ref[i] = c_block
+        weight = ms[at][:, 1:2].astype(F32)
+        back = dot_nt(c_block, down_ref[i])
+        g, u = g_ref[i], u_ref[i]
+        sig = jax.nn.sigmoid(g)
+        act = g * sig
+        hidden = act * u
+        router = jnp.sum(hidden.astype(BF).astype(F32) * back, axis=1, keepdims=True)
+        r_ref[i] = jnp.broadcast_to(router, (expert_rows, META)).astype(BF)
+        hw_ref[i] = (hidden * weight).astype(BF)
+        scaled = back * weight
+        dg_ref[i] = (scaled * u * (sig * (1.0 + g * (1.0 - sig)))).astype(BF)
+        du_ref[i] = (scaled * act).astype(BF)
 
 
 def second_layer(x_list, c_list, g, u, down, room, n_shards):
@@ -193,20 +210,21 @@
     experts, hidden, width = down.shape
     expert_rows = g.shape[1]
     slots = c_list[0].shape[0]
+    step = step_of(experts, 4)
     by_expert = lambda e: (e, 0, 0)
     small = jax.ShapeDtypeStruct((experts, expert_rows, hidden), BF)
-    small_spec = pl.BlockSpec((1, expert_rows, hidden), by_expert)
+    small_spec = pl.BlockSpec((step, expert_rows, hidden), by_expert)
     return pl.pallas_call(
         functools.partial(second_kernel, n_dp, room, n_shards),
-        grid=(experts,),
+        grid=(experts // step,),
         in_specs=[pl.BlockSpec((slots, META), lambda e: (0, width // META))] * n_dp
         + [whole(c) for c in c_list]
         + [small_spec] * 2
-        + [pl.BlockSpec((1, hidden, width), by_expert)],
+        + [pl.BlockSpec((step, hidden, width), by_expert)],
         out_specs=[small_spec] * 3
         + [
-            pl.BlockSpec((1, expert_rows, width), by_expert),
-            pl.BlockSpec((1, expert_rows, META), by_expert),
+            pl.BlockSpec((step, expert_rows, width), by_expert),
+            pl.BlockSpec((step, expert_rows, META), by_expert),
         ],
         out_shape=[small] * 3
         + [
@@ -231,23 +249,22 @@
     if with_router:
         r_ref, rest = rest[0], rest[1:]
     out_refs, acc = rest[:n_dp], rest[n_dp]
-    experts, expert_rows = pl.num_programs(0), dg_ref.shape[1]
-    _, _, per_expert, width = acc.shape
-    part = gate_ref.shape[2]
-    at = pl.program_id(0)
-    grad = dot_nn(dg_ref[0], gate_ref[0]) + dot_nn(du_ref[0], up_ref[0])
-    grad = grad.astype(BF)
-    for d in range(n_dp):
-        low = d * per_expert
-        acc[d, at, :, :part] = grad[low : low + per_expert]
-        if with_router:
-            acc[d, at, :, part:] = r_ref[0, low : low + per_expert]
-
-    @pl.when(at == acc.shape[1] - 1)
+    _, experts, per_expert, width = acc.shape
+    step, _, part = gate_ref.shape
+    for i in range(step):
+        at = pl.program_id(0) * step + i
+        grad = (dot_nn(dg_ref[i], gate_ref[i]) + dot_nn(du_ref[i], up_ref[i])).astype(BF)
+        for d in range(n_dp):
+            low = d * per_expert
+            acc[d, at, :, :part] = grad[low : low + per_expert]
+            if with_router:
+                acc[d, at, :, part:] = r_ref[i, low : low + per_expert]
+
+    @pl.when(pl.program_id(0) == pl.num_programs(0) - 1)
     def _():
         for d in range(n_dp):
-            table = sorted_table(m_refs[d][...], room, n_shards, acc.shape[1] * per_expert)
-            rows = acc[d].reshape(acc.shape[1] * per_expert, width)
+            table = sorted_table(m_refs[d][...], room, n_shards, experts * per_expert)
+            rows = acc[d].reshape(experts * per_expert, width)
             out_refs[d][...] = dot_nn(table, rows).astype(BF)
 
 
@@ -258,18 +275,19 @@
     slots = x_list[0].shape[0]
     part = full // n_half
     width = part + (0 if router is None else META)
+    step = step_of(experts, 4)
     by_expert = lambda e: (e, 0, 0)
-    small_spec = pl.BlockSpec((1, expert_rows, hidden), by_expert)
-    weight_spec = pl.BlockSpec((1, hidden, part), lambda e: (e, 0, half))
+    small_spec = pl.BlockSpec((step, expert_rows, hidden), by_expert)
+    weight_spec = pl.BlockSpec((step, hidden, part), lambda e: (e, 0, half))
     args = [*x_list, dg, du, gate, up]
     specs = [pl.BlockSpec((slots, META), lambda e: (0, full // META))] * n_dp
     specs += [small_spec] * 2 + [weight_spec] * 2
     if router is not None:
         args.append(router)
-        specs.append(pl.BlockSpec((1, expert_rows, META), by_expert))
+        specs.append(pl.BlockSpec((step, expert_rows, META), by_expert))
     return pl.pallas_call(
         functools.partial(third_kernel, n_dp, room, n_shards, router is not None),
-        grid=(experts,),
+        grid=(experts // step,),
         in_specs=specs,
         out_specs=[pl.BlockSpec((slots, width), lambda e: (0, 0))] * n_dp,
         out_shape=[jax.ShapeDtypeStruct((slots, width), BF)] * n_dp,
@@ -281,21 +299,23 @@
 
 
 def down_kernel(hw_ref, cs_ref, out_ref):
-    out_ref[0] = dot_tn(hw_ref[0], cs_ref[0]).astype(BF)
+    for i in range(hw_ref.shape[0]):
+        out_ref[i] = dot_tn(hw_ref[i], cs_ref[i]).astype(BF)
 
 
 def down_layer(hw, cs):
     experts, rows, hidden = hw.shape
     width = cs.shape[2]
+    step = step_of(experts, 4)
     by_expert = lambda e: (e, 0, 0)
     return pl.pallas_call(
         down_kernel,
-        grid=(experts,),
+        grid=(experts // step,),
         in_specs=[
-            pl.BlockSpec((1, rows, hidden), by_expert),
-            pl.BlockSpec((1, rows, width), by_expert),
-        ],
-        out_specs=pl.BlockSpec((1, hidden, width), by_expert),
+            pl.BlockSpec((step, rows, hidden), by_expert),
+            pl.BlockSpec((step, rows, width), by_expert),
+        ],
+        out_specs=pl.BlockSpec((step, hidden, width), by_expert),
         out_shape=jax.ShapeDtypeStruct((experts, hidden, width), BF),
         compiler_params=params(),
         cost_estimate=cost(1e9, 1.8e7),
@@ -304,7 +324,7 @@
 
 
 def home_kernel(per_device, room, n_shards, n_half, n_blocks, ids_ref, *refs):
-    table, _ = slot_table(ids_ref[...], per_device, room, n_shards)
+    table, _, _ = slot_table(ids_ref[...], per_device, room, n_shards)
     blocks, (tok_ref, route_ref) = refs[:-2], refs[-2:]
     part = tok_ref.shape[1] // n_half
     size = n_shards * room // n_blocks
@@ -402,13 +422,18 @@
     return have[0]
 
 
-def run(room, ids, tokens, out_grad, route_weight, gate, up, down):
+def begin(room, ids, tokens, out_grad, route_weight, per_device):
+    n_shards = lax.axis_size("expert")
+    send_x, send_c = pack_rows(ids, tokens, out_grad, route_weight, per_device, room, n_shards)
+    own_x = to_shards(send_x, room, n_shards)
+    send_c, own_x = lax.optimization_barrier((send_c, own_x))
+    return own_x, to_shards(send_c, room, n_shards)
+
+
+def finish(room, ids, x_list, own_c, gate, up, down):
     n_shards, n_dp = lax.axis_size("expert"), lax.axis_size("dp")
-    per_device, width = gate.shape[0], tokens.shape[1]
-    gate, up = jnp.swapaxes(gate, 1, 2), jnp.swapaxes(up, 1, 2)
-    send_x, send_c = pack_rows(ids, tokens, out_grad, route_weight, per_device, room, n_shards)
-    x_list = gather_dp(to_shards(send_x, room, n_shards), n_dp)
-    c_list = gather_dp(to_shards(send_c, room, n_shards), n_dp)
+    per_device, width = gate.shape[0], down.shape[2]
+    c_list = gather_dp(own_c, n_dp)
     g, u = first_layer(x_list, gate, up, room, n_shards)
     dg, du, hw, cs, router = second_layer(x_list, c_list, g, u, down, room, n_shards)
     n_half = 2
@@ -424,15 +449,42 @@
     return token_grad, route[:, :1], down_grad
 
 
+def agreed(own_x, width, n_dp):
+    flag = jnp.max(own_x[:, width + OVER : width + OVER + 1].astype(F32))
+    flag = jnp.broadcast_to(flag, (8, 128))
+    for step in range(1, lax.axis_size("groups")):
+        flag = jnp.maximum(flag, shifted(flag, "groups", step))
+    for bit in dp_bits(n_dp):
+        flag = jnp.maximum(flag, swapped(flag, "dp", bit))
+    return flag[0, 0]
+
+
 def shards(tokens, out_grad, route_weight, expert_ids, gate, up, down):
-    n_shards = lax.axis_size("expert")
-    per_device = gate.shape[0]
-    slot_rows = min(expert_ids.shape[0], per_device * MOST)
+    n_shards, n_dp = lax.axis_size("expert"), lax.axis_size("dp")
+    per_device, width = gate.shape[0], tokens.shape[1]
+    most_rows = min(expert_ids.shape[0], per_device * MOST)
     ids = expert_ids
     if direct(n_shards):
         total = n_shards * per_device
         ids = (ids - lax.axis_index("expert") * per_device + total) % total
-    return run(slot_rows, ids, tokens, out_grad, route_weight, gate, up, down)
+    gate, up = jnp.swapaxes(gate, 1, 2), jnp.swapaxes(up, 1, 2)
+    usual = most_rows * 5 // 8
+    adaptive = direct(n_shards) and usual % 8 == 0 and (n_shards * usual) % 16 == 0
+    room = usual if adaptive else most_rows
+    own_x, own_c = begin(room, ids, tokens, out_grad, route_weight, per_device)
+    x_list = gather_dp(own_x, n_dp)
+    if not adaptive:
+        return finish(room, ids, x_list, own_c, gate, up, down)
+    over = agreed(own_x, width, n_dp)
+
+    def fits(_):
+        return finish(room, ids, x_list, own_c, gate, up, down)
+
+    def full(_):
+        full_x, full_c = begin(most_rows, ids, tokens, out_grad, route_weight, per_device)
+        return finish(most_rows, ids, gather_dp(full_x, n_dp), full_c, gate, up, down)
+
+    return lax.cond(over > 0.0, full, fits, 0)
 
 
 def solution(mesh):

time: 215 us -> 147 us (0.68); the launches traced: 212 us -> 147 us
  Pallas kernels: 76.4 us -> 48 us
  starting transfers between devices: 55.4 us -> 27.9 us
  waiting for transfers between devices: 70.2 us -> 63.4 us
  local copies, waits for them, and re-layouts: 7 us -> 3.24 us
    ppermute x12 -> x13, starting transfers between devices: 47.8 us -> 19.9 us  [shifted(): return lax.ppermute(value, axis, [(i, (i + step) % n) for i in range(n)])]
    pallas_call x2, Pallas kernels: 26.3 us -> 14.5 us  [third_layer(): pl.pallas_call(functools.partial(third_kernel, n_dp, room, n_shards, rout...]
    pallas_call x1, Pallas kernels: 17.3 us -> 10.4 us  [second_layer(): pl.pallas_call(functools.partial(second_kernel, n_dp, room, n_shards), gr...]
    pallas_call x1, Pallas kernels: 19.4 us -> 13.6 us  [first_layer(): pl.pallas_call(functools.partial(first_kernel, n_dp, room, n_shards), gri...]
    unnamed x24 -> x7, local copies, waits for them, and re-layouts: 6.5 us -> 1.58 us
    pallas_call x1, Pallas kernels: 10.5 us -> 6.36 us  [down_layer(): pl.pallas_call(down_kernel, grid=(experts // step,), in_specs=[pl.BlockSp...]
    ppermute x12 -> x14, waiting for transfers between devices: 39.6 us -> 36 us  [swapped(): return lax.ppermute(value, axis, [(i, i ^ bit) for i in range(n)])]
    ppermute x12 -> x13, waiting for transfers between devices: 30.7 us -> 27.4 us  [shifted(): return lax.ppermute(value, axis, [(i, (i + step) % n) for i in range(n)])]
  transfers between devices with their start and end apart: 24 -> 27, of which waited for: 8 -> 10; matrix products, arithmetic and copies ran while one was open for 1% -> 2% of each run, Pallas kernels for 20% -> 19%
where the time goes in v2:
time: 147 us
  waiting for transfers between devices  63.4 us (43%)
  Pallas kernels  48 us (33%)
  starting transfers between devices  27.9 us (19%)
  local copies, waits for them, and re-layouts  3.24 us (2%)
  between operations  2.07 us (1%)
  other arithmetic  1.98 us (1%)
    ppermute x14, waiting for transfers between devices, swapped(): return lax.ppermute(value, axis, [(i, i ^ bit) for i in range(n)])  36 us
    ppermute x13, waiting for transfers between devices, shifted(): return lax.ppermute(value, axis, [(i, (i + step) % n) for i in range(n)])  27.4 us
    ppermute x13, starting transfers between devices, shifted(): return lax.ppermute(value, axis, [(i, (i + step) % n) for i in range(n)])  19.9 us
    pallas_call x2, Pallas kernels, third_layer(): pl.pallas_call(functools.partial(third_kernel, n_dp, room, n_shards, rout...  14.5 us
    pallas_call x1, Pallas kernels, first_layer(): pl.pallas_call(functools.partial(first_kernel, n_dp, room, n_shards), gri...  13.6 us
    pallas_call x1, Pallas kernels, second_layer(): pl.pallas_call(functools.partial(second_kernel, n_dp, room, n_shards), gr...  10.4 us
    ppermute x14, starting transfers between devices, swapped(): return lax.ppermute(value, axis, [(i, i ^ bit) for i in range(n)])  7.99 us
    pallas_call x1, Pallas kernels, down_layer(): pl.pallas_call(down_kernel, grid=(experts // step,), in_specs=[pl.BlockSp...  6.36 us
  transfers between devices with their start and end apart: 27, of which 10 were waited for; matrix products, arithmetic and copies ran while one was open for 2% of the time, Pallas kernels for 19%

profile of v2, /device:TPU:0, one launch (start us, length us, event | category | flops | bytes accessed | tf_op | source)
XLA Modules:
  0.0 146.9 jit_solution(2791693295232587943)
XLA Ops:
  0.6 0.7 broadcast_compare_fusion
  1.3 0.1 copy.29
  1.4 0.8 copy.30.wgt_ref
  2.2 0.1 copy.26
  2.4 2.0 %pack_rows.3 = (bf16[160,2176]{1,0:T(8,128)(2,1)S(1)}, bf16[160,2048]{1,0:T(8,128)(2,1)S(1)}) custom-call(s32[128,1]{1,0:T(8,128)S(1)} %add_select_fusion.ids_ref, bf16[128,2048]{1,0:T(8,128)(2,1)} %tok_ref.1, bf16[128,2048]{1,0:T(8,128)(2,1)} %cot_ref.1, bf16[128,1]{1,0:T(8,128)(2,1)S(1)} %copy.30.wgt_ref), custom_call_target="tpu_custom_call" | custom-call | flops 400000000 | bytes 4000000 | tf_op jit(solution)/shard_map/pack_rows/pallas_call | solution.py:93
  4.5 5.1 %collective-permute-start.41 = (bf16[40,2176]{1,0:T(8,128)(2,1)S(1)}, bf16[40,2176]{1,0:T(8,128)(2,1)S(1)}, u32[]{:S(2)}, u32[]{:S(2)}) collective-permute-start(bf16[40,2176]{1,0:T(8,128)(2,1)S(1)} %get-tuple-element.147), channel_id=1, source_target_pairs={{0,12},{4,0},{8,4},{12,8},{1,13},{5,1},{9,5},{13,9},{2,14},{6,2},{... | collective-permute-start | bytes 522248 | tf_op jit(solution)/shard_map/ppermute | solution.py:365
  9.6 1.0 collective-permute-start.39
  10.6 3.8 %collective-permute-done.41 = bf16[40,2176]{1,0:T(8,128)(2,1)S(1)} collective-permute-done((bf16[40,2176]{1,0:T(8,128)(2,1)S(1)}, bf16[40,2176]{1,0:T(8,128)(2,1)S(1)}, u32[]{:S(2)}, u32[]{:S(2)}) %collective-permute-start.41) | collective-permute-done | bytes 174112 | tf_op jit(solution)/shard_map/ppermute | solution.py:365
  14.5 9.9 %collective-permute-done.40 = bf16[40,2176]{1,0:T(8,128)(2,1)S(1)} collective-permute-done((bf16[40,2176]{1,0:T(8,128)(2,1)S(1)}, bf16[40,2176]{1,0:T(8,128)(2,1)S(1)}, u32[]{:S(2)}, u32[]{:S(2)}) %collective-permute-start.40) | collective-permute-done | bytes 174112 | tf_op jit(solution)/shard_map/ppermute | solution.py:365
  24.4 1.6 %collective-permute-start.49 = (bf16[160,2176]{1,0:T(8,128)(2,1)S(1)}, bf16[160,2176]{1,0:T(8,128)(2,1)S(1)}, u32[]{:S(2)}, u32[]{:S(2)}) collective-permute-start(bf16[160,2176]{1,0:T(8,128)(2,1)S(1)} %pad_maximum_fusion.2), channel_id=1, source_target_pairs={{0,2},{1,3},{2,0},{3,1},{4,6},{5,7},{6,4},{7,5},{8,10},{9,11},{10,... | collective-permute-start | bytes 2088968 | tf_op jit(solution)/shard_map/ppermute | solution.py:370
  26.0 0.7 slice_reduce_fusion
  26.7 0.6 broadcast_in_dim.3
  27.3 1.6 %collective-permute-start.42 = (f32[8,128]{1,0:T(8,128)S(1)}, f32[8,128]{1,0:T(8,128)S(1)}, u32[]{:S(2)}, u32[]{:S(2)}) collective-permute-start(f32[8,128]{1,0:T(8,128)S(1)} %broadcast_in_dim.3), channel_id=1, source_target_pairs={{0,16},{16,0},{1,17},{17,1},{2,18},{18,2},{3,19},{19,3},{4,20},{20... | collective-permute-start | bytes 12296 | tf_op jit(solution)/shard_map/ppermute | solution.py:365
  29.6 1.4 collective-permute-done.42
  31.0 0.5 collective-permute-start.48
  31.5 0.7 collective-permute-done.43
  32.2 0.5 collective-permute-start.44
  32.7 9.0 %collective-permute-done.49 = bf16[160,2176]{1,0:T(8,128)(2,1)S(1)} collective-permute-done((bf16[160,2176]{1,0:T(8,128)(2,1)S(1)}, bf16[160,2176]{1,0:T(8,128)(2,1)S(1)}, u32[]{:S(2)}, u32[]{:S(2)}) %collective-permute-start.49) | collective-permute-done | bytes 696352 | tf_op jit(solution)/shard_map/ppermute | solution.py:370
  41.8 2.4 %collective-permute-start.46 = (bf16[40,2048]{1,0:T(8,128)(2,1)S(1)}, bf16[40,2048]{1,0:T(8,128)(2,1)S(1)}, u32[]{:S(2)}, u32[]{:S(2)}) collective-permute-start(bf16[40,2048]{1,0:T(8,128)(2,1)S(1)} %get-tuple-element.152), channel_id=1, source_target_pairs={{0,8},{4,12},{8,0},{12,4},{1,9},{5,13},{9,1},{13,5},{2,10},{6,14},... | collective-permute-start | bytes 491528 | tf_op jit(solution)/shard_map/ppermute | solution.py:365
  44.3 1.9 %collective-permute-start.45 = (bf16[40,2048]{1,0:T(8,128)(2,1)S(1)}, bf16[40,2048]{1,0:T(8,128)(2,1)S(1)}, u32[]{:S(2)}, u32[]{:S(2)}) collective-permute-start(bf16[40,2048]{1,0:T(8,128)(2,1)S(1)} %get-tuple-element.153), channel_id=1, source_target_pairs={{0,4},{4,8},{8,12},{12,0},{1,5},{5,9},{9,13},{13,1},{2,6},{6,10},{... | collective-permute-start | bytes 491528 | tf_op jit(solution)/shard_map/ppermute | solution.py:365
  46.2 0.5 slice.113
  47.4 1.0 collective-permute-done.47
  48.4 11.2 %collective-permute-done.46 = bf16[40,2048]{1,0:T(8,128)(2,1)S(1)} collective-permute-done((bf16[40,2048]{1,0:T(8,128)(2,1)S(1)}, bf16[40,2048]{1,0:T(8,128)(2,1)S(1)}, u32[]{:S(2)}, u32[]{:S(2)}) %collective-permute-start.46) | collective-permute-done | bytes 163872 | tf_op jit(solution)/shard_map/ppermute | solution.py:365
  59.7 86.4 %conditional.1 = (bf16[128,2048]{1,0:T(8,128)(2,1)S(1)}, bf16[16,192,2048]{2,1,0:T(8,128)(2,1)}, bf16[128,1]{0,1:T(2,128)(2,1)S(1)}) conditional(s32[]{:T(128)} %bitcast, (bf16[160,2048]{1,0:T(8,128)(2,1)S(1)}, bf16[160,2176]{1,0:T(8,128)(2,1)S(1)}, bf16[160,2176]{1,0:T(8,128)(2,1)S(1)}, bf16[160,2176]{1,0:T(8,128)(2,1)S(1)}, ...), branch_computations={%region_1.2_spmd, %region_2.3_spmd} | conditional | flops 7615335424 | bytes 221639296 | solution.py:487
  59.7 1.6 %collective-permute-start.1 = (bf16[160,2048]{1,0:T(8,128)(2,1)S(1)}, bf16[160,2048]{1,0:T(8,128)(2,1)S(1)}, u32[]{:S(2)}, u32[]{:S(2)}) collective-permute-start(bf16[160,2048]{1,0:T(8,128)(2,1)S(1)} %get-tuple-element.37.refs_4_), channel_id=1, source_target_pairs={{0,2},{1,3},{2,0},{3,1},{4,6},{5,7},{6,4},{7,5},{8,10},{9,11},{10,... | collective-permute-start | bytes 1966088 | tf_op jit(solution)/shard_map/cond/branch_0_fun/ppermute | solution.py:370
  61.3 15.0 %collective-permute-done.1.refs_6_ = bf16[160,2048]{1,0:T(8,128)(2,1)S(1)} collective-permute-done((bf16[160,2048]{1,0:T(8,128)(2,1)S(1)}, bf16[160,2048]{1,0:T(8,128)(2,1)S(1)}, u32[]{:S(2)}, u32[]{:S(2)}) %collective-permute-start.1) | collective-permute-done | bytes 655392 | tf_op jit(solution)/shard_map/cond/branch_0_fun/ppermute | solution.py:370
  76.3 13.6 %gate_up.2 = (f32[16,64,192]{2,1,0:T(8,128)S(1)}, f32[16,64,192]{2,1,0:T(8,128)S(1)}) custom-call(bf16[160,2176]{1,0:T(8,128)(2,1)S(1)} %get-tuple-element.33.refs_0_, bf16[160,2176]{1,0:T(8,128)(2,1)S(1)} %get-tuple-element.34.refs_1_, bf16[160,2176]{1,0:T(8,128)(2,1)S(1)} %get-tuple-element.35.refs_2_, bf16[160,2176]{1,0:T(8,128)(2,1)S(1)} %get-tuple-element.36.refs_3_, ...), custom_call_target="tpu_custom_call" | custom-call | flops 2000000000 | bytes 30000000 | tf_op jit(solution)/shard_map/cond/branch_0_fun/gate_up/pallas_call | solution.py:161
  90.0 10.4 %hidden_grads.2 = (bf16[16,64,192]{2,1,0:T(8,128)(2,1)S(1)}, bf16[16,64,192]{2,1,0:T(8,128)(2,1)S(1)}, bf16[16,64,192]{2,1,0:T(8,128)(2,1)S(1)}, bf16[16,64,2048]{2,1,0:T(8,128)(2,1)}, bf16[16,64,128]{2,1,0:T(8,128)(2,1)S(1)}) custom-call(bf16[160,2176]{1,0:T(8,128)(2,1)S(1)} %get-tuple-element.33.refs_0_, bf16[160,2176]{1,0:T(8,128)(2,1)S(1)} %get-tuple-element.34.refs_1_, ...), custom_call_target="tpu_custom_call" | custom-call | flops 2000000000 | bytes 20000000 | tf_op jit(solution)/shard_map/cond/branch_0_fun/hidden_grads/pallas_call | solution.py:217
  100.4 7.2 %input_grads.4 = (bf16[160,1024]{1,0:T(8,128)(2,1)S(1)}, bf16[160,1024]{1,0:T(8,128)(2,1)S(1)}, bf16[160,1024]{1,0:T(8,128)(2,1)S(1)}, bf16[160,1024]{1,0:T(8,128)(2,1)S(1)}) custom-call(bf16[160,2176]{1,0:T(8,128)(2,1)S(1)} %get-tuple-element.33.refs_0_, bf16[160,2176]{1,0:T(8,128)(2,1)S(1)} %get-tuple-element.34.refs_1_, ...), custom_call_target="tpu_custom_call" | custom-call | flops 1000000000 | bytes 15000000 | tf_op jit(solution)/shard_map/cond/branch_0_fun/input_grads/pallas_call | solution.py:288
  107.7 0.6 collective-permute-start.4
  108.2 7.3 %input_grads.5 = (bf16[160,1152]{1,0:T(8,128)(2,1)S(1)}, bf16[160,1152]{1,0:T(8,128)(2,1)S(1)}, bf16[160,1152]{1,0:T(8,128)(2,1)S(1)}, bf16[160,1152]{1,0:T(8,128)(2,1)S(1)}) custom-call(bf16[160,2176]{1,0:T(8,128)(2,1)S(1)} %get-tuple-element.33.refs_0_, bf16[160,2176]{1,0:T(8,128)(2,1)S(1)} %get-tuple-element.34.refs_1_, ...), custom_call_target="tpu_custom_call" | custom-call | flops 1000000000 | bytes 15000000 | tf_op jit(solution)/shard_map/cond/branch_0_fun/input_grads/pallas_call | solution.py:288
  115.5 0.1 collective-permute-start.10
  115.6 0.5 collective-permute-start.3
  116.2 0.1 add_convert_fusion.4
  116.3 1.6 %collective-permute-start.5 = (bf16[160,1024]{1,0:T(8,128)(2,1)S(1)}, bf16[160,1024]{1,0:T(8,128)(2,1)S(1)}, u32[]{:S(2)}, u32[]{:S(2)}) collective-permute-start(bf16[160,1024]{1,0:T(8,128)(2,1)S(1)} %add_convert_fusion.4), channel_id=1, source_target_pairs={{0,2},{1,3},{2,0},{3,1},{4,6},{5,7},{6,4},{7,5},{8,10},{9,11},{10,... | collective-permute-start | bytes 983048 | tf_op jit(solution)/shard_map/cond/branch_0_fun/ppermute | solution.py:370
  118.0 1.0 collective-permute-start.11
  118.9 7.9 %collective-permute-done.5 = bf16[160,1024]{1,0:T(8,128)(2,1)S(1)} collective-permute-done((bf16[160,1024]{1,0:T(8,128)(2,1)S(1)}, bf16[160,1024]{1,0:T(8,128)(2,1)S(1)}, u32[]{:S(2)}, u32[]{:S(2)}) %collective-permute-start.5) | collective-permute-done | bytes 327712 | tf_op jit(solution)/shard_map/cond/branch_0_fun/ppermute | solution.py:370
  126.9 0.2 add_convert_fusion.3
  127.1 0.8 collective-permute-start.7
  127.9 3.1 %collective-permute-start.6 = (bf16[40,1024]{1,0:T(8,128)(2,1)S(1)}, bf16[40,1024]{1,0:T(8,128)(2,1)S(1)}, u32[]{:S(2)}, u32[]{:S(2)}) collective-permute-start(bf16[40,1024]{1,0:T(8,128)(2,1)S(1)} %get-tuple-element.128), channel_id=1, source_target_pairs={{0,12},{4,0},{8,4},{12,8},{1,13},{5,1},{9,5},{13,9},{2,14},{6,2},{... | collective-permute-start | bytes 245768 | tf_op jit(solution)/shard_map/cond/branch_0_fun/ppermute | solution.py:365
  130.9 3.4 %collective-permute-done.11 = bf16[160,1152]{1,0:T(8,128)(2,1)S(1)} collective-permute-done((bf16[160,1152]{1,0:T(8,128)(2,1)S(1)}, bf16[160,1152]{1,0:T(8,128)(2,1)S(1)}, u32[]{:S(2)}, u32[]{:S(2)}) %collective-permute-start.11) | collective-permute-done | bytes 368672 | tf_op jit(solution)/shard_map/cond/branch_0_fun/ppermute | solution.py:370
  134.3 0.1 add_convert_fusion
  134.6 0.8 collective-permute-start.13
  135.3 3.1 %collective-permute-start.12 = (bf16[40,1152]{1,0:T(8,128)(2,1)S(1)}, bf16[40,1152]{1,0:T(8,128)(2,1)S(1)}, u32[]{:S(2)}, u32[]{:S(2)}) collective-permute-start(bf16[40,1152]{1,0:T(8,128)(2,1)S(1)} %get-tuple-element.124), channel_id=1, source_target_pairs={{0,12},{4,0},{8,4},{12,8},{1,13},{5,1},{9,5},{13,9},{2,14},{6,2},{... | collective-permute-start | bytes 276488 | tf_op jit(solution)/shard_map/cond/branch_0_fun/ppermute | solution.py:365
  138.4 6.4 %down_grads.2 = bf16[16,192,2048]{2,1,0:T(8,128)(2,1)} custom-call(bf16[16,64,192]{2,1,0:T(8,128)(2,1)S(1)} %get-tuple-element.56.hw_ref, bf16[16,64,2048]{2,1,0:T(8,128)(2,1)S(1)} %copy-done.6), custom_call_target="tpu_custom_call" | custom-call | flops 1000000000 | bytes 18000000 | tf_op jit(solution)/shard_map/cond/branch_0_fun/down_grads/pallas_call | solution.py:311
  144.8 1.1 home_rows.2
  146.1 0.5 copy-done.11
  146.6 0.3 copy-done.12
  (44 shorter events, 0.8 us)
Async XLA Ops:
  4.5 10.0 %collective-permute-start.41 = (bf16[40,2176]{1,0:T(8,128)(2,1)S(1)}, bf16[40,2176]{1,0:T(8,128)(2,1)S(1)}, u32[]{:S(2)}, u32[]{:S(2)}) collective-permute-start(bf16[40,2176]{1,0:T(8,128)(2,1)S(1)} %get-tuple-element.147), channel_id=1, source_target_pairs={{0,12},{4,0},{8,4},{12,8},{1,13},{5,1},{9,5},{13,9},{2,14},{6,2},{... | collective-permute-start | bytes 522248 | tf_op jit(solution)/shard_map/ppermute | solution.py:365
  9.6 14.8 %collective-permute-start.40 = (bf16[40,2176]{1,0:T(8,128)(2,1)S(1)}, bf16[40,2176]{1,0:T(8,128)(2,1)S(1)}, u32[]{:S(2)}, u32[]{:S(2)}) collective-permute-start(bf16[40,2176]{1,0:T(8,128)(2,1)S(1)} %get-tuple-element.148), channel_id=1, source_target_pairs={{0,8},{4,12},{8,0},{12,4},{1,9},{5,13},{9,1},{13,5},{2,10},{6,14},... | collective-permute-start | bytes 522248 | tf_op jit(solution)/shard_map/ppermute | solution.py:365
  9.6 14.8 %collective-permute-start.39 = (bf16[40,2176]{1,0:T(8,128)(2,1)S(1)}, bf16[40,2176]{1,0:T(8,128)(2,1)S(1)}, u32[]{:S(2)}, u32[]{:S(2)}) collective-permute-start(bf16[40,2176]{1,0:T(8,128)(2,1)S(1)} %get-tuple-element.149), channel_id=1, source_target_pairs={{0,4},{4,8},{8,12},{12,0},{1,5},{5,9},{9,13},{13,1},{2,6},{6,10},{... | collective-permute-start | bytes 522248 | tf_op jit(solution)/shard_map/ppermute | solution.py:365
  24.4 35.3 %copy-start.10 = (bf16[128,1]{0,1:T(2,128)(2,1)S(1)}, bf16[128,1]{0,1:T(2,128)(2,1)}, u32[]{:S(2)}) copy-start(bf16[128,1]{0,1:T(2,128)(2,1)} %param.11) | copy-start | bytes 772
  24.4 17.3 %collective-permute-start.49 = (bf16[160,2176]{1,0:T(8,128)(2,1)S(1)}, bf16[160,2176]{1,0:T(8,128)(2,1)S(1)}, u32[]{:S(2)}, u32[]{:S(2)}) collective-permute-start(bf16[160,2176]{1,0:T(8,128)(2,1)S(1)} %pad_maximum_fusion.2), channel_id=1, source_target_pairs={{0,2},{1,3},{2,0},{3,1},{4,6},{5,7},{6,4},{7,5},{8,10},{9,11},{10,... | collective-permute-start | bytes 2088968 | tf_op jit(solution)/shard_map/ppermute | solution.py:370
  27.3 3.7 %collective-permute-start.42 = (f32[8,128]{1,0:T(8,128)S(1)}, f32[8,128]{1,0:T(8,128)S(1)}, u32[]{:S(2)}, u32[]{:S(2)}) collective-permute-start(f32[8,128]{1,0:T(8,128)S(1)} %broadcast_in_dim.3), channel_id=1, source_target_pairs={{0,16},{16,0},{1,17},{17,1},{2,18},{18,2},{3,19},{19,3},{4,20},{20... | collective-permute-start | bytes 12296 | tf_op jit(solution)/shard_map/ppermute | solution.py:365
  31.0 1.2 collective-permute-start.43
  31.0 28.6 %collective-permute-start.48 = (bf16[160,2176]{1,0:T(8,128)(2,1)S(1)}, bf16[160,2176]{1,0:T(8,128)(2,1)S(1)}, u32[]{:S(2)}, u32[]{:S(2)}) collective-permute-start(bf16[160,2176]{1,0:T(8,128)(2,1)S(1)} %pad_maximum_fusion.2), channel_id=1, source_target_pairs={{0,1},{1,0},{2,3},{3,2},{4,5},{5,4},{6,7},{7,6},{8,9},{9,8},{10,11... | collective-permute-start | bytes 2088968 | tf_op jit(solution)/shard_map/ppermute | solution.py:370
  32.2 12.1 %collective-permute-start.44 = (f32[8,128]{1,0:T(8,128)S(1)}, f32[8,128]{1,0:T(8,128)S(1)}, u32[]{:S(2)}, u32[]{:S(2)}) collective-permute-start(f32[8,128]{1,0:T(8,128)S(1)} %fusion.9), channel_id=1, source_target_pairs={{0,2},{1,3},{2,0},{3,1},{4,6},{5,7},{6,4},{7,5},{8,10},{9,11},{10,... | collective-permute-start | bytes 12296 | tf_op jit(solution)/shard_map/ppermute | solution.py:370
  41.7 18.0 %collective-permute-start.50 = (bf16[160,2176]{1,0:T(8,128)(2,1)S(1)}, bf16[160,2176]{1,0:T(8,128)(2,1)S(1)}, u32[]{:S(2)}, u32[]{:S(2)}) collective-permute-start(bf16[160,2176]{1,0:T(8,128)(2,1)S(1)} %collective-permute-done.49), channel_id=1, source_target_pairs={{0,1},{1,0},{2,3},{3,2},{4,5},{5,4},{6,7},{7,6},{8,9},{9,8},{10,11... | collective-permute-start | bytes 2088968 | tf_op jit(solution)/shard_map/ppermute | solution.py:370
  41.8 6.7 %collective-permute-start.47 = (bf16[40,2048]{1,0:T(8,128)(2,1)S(1)}, bf16[40,2048]{1,0:T(8,128)(2,1)S(1)}, u32[]{:S(2)}, u32[]{:S(2)}) collective-permute-start(bf16[40,2048]{1,0:T(8,128)(2,1)S(1)} %get-tuple-element.151), channel_id=1, source_target_pairs={{0,12},{4,0},{8,4},{12,8},{1,13},{5,1},{9,5},{13,9},{2,14},{6,2},{... | collective-permute-start | bytes 491528 | tf_op jit(solution)/shard_map/ppermute | solution.py:365
  41.8 17.8 %collective-permute-start.46 = (bf16[40,2048]{1,0:T(8,128)(2,1)S(1)}, bf16[40,2048]{1,0:T(8,128)(2,1)S(1)}, u32[]{:S(2)}, u32[]{:S(2)}) collective-permute-start(bf16[40,2048]{1,0:T(8,128)(2,1)S(1)} %get-tuple-element.152), channel_id=1, source_target_pairs={{0,8},{4,12},{8,0},{12,4},{1,9},{5,13},{9,1},{13,5},{2,10},{6,14},... | collective-permute-start | bytes 491528 | tf_op jit(solution)/shard_map/ppermute | solution.py:365
  44.3 15.3 %collective-permute-start.45 = (bf16[40,2048]{1,0:T(8,128)(2,1)S(1)}, bf16[40,2048]{1,0:T(8,128)(2,1)S(1)}, u32[]{:S(2)}, u32[]{:S(2)}) collective-permute-start(bf16[40,2048]{1,0:T(8,128)(2,1)S(1)} %get-tuple-element.153), channel_id=1, source_target_pairs={{0,4},{4,8},{8,12},{12,0},{1,5},{5,9},{9,13},{13,1},{2,6},{6,10},{... | collective-permute-start | bytes 491528 | tf_op jit(solution)/shard_map/ppermute | solution.py:365
  59.7 16.6 %collective-permute-start.1 = (bf16[160,2048]{1,0:T(8,128)(2,1)S(1)}, bf16[160,2048]{1,0:T(8,128)(2,1)S(1)}, u32[]{:S(2)}, u32[]{:S(2)}) collective-permute-start(bf16[160,2048]{1,0:T(8,128)(2,1)S(1)} %get-tuple-element.37.refs_4_), channel_id=1, source_target_pairs={{0,2},{1,3},{2,0},{3,1},{4,6},{5,7},{6,4},{7,5},{8,10},{9,11},{10,... | collective-permute-start | bytes 1966088 | tf_op jit(solution)/shard_map/cond/branch_0_fun/ppermute | solution.py:370
  61.3 28.7 %collective-permute-start = (bf16[160,2048]{1,0:T(8,128)(2,1)S(1)}, bf16[160,2048]{1,0:T(8,128)(2,1)S(1)}, u32[]{:S(2)}, u32[]{:S(2)}) collective-permute-start(bf16[160,2048]{1,0:T(8,128)(2,1)S(1)} %get-tuple-element.37.refs_4_), channel_id=1, source_target_pairs={{0,1},{1,0},{2,3},{3,2},{4,5},{5,4},{6,7},{7,6},{8,9},{9,8},{10,11... | collective-permute-start | bytes 1966088 | tf_op jit(solution)/shard_map/cond/branch_0_fun/ppermute | solution.py:370
  76.3 13.7 %collective-permute-start.2 = (bf16[160,2048]{1,0:T(8,128)(2,1)S(1)}, bf16[160,2048]{1,0:T(8,128)(2,1)S(1)}, u32[]{:S(2)}, u32[]{:S(2)}) collective-permute-start(bf16[160,2048]{1,0:T(8,128)(2,1)S(1)} %collective-permute-done.1.refs_6_), channel_id=1, source_target_pairs={{0,1},{1,0},{2,3},{3,2},{4,5},{5,4},{6,7},{7,6},{8,9},{9,8},{10,11... | collective-permute-start | bytes 1966088 | tf_op jit(solution)/shard_map/cond/branch_0_fun/ppermute | solution.py:370
  107.7 8.5 %collective-permute-start.4 = (bf16[160,1024]{1,0:T(8,128)(2,1)S(1)}, bf16[160,1024]{1,0:T(8,128)(2,1)S(1)}, u32[]{:S(2)}, u32[]{:S(2)}) collective-permute-start(bf16[160,1024]{1,0:T(8,128)(2,1)S(1)} %get-tuple-element.48), channel_id=1, source_target_pairs={{0,1},{1,0},{2,3},{3,2},{4,5},{5,4},{6,7},{7,6},{8,9},{9,8},{10,11... | collective-permute-start | bytes 983048 | tf_op jit(solution)/shard_map/cond/branch_0_fun/ppermute | solution.py:370
  115.5 2.4 %collective-permute-start.10 = (bf16[160,1152]{1,0:T(8,128)(2,1)S(1)}, bf16[160,1152]{1,0:T(8,128)(2,1)S(1)}, u32[]{:S(2)}, u32[]{:S(2)}) collective-permute-start(bf16[160,1152]{1,0:T(8,128)(2,1)S(1)} %get-tuple-element.53), channel_id=1, source_target_pairs={{0,1},{1,0},{2,3},{3,2},{4,5},{5,4},{6,7},{7,6},{8,9},{9,8},{10,11... | collective-permute-start | bytes 1105928 | tf_op jit(solution)/shard_map/cond/branch_0_fun/ppermute | solution.py:370
  115.6 3.3 %collective-permute-start.3 = (bf16[160,1024]{1,0:T(8,128)(2,1)S(1)}, bf16[160,1024]{1,0:T(8,128)(2,1)S(1)}, u32[]{:S(2)}, u32[]{:S(2)}) collective-permute-start(bf16[160,1024]{1,0:T(8,128)(2,1)S(1)} %get-tuple-element.46), channel_id=1, source_target_pairs={{0,1},{1,0},{2,3},{3,2},{4,5},{5,4},{6,7},{7,6},{8,9},{9,8},{10,11... | collective-permute-start | bytes 983048 | tf_op jit(solution)/shard_map/cond/branch_0_fun/ppermute | solution.py:370
  116.1 14.8 %collective-permute-start.9 = (bf16[160,1152]{1,0:T(8,128)(2,1)S(1)}, bf16[160,1152]{1,0:T(8,128)(2,1)S(1)}, u32[]{:S(2)}, u32[]{:S(2)}) collective-permute-start(bf16[160,1152]{1,0:T(8,128)(2,1)S(1)} %get-tuple-element.51), channel_id=1, source_target_pairs={{0,1},{1,0},{2,3},{3,2},{4,5},{5,4},{6,7},{7,6},{8,9},{9,8},{10,11... | collective-permute-start | bytes 1105928 | tf_op jit(solution)/shard_map/cond/branch_0_fun/ppermute | solution.py:370
  116.3 10.6 %collective-permute-start.5 = (bf16[160,1024]{1,0:T(8,128)(2,1)S(1)}, bf16[160,1024]{1,0:T(8,128)(2,1)S(1)}, u32[]{:S(2)}, u32[]{:S(2)}) collective-permute-start(bf16[160,1024]{1,0:T(8,128)(2,1)S(1)} %add_convert_fusion.4), channel_id=1, source_target_pairs={{0,2},{1,3},{2,0},{3,1},{4,6},{5,7},{6,4},{7,5},{8,10},{9,11},{10,... | collective-permute-start | bytes 983048 | tf_op jit(solution)/shard_map/cond/branch_0_fun/ppermute | solution.py:370
  118.0 16.3 %collective-permute-start.11 = (bf16[160,1152]{1,0:T(8,128)(2,1)S(1)}, bf16[160,1152]{1,0:T(8,128)(2,1)S(1)}, u32[]{:S(2)}, u32[]{:S(2)}) collective-permute-start(bf16[160,1152]{1,0:T(8,128)(2,1)S(1)} %add_convert_fusion.1), channel_id=1, source_target_pairs={{0,2},{1,3},{2,0},{3,1},{4,6},{5,7},{6,4},{7,5},{8,10},{9,11},{10,... | collective-permute-start | bytes 1105928 | tf_op jit(solution)/shard_map/cond/branch_0_fun/ppermute | solution.py:370
  126.9 11.5 %copy-start.6 = (bf16[16,64,2048]{2,1,0:T(8,128)(2,1)S(1)}, bf16[16,64,2048]{2,1,0:T(8,128)(2,1)}, u32[]{:S(2)}) copy-start(bf16[16,64,2048]{2,1,0:T(8,128)(2,1)} %get-tuple-element.57.cs_ref) | copy-start | bytes 12582916 | tf_op jit(solution)/shard_map/cond
  127.1 8.3 %collective-permute-start.8 = (bf16[40,1024]{1,0:T(8,128)(2,1)S(1)}, bf16[40,1024]{1,0:T(8,128)(2,1)S(1)}, u32[]{:S(2)}, u32[]{:S(2)}) collective-permute-start(bf16[40,1024]{1,0:T(8,128)(2,1)S(1)} %get-tuple-element.126), channel_id=1, source_target_pairs={{0,4},{4,8},{8,12},{12,0},{1,5},{5,9},{9,13},{13,1},{2,6},{6,10},{... | collective-permute-start | bytes 245768 | tf_op jit(solution)/shard_map/cond/branch_0_fun/ppermute | solution.py:365
  127.1 17.6 %collective-permute-start.7 = (bf16[40,1024]{1,0:T(8,128)(2,1)S(1)}, bf16[40,1024]{1,0:T(8,128)(2,1)S(1)}, u32[]{:S(2)}, u32[]{:S(2)}) collective-permute-start(bf16[40,1024]{1,0:T(8,128)(2,1)S(1)} %get-tuple-element.127), channel_id=1, source_target_pairs={{0,8},{4,12},{8,0},{12,4},{1,9},{5,13},{9,1},{13,5},{2,10},{6,14},... | collective-permute-start | bytes 245768 | tf_op jit(solution)/shard_map/cond/branch_0_fun/ppermute | solution.py:365
  127.9 16.9 %collective-permute-start.6 = (bf16[40,1024]{1,0:T(8,128)(2,1)S(1)}, bf16[40,1024]{1,0:T(8,128)(2,1)S(1)}, u32[]{:S(2)}, u32[]{:S(2)}) collective-permute-start(bf16[40,1024]{1,0:T(8,128)(2,1)S(1)} %get-tuple-element.128), channel_id=1, source_target_pairs={{0,12},{4,0},{8,4},{12,8},{1,13},{5,1},{9,5},{13,9},{2,14},{6,2},{... | collective-permute-start | bytes 245768 | tf_op jit(solution)/shard_map/cond/branch_0_fun/ppermute | solution.py:365
  134.5 10.3 %collective-permute-start.14 = (bf16[40,1152]{1,0:T(8,128)(2,1)S(1)}, bf16[40,1152]{1,0:T(8,128)(2,1)S(1)}, u32[]{:S(2)}, u32[]{:S(2)}) collective-permute-start(bf16[40,1152]{1,0:T(8,128)(2,1)S(1)} %get-tuple-element.122), channel_id=1, source_target_pairs={{0,4},{4,8},{8,12},{12,0},{1,5},{5,9},{9,13},{13,1},{2,6},{6,10},{... | collective-permute-start | bytes 276488 | tf_op jit(solution)/shard_map/cond/branch_0_fun/ppermute | solution.py:365
  134.6 10.2 %collective-permute-start.13 = (bf16[40,1152]{1,0:T(8,128)(2,1)S(1)}, bf16[40,1152]{1,0:T(8,128)(2,1)S(1)}, u32[]{:S(2)}, u32[]{:S(2)}) collective-permute-start(bf16[40,1152]{1,0:T(8,128)(2,1)S(1)} %get-tuple-element.123), channel_id=1, source_target_pairs={{0,8},{4,12},{8,0},{12,4},{1,9},{5,13},{9,1},{13,5},{2,10},{6,14},... | collective-permute-start | bytes 276488 | tf_op jit(solution)/shard_map/cond/branch_0_fun/ppermute | solution.py:365
  135.3 9.4 %collective-permute-start.12 = (bf16[40,1152]{1,0:T(8,128)(2,1)S(1)}, bf16[40,1152]{1,0:T(8,128)(2,1)S(1)}, u32[]{:S(2)}, u32[]{:S(2)}) collective-permute-start(bf16[40,1152]{1,0:T(8,128)(2,1)S(1)} %get-tuple-element.124), channel_id=1, source_target_pairs={{0,12},{4,0},{8,4},{12,8},{1,13},{5,1},{9,5},{13,9},{2,14},{6,2},{... | collective-permute-start | bytes 276488 | tf_op jit(solution)/shard_map/cond/branch_0_fun/ppermute | solution.py:365
  146.1 0.5 copy-start.11
  146.1 0.8 copy-start.12

commit v3 on v2

--- a/solution.py
+++ b/solution.py
@@ -47,29 +47,34 @@
     return pl.BlockSpec(array.shape, lambda *_: zeros)
 
 
-def route_columns(ids, per_device):
-    count = ids.shape[0]
-    across = jnp.broadcast_to(ids.astype(F32), (count, count))
-    down = jnp.transpose(across)
+def route_columns(ids, per_device, n_shards):
+    count = ids.shape[1]
+    here = lax.axis_index("expert") if direct(n_shards) else 0
+    total = n_shards * per_device
+    ids = ids - here * per_device
+    ids = jnp.where(ids < 0, ids + total, ids)
+    down = jnp.broadcast_to(ids.astype(F32), (count, count))
+    across = jnp.transpose(down)
     row = lax.broadcasted_iota(jnp.int32, (count, count), 0)
     col = lax.broadcasted_iota(jnp.int32, (count, count), 1)
     earlier = col < row
     inv = 1.0 / per_device
+    across_shard = jnp.floor((across + 0.5) * inv)
     same_expert = jnp.where((across == down) & earlier, 1.0, 0.0)
     same_shard = jnp.where(
-        (jnp.floor((across + 0.5) * inv) == jnp.floor((down + 0.5) * inv)) & earlier, 1.0, 0.0
+        (across_shard == jnp.floor((down + 0.5) * inv)) & earlier, 1.0, 0.0
     )
     rank = jnp.sum(same_expert, axis=1, keepdims=True)
     place = jnp.sum(same_shard, axis=1, keepdims=True)
-    shard = jnp.floor((ids.astype(F32) + 0.5) * inv)
-    local = ids.astype(F32) - shard * per_device
+    shard = across_shard[:, 0:1]
+    local = across[:, 0:1] - shard * per_device
     return shard, local, rank, place
 
 
 def slot_table(ids, per_device, room, n_shards):
-    shard, local, rank, place = route_columns(ids, per_device)
+    shard, local, rank, place = route_columns(ids, per_device, n_shards)
     slot = jnp.where(place < room, shard * room + place, -1.0).astype(jnp.int32)
-    lanes = lax.broadcasted_iota(jnp.int32, (ids.shape[0], n_shards * room), 1)
+    lanes = lax.broadcasted_iota(jnp.int32, (ids.shape[1], n_shards * room), 1)
     over = jnp.max(place, axis=0, keepdims=True) >= room
     return jnp.where(lanes == slot, 1.0, 0.0).astype(BF), local * MOST + rank + 1.0, over
 
@@ -79,7 +84,9 @@
     width = tok_ref.shape[1]
     x_ref[:, :width] = dot_tn(table, tok_ref[...]).astype(BF)
     lane = lax.broadcasted_iota(jnp.int32, (tag.shape[0], META), 1)
-    info = jnp.where(lane == 0, tag, jnp.where(lane == 1, wgt_ref[...].astype(F32), 0.0))
+    count = tok_ref.shape[0]
+    wgt = jnp.transpose(jnp.broadcast_to(wgt_ref[...].astype(F32), (count, count)))[:, 0:1]
+    info = jnp.where(lane == 0, tag, jnp.where(lane == 1, wgt, 0.0))
     packed = dot_tn(table, info.astype(BF))
     lane = lax.broadcasted_iota(jnp.int32, packed.shape, 1)
     flag = jnp.broadcast_to(jnp.where(over, 1.0, 0.0), packed.shape)
@@ -334,13 +341,14 @@
             term = dot_nn(table[:, k * size : (k + 1) * size], blocks[h * n_blocks + k][...])
             total = term if total is None else total + term
         tok_ref[:, h * part : (h + 1) * part] = total[:, :part].astype(BF)
-        if h == n_half - 1:
-            route_ref[...] = total[:, part : part + META].astype(BF)
+        if h == 0:
+            column = jnp.broadcast_to(total[:, part : part + 1], (total.shape[0],) * 2)
+            route_ref[...] = jnp.transpose(column)[0:1].astype(BF)
 
 
 def home_rows(ids, halves, width, per_device, room, n_shards):
     n_half, n_blocks = len(halves), len(halves[0])
-    count = ids.shape[0]
+    count = ids.shape[1]
     blocks = [b for half in halves for b in half]
     return pl.pallas_call(
         functools.partial(home_kernel, per_device, room, n_shards, n_half, n_blocks),
@@ -348,11 +356,11 @@
         in_specs=[whole(ids)] + [whole(b) for b in blocks],
         out_specs=[
             pl.BlockSpec((count, width), lambda i: (0, 0)),
-            pl.BlockSpec((count, META), lambda i: (0, 0)),
+            pl.BlockSpec((1, count), lambda i: (0, 0)),
         ],
         out_shape=[
             jax.ShapeDtypeStruct((count, width), BF),
-            jax.ShapeDtypeStruct((count, META), BF),
+            jax.ShapeDtypeStruct((1, count), BF),
         ],
         compiler_params=params(),
         cost_estimate=cost(2e8, 2e6),
@@ -370,18 +378,30 @@
     return lax.ppermute(value, axis, [(i, i ^ bit) for i in range(n)])
 
 
+def after(value, other):
+    return lax.optimization_barrier((value, other))[0]
+
+
 def direct(n_shards):
     return n_shards <= 4
 
 
 def to_shards(rows, room, n_shards):
+    return join_shards(shard_parts(rows, room, n_shards))
+
+
+def shard_parts(rows, room, n_shards):
     if not direct(n_shards):
         shaped = rows.reshape(n_shards, room, rows.shape[1])
-        return lax.all_to_all(shaped, "expert", 0, 0, tiled=True).reshape(rows.shape)
+        return [lax.all_to_all(shaped, "expert", 0, 0, tiled=True).reshape(rows.shape)]
     parts = [rows[:room]]
     for k in range(1, n_shards):
         parts.append(shifted(rows[k * room : (k + 1) * room], "expert", k))
-    return jnp.concatenate(parts)
+    return parts
+
+
+def join_shards(parts):
+    return parts[0] if len(parts) == 1 else jnp.concatenate(parts)
 
 
 def from_shards(rows, room, n_shards):
@@ -401,90 +421,99 @@
     return bits
 
 
-def gather_dp(rows, n_dp):
-    got = {0: rows}
-    for bit in reversed(dp_bits(n_dp)):
-        for k in list(got):
-            got[k ^ bit] = swapped(got[k], "dp", bit)
-    return [got[k] for k in range(n_dp)]
-
-
-def scatter_dp(parts, n_dp):
+def far_hop(rows, n_dp):
+    return swapped(rows, "dp", dp_bits(n_dp)[-1])
+
+
+def near_hops(rows, n_dp):
+    got = [rows]
+    for bit in dp_bits(n_dp)[:-1]:
+        got = got + [swapped(r, "dp", bit) for r in got]
+    return got
+
+
+def add_rows(a, b):
+    return (a.astype(F32) + b.astype(F32)).astype(BF)
+
+
+def near_sums(parts, n_dp):
     have = dict(enumerate(parts))
-    bits = dp_bits(n_dp)
-    for bit in bits:
+    for bit in dp_bits(n_dp)[:-1]:
         left = {}
         for k in sorted(have, reverse=True):
             if k & bit == 0:
-                moved = swapped(have[k ^ bit], "dp", bit)
-                left[k] = (have[k].astype(F32) + moved.astype(F32)).astype(BF)
+                left[k] = add_rows(have[k], swapped(have[k ^ bit], "dp", bit))
         have = left
-    return have[0]
-
-
-def begin(room, ids, tokens, out_grad, route_weight, per_device):
-    n_shards = lax.axis_size("expert")
-    send_x, send_c = pack_rows(ids, tokens, out_grad, route_weight, per_device, room, n_shards)
-    own_x = to_shards(send_x, room, n_shards)
-    send_c, own_x = lax.optimization_barrier((send_c, own_x))
-    return own_x, to_shards(send_c, room, n_shards)
-
-
-def finish(room, ids, x_list, own_c, gate, up, down):
+    return have[0], have[dp_bits(n_dp)[-1]]
+
+
+def finish(room, ids, near_x, far_x, own_c, gate, up, down):
     n_shards, n_dp = lax.axis_size("expert"), lax.axis_size("dp")
     per_device, width = gate.shape[0], down.shape[2]
-    c_list = gather_dp(own_c, n_dp)
+    far_c = far_hop(own_c, n_dp)
+    x_list = near_x + near_hops(far_x, n_dp)
     g, u = first_layer(x_list, gate, up, room, n_shards)
+    c_list = near_hops(own_c, n_dp) + near_hops(after(far_c, g), n_dp)
     dg, du, hw, cs, router = second_layer(x_list, c_list, g, u, down, room, n_shards)
-    n_half = 2
-    halves = []
-    for half in range(n_half):
-        column = router if half == n_half - 1 else None
-        parts = third_layer(
-            x_list, dg, du, gate, up, column, half, n_half, room, n_shards
-        )
-        halves.append(from_shards(scatter_dp(parts, n_dp), room, n_shards))
-    down_grad = down_layer(hw, cs)
-    token_grad, route = home_rows(ids, halves, width, per_device, room, n_shards)
-    return token_grad, route[:, :1], down_grad
-
-
-def agreed(own_x, width, n_dp):
-    flag = jnp.max(own_x[:, width + OVER : width + OVER + 1].astype(F32))
-    flag = jnp.broadcast_to(flag, (8, 128))
+    first = third_layer(x_list, dg, du, gate, up, router, 0, 2, room, n_shards)
+    stay_1, go_1 = near_sums(first, n_dp)
+    come_1 = far_hop(go_1, n_dp)
+    dg, du = lax.optimization_barrier((dg, du, go_1))[:2]
+    second = third_layer(x_list, dg, du, gate, up, None, 1, 2, room, n_shards)
+    second = after(second, come_1)
+    stay_2, go_2 = near_sums(second, n_dp)
+    come_2 = far_hop(go_2, n_dp)
+    down_grad = down_layer(after(hw, go_2), cs)
+    home_1 = from_shards(add_rows(stay_1, come_1), room, n_shards)
+    come_2 = after(come_2, (down_grad, home_1))
+    home_2 = from_shards(add_rows(stay_2, come_2), room, n_shards)
+    token_grad, route = home_rows(ids, [home_1, home_2], width, per_device, room, n_shards)
+    return token_grad, route.reshape(-1, 1), down_grad
+
+
+def exchange(room, ids, tokens, out_grad, route_weight, per_device, n_shards, n_dp):
+    send_x, send_c = pack_rows(ids, tokens, out_grad, route_weight, per_device, room, n_shards)
+    own_x = join_shards(shard_parts(send_x, room, n_shards))
+    send_c, own_x = lax.optimization_barrier((send_c, own_x))
+    far_x, near_x = far_hop(own_x, n_dp), near_hops(own_x, n_dp)
+    return near_x, far_x, shard_parts(send_c, room, n_shards)
+
+
+def agreed(flag, n_dp):
     for step in range(1, lax.axis_size("groups")):
         flag = jnp.maximum(flag, shifted(flag, "groups", step))
     for bit in dp_bits(n_dp):
         flag = jnp.maximum(flag, swapped(flag, "dp", bit))
-    return flag[0, 0]
+    return flag
 
 
 def shards(tokens, out_grad, route_weight, expert_ids, gate, up, down):
     n_shards, n_dp = lax.axis_size("expert"), lax.axis_size("dp")
     per_device, width = gate.shape[0], tokens.shape[1]
     most_rows = min(expert_ids.shape[0], per_device * MOST)
-    ids = expert_ids
-    if direct(n_shards):
-        total = n_shards * per_device
-        ids = (ids - lax.axis_index("expert") * per_device + total) % total
+    ids, route_weight = expert_ids.reshape(1, -1), route_weight.reshape(1, -1)
     gate, up = jnp.swapaxes(gate, 1, 2), jnp.swapaxes(up, 1, 2)
     usual = most_rows * 5 // 8
     adaptive = direct(n_shards) and usual % 8 == 0 and (n_shards * usual) % 16 == 0
     room = usual if adaptive else most_rows
-    own_x, own_c = begin(room, ids, tokens, out_grad, route_weight, per_device)
-    x_list = gather_dp(own_x, n_dp)
+    args = (ids, tokens, out_grad, route_weight, per_device, n_shards, n_dp)
+    near_x, far_x, parts_c = exchange(room, *args)
     if not adaptive:
-        return finish(room, ids, x_list, own_c, gate, up, down)
-    over = agreed(own_x, width, n_dp)
+        return finish(room, ids, near_x, far_x, join_shards(parts_c), gate, up, down)
+    meta = near_x[0][:, width : width + META].astype(F32)
+    over = jnp.max(meta, axis=0, keepdims=True)
+    over = agreed(after(jnp.broadcast_to(over, (8, META)), near_x[-1]), n_dp)
+    own_c = join_shards(parts_c)
+    far_x, own_c, over = lax.optimization_barrier((far_x, own_c, over))
 
     def fits(_):
-        return finish(room, ids, x_list, own_c, gate, up, down)
+        return finish(room, ids, near_x, far_x, own_c, gate, up, down)
 
     def full(_):
-        full_x, full_c = begin(most_rows, ids, tokens, out_grad, route_weight, per_device)
-        return finish(most_rows, ids, gather_dp(full_x, n_dp), full_c, gate, up, down)
-
-    return lax.cond(over > 0.0, full, fits, 0)
+        full_near, full_far, full_c = exchange(most_rows, *args)
+        return finish(most_rows, ids, full_near, full_far, join_shards(full_c), gate, up, down)
+
+    return lax.cond(over[0, OVER] > 0.0, full, fits, 0)
 
 
 def solution(mesh):

time: 147 us -> 119 us (0.81)
  waiting for transfers between devices: 63.4 us -> 39 us
  local copies, waits for them, and re-layouts: 3.24 us -> 1.74 us
    ppermute x14, waiting for transfers between devices: 36 us -> 10.6 us  [swapped(): return lax.ppermute(value, axis, [(i, i ^ bit) for i in range(n)])]
    ppermute x14, starting transfers between devices: 7.99 us -> 4.91 us  [swapped(): return lax.ppermute(value, axis, [(i, i ^ bit) for i in range(n)])]
    ppermute x13, starting transfers between devices: 19.9 us -> 21.7 us  [shifted(): return lax.ppermute(value, axis, [(i, (i + step) % n) for i in range(n)])]
    unnamed x7 -> x8, local copies, waits for them, and re-layouts: 1.58 us -> 0.03 us
  transfers between devices with their start and end apart: 27 -> 27, of which waited for: 10 -> 13; matrix products, arithmetic and copies ran while one was open for 2% -> 0% of each run, Pallas kernels for 19% -> 23%
where the time goes in v3:
time: 119 us
  Pallas kernels  49.2 us (41%)
  waiting for transfers between devices  39 us (33%)
  starting transfers between devices  26.6 us (22%)
  local copies, waits for them, and re-layouts  1.74 us (1%)
  between operations  1.43 us (1%)
    ppermute x13, waiting for transfers between devices, shifted(): return lax.ppermute(value, axis, [(i, (i + step) % n) for i in range(n)])  28.4 us
    ppermute x13, starting transfers between devices, shifted(): return lax.ppermute(value, axis, [(i, (i + step) % n) for i in range(n)])  21.7 us
    pallas_call x2, Pallas kernels, third_layer(): pl.pallas_call(functools.partial(third_kernel, n_dp, room, n_shards, rout...  14.8 us
    pallas_call x1, Pallas kernels, first_layer(): pl.pallas_call(functools.partial(first_kernel, n_dp, room, n_shards), gri...  13.6 us
    ppermute x14, waiting for transfers between devices, swapped(): return lax.ppermute(value, axis, [(i, i ^ bit) for i in range(n)])  10.6 us
    pallas_call x1, Pallas kernels, second_layer(): pl.pallas_call(functools.partial(second_kernel, n_dp, room, n_shards), gr...  10.5 us
    pallas_call x1, Pallas kernels, down_layer(): pl.pallas_call(down_kernel, grid=(experts // step,), in_specs=[pl.BlockSp...  6.38 us
    ppermute x14, starting transfers between devices, swapped(): return lax.ppermute(value, axis, [(i, i ^ bit) for i in range(n)])  4.91 us
  transfers between devices with their start and end apart: 27, of which 13 were waited for; matrix products, arithmetic and copies ran while one was open for 0% of the time, Pallas kernels for 23%

profile of v3, /device:TPU:0, one launch (start us, length us, event | category | flops | bytes accessed | tf_op | source)
XLA Modules:
  0.0 118.7 jit_solution(13731056548691089757)
XLA Ops:
  0.6 2.0 %pack_rows.3 = (bf16[160,2176]{1,0:T(8,128)(2,1)S(1)}, bf16[160,2048]{1,0:T(8,128)(2,1)S(1)}) custom-call(s32[1,128]{1,0:T(1,128)} %bitcast.11, bf16[128,2048]{1,0:T(8,128)(2,1)} %tok_ref.1, bf16[128,2048]{1,0:T(8,128)(2,1)} %cot_ref.1, bf16[1,128]{1,0:T(2,128)(2,1)} %bitcast.14), custom_call_target="tpu_custom_call" | custom-call | flops 400000000 | bytes 4000000 | tf_op jit(solution)/shard_map/pack_rows/pallas_call | solution.py:100
  2.7 5.1 %collective-permute-start.42 = (bf16[40,2176]{1,0:T(8,128)(2,1)S(1)}, bf16[40,2176]{1,0:T(8,128)(2,1)S(1)}, u32[]{:S(2)}, u32[]{:S(2)}) collective-permute-start(bf16[40,2176]{1,0:T(8,128)(2,1)S(1)} %get-tuple-element.147), channel_id=1, source_target_pairs={{0,12},{4,0},{8,4},{12,8},{1,13},{5,1},{9,5},{13,9},{2,14},{6,2},{... | collective-permute-start | bytes 522248 | tf_op jit(solution)/shard_map/ppermute | solution.py:373
  7.8 1.0 collective-permute-start.40
  8.8 3.9 %collective-permute-done.42 = bf16[40,2176]{1,0:T(8,128)(2,1)S(1)} collective-permute-done((bf16[40,2176]{1,0:T(8,128)(2,1)S(1)}, bf16[40,2176]{1,0:T(8,128)(2,1)S(1)}, u32[]{:S(2)}, u32[]{:S(2)}) %collective-permute-start.42) | collective-permute-done | bytes 174112 | tf_op jit(solution)/shard_map/ppermute | solution.py:373
  12.7 9.9 %collective-permute-done.41 = bf16[40,2176]{1,0:T(8,128)(2,1)S(1)} collective-permute-done((bf16[40,2176]{1,0:T(8,128)(2,1)S(1)}, bf16[40,2176]{1,0:T(8,128)(2,1)S(1)}, u32[]{:S(2)}, u32[]{:S(2)}) %collective-permute-start.41) | collective-permute-done | bytes 174112 | tf_op jit(solution)/shard_map/ppermute | solution.py:373
  22.7 0.1 collective-permute-start.47
  22.8 1.6 %collective-permute-start.43 = (bf16[160,2176]{1,0:T(8,128)(2,1)S(1)}, bf16[160,2176]{1,0:T(8,128)(2,1)S(1)}, u32[]{:S(2)}, u32[]{:S(2)}) collective-permute-start(bf16[160,2176]{1,0:T(8,128)(2,1)S(1)} %pad_maximum_fusion.2), channel_id=1, source_target_pairs={{0,2},{1,3},{2,0},{3,1},{4,6},{5,7},{6,4},{7,5},{8,10},{9,11},{10,... | collective-permute-start | bytes 2088968 | tf_op jit(solution)/shard_map/ppermute | solution.py:378
  24.4 0.9 collective-permute-start.46
  25.3 2.0 %collective-permute-start.45 = (bf16[40,2048]{1,0:T(8,128)(2,1)S(1)}, bf16[40,2048]{1,0:T(8,128)(2,1)S(1)}, u32[]{:S(2)}, u32[]{:S(2)}) collective-permute-start(bf16[40,2048]{1,0:T(8,128)(2,1)S(1)} %get-tuple-element.152), channel_id=1, source_target_pairs={{0,8},{4,12},{8,0},{12,4},{1,9},{5,13},{9,1},{13,5},{2,10},{6,14},... | collective-permute-start | bytes 491528 | tf_op jit(solution)/shard_map/ppermute | solution.py:373
  27.3 1.9 %collective-permute-start.44 = (bf16[40,2048]{1,0:T(8,128)(2,1)S(1)}, bf16[40,2048]{1,0:T(8,128)(2,1)S(1)}, u32[]{:S(2)}, u32[]{:S(2)}) collective-permute-start(bf16[40,2048]{1,0:T(8,128)(2,1)S(1)} %get-tuple-element.153), channel_id=1, source_target_pairs={{0,4},{4,8},{8,12},{12,0},{1,5},{5,9},{9,13},{13,1},{2,6},{6,10},{... | collective-permute-start | bytes 491528 | tf_op jit(solution)/shard_map/ppermute | solution.py:373
  29.3 1.6 %collective-permute-start.48 = (f32[8,128]{1,0:T(8,128)S(1)}, f32[8,128]{1,0:T(8,128)S(1)}, u32[]{:S(2)}, u32[]{:S(2)}) collective-permute-start(f32[8,128]{1,0:T(8,128)S(1)} %broadcast_in_dim.2), channel_id=1, source_target_pairs={{0,16},{16,0},{1,17},{17,1},{2,18},{18,2},{3,19},{19,3},{4,20},{20... | collective-permute-start | bytes 12296 | tf_op jit(solution)/shard_map/ppermute | solution.py:373
  30.9 2.1 %collective-permute-done.48 = f32[8,128]{1,0:T(8,128)S(1)} collective-permute-done((f32[8,128]{1,0:T(8,128)S(1)}, f32[8,128]{1,0:T(8,128)S(1)}, u32[]{:S(2)}, u32[]{:S(2)}) %collective-permute-start.48) | collective-permute-done | bytes 4128 | tf_op jit(solution)/shard_map/ppermute | solution.py:373
  33.0 1.2 collective-permute-done.49
  34.2 0.5 collective-permute-start.50
  34.7 7.6 %collective-permute-done.45 = bf16[40,2048]{1,0:T(8,128)(2,1)S(1)} collective-permute-done((bf16[40,2048]{1,0:T(8,128)(2,1)S(1)}, bf16[40,2048]{1,0:T(8,128)(2,1)S(1)}, u32[]{:S(2)}, u32[]{:S(2)}) %collective-permute-start.45) | collective-permute-done | bytes 163872 | tf_op jit(solution)/shard_map/ppermute | solution.py:373
  42.4 0.6 slice.111
  43.7 75.0 %conditional.1 = (bf16[128,2048]{1,0:T(8,128)(2,1)}, bf16[128,1]{0,1:T(2,128)(2,1)}, bf16[16,192,2048]{2,1,0:T(8,128)(2,1)}) conditional(s32[]{:T(128)} %bitcast.4, (bf16[160,2176]{1,0:T(8,128)(2,1)S(1)}, bf16[160,2048]{1,0:T(8,128)(2,1)S(1)}, bf16[160,2176]{1,0:T(8,128)(2,1)S(1)}, bf16[160,2176]{1,0:T(8,128)(2,1)S(1)}, ...), branch_computations={%region_1.0_spmd, %region_2.0_spmd} | conditional | flops 7615335424 | bytes 221638272 | solution.py:516
  43.8 0.6 collective-permute-start.2
  44.4 0.2 collective-permute-start.1
  44.5 1.4 %collective-permute-done.refs_3_ = bf16[160,2176]{1,0:T(8,128)(2,1)S(1)} collective-permute-done((bf16[160,2176]{1,0:T(8,128)(2,1)S(1)}, bf16[160,2176]{1,0:T(8,128)(2,1)S(1)}, u32[]{:S(2)}, u32[]{:S(2)}) %collective-permute-start) | collective-permute-done | bytes 696352 | tf_op jit(solution)/shard_map/cond/branch_0_fun/ppermute | solution.py:378
  45.9 13.6 %gate_up.2 = (f32[16,64,192]{2,1,0:T(8,128)S(1)}, f32[16,64,192]{2,1,0:T(8,128)S(1)}) custom-call(bf16[160,2176]{1,0:T(8,128)(2,1)S(1)} %get-tuple-element.31.refs_0_, bf16[160,2176]{1,0:T(8,128)(2,1)S(1)} %get-tuple-element.32.refs_1_, bf16[160,2176]{1,0:T(8,128)(2,1)S(1)} %get-tuple-element.33.refs_2_, bf16[160,2176]{1,0:T(8,128)(2,1)S(1)} %collective-permute-done.refs_3_, ...), custom_call_target="tpu_custom_call" | custom-call | flops 2000000000 | bytes 30000000 | tf_op jit(solution)/shard_map/cond/branch_0_fun/gate_up/pallas_call | solution.py:168
  59.6 1.0 copy-done.9
  60.5 0.4 collective-permute-done.2.refs_6_
  60.9 2.1 %collective-permute-done.3.refs_7_ = bf16[160,2048]{1,0:T(8,128)(2,1)S(1)} collective-permute-done((bf16[160,2048]{1,0:T(8,128)(2,1)S(1)}, bf16[160,2048]{1,0:T(8,128)(2,1)S(1)}, u32[]{:S(2)}, u32[]{:S(2)}) %collective-permute-start.3) | collective-permute-done | bytes 655392 | tf_op jit(solution)/shard_map/cond/branch_0_fun/ppermute | solution.py:378
  63.0 10.5 %hidden_grads.2 = (bf16[16,64,192]{2,1,0:T(8,128)(2,1)S(1)}, bf16[16,64,192]{2,1,0:T(8,128)(2,1)S(1)}, bf16[16,64,192]{2,1,0:T(8,128)(2,1)S(1)}, bf16[16,64,2048]{2,1,0:T(8,128)(2,1)}, bf16[16,64,128]{2,1,0:T(8,128)(2,1)S(1)}) custom-call(bf16[160,2176]{1,0:T(8,128)(2,1)S(1)} %get-tuple-element.31.refs_0_, bf16[160,2176]{1,0:T(8,128)(2,1)S(1)} %get-tuple-element.32.refs_1_, ...), custom_call_target="tpu_custom_call" | custom-call | flops 2000000000 | bytes 20000000 | tf_op jit(solution)/shard_map/cond/branch_0_fun/hidden_grads/pallas_call | solution.py:224
  73.5 7.3 %input_grads.4 = (bf16[160,1152]{1,0:T(8,128)(2,1)S(1)}, bf16[160,1152]{1,0:T(8,128)(2,1)S(1)}, bf16[160,1152]{1,0:T(8,128)(2,1)S(1)}, bf16[160,1152]{1,0:T(8,128)(2,1)S(1)}) custom-call(bf16[160,2176]{1,0:T(8,128)(2,1)S(1)} %get-tuple-element.31.refs_0_, bf16[160,2176]{1,0:T(8,128)(2,1)S(1)} %get-tuple-element.32.refs_1_, ...), custom_call_target="tpu_custom_call" | custom-call | flops 1000000000 | bytes 15000000 | tf_op jit(solution)/shard_map/cond/branch_0_fun/input_grads/pallas_call | solution.py:295
  80.8 0.2 collective-permute-start.5
  81.0 1.6 %collective-permute-done.5 = bf16[160,1152]{1,0:T(8,128)(2,1)S(1)} collective-permute-done((bf16[160,1152]{1,0:T(8,128)(2,1)S(1)}, bf16[160,1152]{1,0:T(8,128)(2,1)S(1)}, u32[]{:S(2)}, u32[]{:S(2)}) %collective-permute-start.5) | collective-permute-done | bytes 368672 | tf_op jit(solution)/shard_map/cond/branch_0_fun/ppermute | solution.py:378
  82.6 0.1 add_convert_fusion.1
  82.7 0.6 collective-permute-start.6
  83.3 7.5 %input_grads.5 = (bf16[160,1024]{1,0:T(8,128)(2,1)S(1)}, bf16[160,1024]{1,0:T(8,128)(2,1)S(1)}, bf16[160,1024]{1,0:T(8,128)(2,1)S(1)}, bf16[160,1024]{1,0:T(8,128)(2,1)S(1)}) custom-call(bf16[160,2176]{1,0:T(8,128)(2,1)S(1)} %get-tuple-element.31.refs_0_, bf16[160,2176]{1,0:T(8,128)(2,1)S(1)} %get-tuple-element.32.refs_1_, ...), custom_call_target="tpu_custom_call" | custom-call | flops 1000000000 | bytes 15000000 | tf_op jit(solution)/shard_map/cond/branch_0_fun/input_grads/pallas_call | solution.py:295
  90.8 2.5 %collective-permute-done.6 = bf16[160,1152]{1,0:T(8,128)(2,1)S(1)} collective-permute-done((bf16[160,1152]{1,0:T(8,128)(2,1)S(1)}, bf16[160,1152]{1,0:T(8,128)(2,1)S(1)}, u32[]{:S(2)}, u32[]{:S(2)}) %collective-permute-start.6) | collective-permute-done | bytes 368672 | tf_op jit(solution)/shard_map/cond/branch_0_fun/ppermute | solution.py:378
  93.4 0.5 collective-permute-start.11
  93.9 0.1 add_convert_fusion
  94.0 1.4 %collective-permute-done.11 = bf16[160,1024]{1,0:T(8,128)(2,1)S(1)} collective-permute-done((bf16[160,1024]{1,0:T(8,128)(2,1)S(1)}, bf16[160,1024]{1,0:T(8,128)(2,1)S(1)}, u32[]{:S(2)}, u32[]{:S(2)}) %collective-permute-start.11) | collective-permute-done | bytes 327712 | tf_op jit(solution)/shard_map/cond/branch_0_fun/ppermute | solution.py:378
  95.5 0.1 add_convert_fusion.4
  95.6 0.6 collective-permute-start.12
  96.2 0.4 collective-permute-start.9
  96.6 2.0 %collective-permute-start.8 = (bf16[40,1152]{1,0:T(8,128)(2,1)S(1)}, bf16[40,1152]{1,0:T(8,128)(2,1)S(1)}, u32[]{:S(2)}, u32[]{:S(2)}) collective-permute-start(bf16[40,1152]{1,0:T(8,128)(2,1)S(1)} %get-tuple-element.123), channel_id=1, source_target_pairs={{0,8},{4,12},{8,0},{12,4},{1,9},{5,13},{9,1},{13,5},{2,10},{6,14},... | collective-permute-start | bytes 276488 | tf_op jit(solution)/shard_map/cond/branch_0_fun/ppermute | solution.py:373
  98.6 2.8 %collective-permute-start.7 = (bf16[40,1152]{1,0:T(8,128)(2,1)S(1)}, bf16[40,1152]{1,0:T(8,128)(2,1)S(1)}, u32[]{:S(2)}, u32[]{:S(2)}) collective-permute-start(bf16[40,1152]{1,0:T(8,128)(2,1)S(1)} %get-tuple-element.124), channel_id=1, source_target_pairs={{0,12},{4,0},{8,4},{12,8},{1,13},{5,1},{9,5},{13,9},{2,14},{6,2},{... | collective-permute-start | bytes 276488 | tf_op jit(solution)/shard_map/cond/branch_0_fun/ppermute | solution.py:373
  101.4 6.4 %down_grads.2 = bf16[16,192,2048]{2,1,0:T(8,128)(2,1)} custom-call(bf16[16,64,192]{2,1,0:T(8,128)(2,1)S(1)} %get-tuple-element.59.hw_ref, bf16[16,64,2048]{2,1,0:T(8,128)(2,1)S(1)} %copy-done.6), custom_call_target="tpu_custom_call" | custom-call | flops 1000000000 | bytes 18000000 | tf_op jit(solution)/shard_map/cond/branch_0_fun/down_grads/pallas_call | solution.py:318
  107.9 0.2 add_convert_fusion.3
  108.1 0.3 collective-permute-start.15
  108.4 2.2 %collective-permute-start.14 = (bf16[40,1024]{1,0:T(8,128)(2,1)S(1)}, bf16[40,1024]{1,0:T(8,128)(2,1)S(1)}, u32[]{:S(2)}, u32[]{:S(2)}) collective-permute-start(bf16[40,1024]{1,0:T(8,128)(2,1)S(1)} %get-tuple-element.127), channel_id=1, source_target_pairs={{0,8},{4,12},{8,0},{12,4},{1,9},{5,13},{9,1},{13,5},{2,10},{6,14},... | collective-permute-start | bytes 245768 | tf_op jit(solution)/shard_map/cond/branch_0_fun/ppermute | solution.py:373
  110.6 1.3 %collective-permute-start.13 = (bf16[40,1024]{1,0:T(8,128)(2,1)S(1)}, bf16[40,1024]{1,0:T(8,128)(2,1)S(1)}, u32[]{:S(2)}, u32[]{:S(2)}) collective-permute-start(bf16[40,1024]{1,0:T(8,128)(2,1)S(1)} %get-tuple-element.128), channel_id=1, source_target_pairs={{0,12},{4,0},{8,4},{12,8},{1,13},{5,1},{9,5},{13,9},{2,14},{6,2},{... | collective-permute-start | bytes 245768 | tf_op jit(solution)/shard_map/cond/branch_0_fun/ppermute | solution.py:373
  111.9 3.1 %collective-permute-done.15.refs_7_ = bf16[40,1024]{1,0:T(8,128)(2,1)S(1)} collective-permute-done((bf16[40,1024]{1,0:T(8,128)(2,1)S(1)}, bf16[40,1024]{1,0:T(8,128)(2,1)S(1)}, u32[]{:S(2)}, u32[]{:S(2)}) %collective-permute-start.15) | collective-permute-done | bytes 81952 | tf_op jit(solution)/shard_map/cond/branch_0_fun/ppermute | solution.py:373
  115.1 1.8 %collective-permute-done.14.refs_6_ = bf16[40,1024]{1,0:T(8,128)(2,1)S(1)} collective-permute-done((bf16[40,1024]{1,0:T(8,128)(2,1)S(1)}, bf16[40,1024]{1,0:T(8,128)(2,1)S(1)}, u32[]{:S(2)}, u32[]{:S(2)}) %collective-permute-start.14) | collective-permute-done | bytes 81952 | tf_op jit(solution)/shard_map/cond/branch_0_fun/ppermute | solution.py:373
  116.9 1.8 %home_rows.2 = (bf16[128,2048]{1,0:T(8,128)(2,1)}, bf16[1,128]{1,0:T(2,128)(2,1)}) custom-call(s32[1,128]{1,0:T(1,128)S(1)} %get-tuple-element.30.ids_ref, bf16[40,1152]{1,0:T(8,128)(2,1)S(1)} %get-tuple-element.125.refs_0_, bf16[40,1152]{1,0:T(8,128)(2,1)S(1)} %collective-permute-done.7.refs_1_, bf16[40,1152]{1,0:T(8,128)(2,1)S(1)} %collective-permute-done.8.refs_2_, ...), custom_call_target="tpu_custom_call" | custom-call | flops 200000000 | bytes 2000000 | tf_op jit(solution)/shard_map/cond/branch_0_fun/home_rows/pallas_call | solution.py:353
  (42 shorter events, 0.5 us)
Async XLA Ops:
  2.7 10.0 %collective-permute-start.42 = (bf16[40,2176]{1,0:T(8,128)(2,1)S(1)}, bf16[40,2176]{1,0:T(8,128)(2,1)S(1)}, u32[]{:S(2)}, u32[]{:S(2)}) collective-permute-start(bf16[40,2176]{1,0:T(8,128)(2,1)S(1)} %get-tuple-element.147), channel_id=1, source_target_pairs={{0,12},{4,0},{8,4},{12,8},{1,13},{5,1},{9,5},{13,9},{2,14},{6,2},{... | collective-permute-start | bytes 522248 | tf_op jit(solution)/shard_map/ppermute | solution.py:373
  7.8 14.8 %collective-permute-start.41 = (bf16[40,2176]{1,0:T(8,128)(2,1)S(1)}, bf16[40,2176]{1,0:T(8,128)(2,1)S(1)}, u32[]{:S(2)}, u32[]{:S(2)}) collective-permute-start(bf16[40,2176]{1,0:T(8,128)(2,1)S(1)} %get-tuple-element.148), channel_id=1, source_target_pairs={{0,8},{4,12},{8,0},{12,4},{1,9},{5,13},{9,1},{13,5},{2,10},{6,14},... | collective-permute-start | bytes 522248 | tf_op jit(solution)/shard_map/ppermute | solution.py:373
  7.8 14.8 %collective-permute-start.40 = (bf16[40,2176]{1,0:T(8,128)(2,1)S(1)}, bf16[40,2176]{1,0:T(8,128)(2,1)S(1)}, u32[]{:S(2)}, u32[]{:S(2)}) collective-permute-start(bf16[40,2176]{1,0:T(8,128)(2,1)S(1)} %get-tuple-element.149), channel_id=1, source_target_pairs={{0,4},{4,8},{8,12},{12,0},{1,5},{5,9},{9,13},{13,1},{2,6},{6,10},{... | collective-permute-start | bytes 522248 | tf_op jit(solution)/shard_map/ppermute | solution.py:373
  22.6 21.0 %copy-start.11 = (s32[128,1]{0,1:T(1,128)S(1)}, s32[128,1]{0,1:T(1,128)}, u32[]{:S(2)}) copy-start(s32[128,1]{0,1:T(1,128)} %param.12) | copy-start | bytes 1540
  22.7 21.0 %copy-start.12 = (bf16[128,2048]{1,0:T(8,128)(2,1)S(1)}, bf16[128,2048]{1,0:T(8,128)(2,1)}, u32[]{:S(2)}) copy-start(bf16[128,2048]{1,0:T(8,128)(2,1)} %tok_ref.1) | copy-start | bytes 1572868
  22.7 21.0 %copy-start.13 = (bf16[128,2048]{1,0:T(8,128)(2,1)S(1)}, bf16[128,2048]{1,0:T(8,128)(2,1)}, u32[]{:S(2)}) copy-start(bf16[128,2048]{1,0:T(8,128)(2,1)} %cot_ref.1) | copy-start | bytes 1572868
  22.7 21.0 %copy-start.14 = (bf16[128,1]{0,1:T(2,128)(2,1)S(1)}, bf16[128,1]{0,1:T(2,128)(2,1)}, u32[]{:S(2)}) copy-start(bf16[128,1]{0,1:T(2,128)(2,1)} %param.11) | copy-start | bytes 772
  22.7 6.6 %collective-permute-start.47 = (bf16[160,2176]{1,0:T(8,128)(2,1)S(1)}, bf16[160,2176]{1,0:T(8,128)(2,1)S(1)}, u32[]{:S(2)}, u32[]{:S(2)}) collective-permute-start(bf16[160,2176]{1,0:T(8,128)(2,1)S(1)} %pad_maximum_fusion.2), channel_id=1, source_target_pairs={{0,1},{1,0},{2,3},{3,2},{4,5},{5,4},{6,7},{7,6},{8,9},{9,8},{10,11... | collective-permute-start | bytes 2088968 | tf_op jit(solution)/shard_map/ppermute | solution.py:378
  22.8 19.6 %collective-permute-start.43 = (bf16[160,2176]{1,0:T(8,128)(2,1)S(1)}, bf16[160,2176]{1,0:T(8,128)(2,1)S(1)}, u32[]{:S(2)}, u32[]{:S(2)}) collective-permute-start(bf16[160,2176]{1,0:T(8,128)(2,1)S(1)} %pad_maximum_fusion.2), channel_id=1, source_target_pairs={{0,2},{1,3},{2,0},{3,1},{4,6},{5,7},{6,4},{7,5},{8,10},{9,11},{10,... | collective-permute-start | bytes 2088968 | tf_op jit(solution)/shard_map/ppermute | solution.py:378
  24.4 10.3 %collective-permute-start.46 = (bf16[40,2048]{1,0:T(8,128)(2,1)S(1)}, bf16[40,2048]{1,0:T(8,128)(2,1)S(1)}, u32[]{:S(2)}, u32[]{:S(2)}) collective-permute-start(bf16[40,2048]{1,0:T(8,128)(2,1)S(1)} %get-tuple-element.151), channel_id=1, source_target_pairs={{0,12},{4,0},{8,4},{12,8},{1,13},{5,1},{9,5},{13,9},{2,14},{6,2},{... | collective-permute-start | bytes 491528 | tf_op jit(solution)/shard_map/ppermute | solution.py:373
  25.3 17.0 %collective-permute-start.45 = (bf16[40,2048]{1,0:T(8,128)(2,1)S(1)}, bf16[40,2048]{1,0:T(8,128)(2,1)S(1)}, u32[]{:S(2)}, u32[]{:S(2)}) collective-permute-start(bf16[40,2048]{1,0:T(8,128)(2,1)S(1)} %get-tuple-element.152), channel_id=1, source_target_pairs={{0,8},{4,12},{8,0},{12,4},{1,9},{5,13},{9,1},{13,5},{2,10},{6,14},... | collective-permute-start | bytes 491528 | tf_op jit(solution)/shard_map/ppermute | solution.py:373
  27.3 15.0 %collective-permute-start.44 = (bf16[40,2048]{1,0:T(8,128)(2,1)S(1)}, bf16[40,2048]{1,0:T(8,128)(2,1)S(1)}, u32[]{:S(2)}, u32[]{:S(2)}) collective-permute-start(bf16[40,2048]{1,0:T(8,128)(2,1)S(1)} %get-tuple-element.153), channel_id=1, source_target_pairs={{0,4},{4,8},{8,12},{12,0},{1,5},{5,9},{9,13},{13,1},{2,6},{6,10},{... | collective-permute-start | bytes 491528 | tf_op jit(solution)/shard_map/ppermute | solution.py:373
  29.3 3.7 %collective-permute-start.48 = (f32[8,128]{1,0:T(8,128)S(1)}, f32[8,128]{1,0:T(8,128)S(1)}, u32[]{:S(2)}, u32[]{:S(2)}) collective-permute-start(f32[8,128]{1,0:T(8,128)S(1)} %broadcast_in_dim.2), channel_id=1, source_target_pairs={{0,16},{16,0},{1,17},{17,1},{2,18},{18,2},{3,19},{19,3},{4,20},{20... | collective-permute-start | bytes 12296 | tf_op jit(solution)/shard_map/ppermute | solution.py:373
  33.0 1.2 collective-permute-start.49
  34.2 8.2 %collective-permute-start.50 = (f32[8,128]{1,0:T(8,128)S(1)}, f32[8,128]{1,0:T(8,128)S(1)}, u32[]{:S(2)}, u32[]{:S(2)}) collective-permute-start(f32[8,128]{1,0:T(8,128)S(1)} %max.10), channel_id=1, source_target_pairs={{0,2},{1,3},{2,0},{3,1},{4,6},{5,7},{6,4},{7,5},{8,10},{9,11},{10,... | collective-permute-start | bytes 12296 | tf_op jit(solution)/shard_map/ppermute | solution.py:378
  43.7 2.2 %collective-permute-start = (bf16[160,2176]{1,0:T(8,128)(2,1)S(1)}, bf16[160,2176]{1,0:T(8,128)(2,1)S(1)}, u32[]{:S(2)}, u32[]{:S(2)}) collective-permute-start(bf16[160,2176]{1,0:T(8,128)(2,1)S(1)} %get-tuple-element.33.refs_2_), channel_id=1, source_target_pairs={{0,1},{1,0},{2,3},{3,2},{4,5},{5,4},{6,7},{7,6},{8,9},{9,8},{10,11... | collective-permute-start | bytes 2088968 | tf_op jit(solution)/shard_map/cond/branch_0_fun/ppermute | solution.py:378
  43.8 17.1 %collective-permute-start.2 = (bf16[160,2048]{1,0:T(8,128)(2,1)S(1)}, bf16[160,2048]{1,0:T(8,128)(2,1)S(1)}, u32[]{:S(2)}, u32[]{:S(2)}) collective-permute-start(bf16[160,2048]{1,0:T(8,128)(2,1)S(1)} %get-tuple-element.34.refs_4_), channel_id=1, source_target_pairs={{0,2},{1,3},{2,0},{3,1},{4,6},{5,7},{6,4},{7,5},{8,10},{9,11},{10,... | collective-permute-start | bytes 1966088 | tf_op jit(solution)/shard_map/cond/branch_0_fun/ppermute | solution.py:378
  44.4 16.6 %collective-permute-start.1 = (bf16[160,2048]{1,0:T(8,128)(2,1)S(1)}, bf16[160,2048]{1,0:T(8,128)(2,1)S(1)}, u32[]{:S(2)}, u32[]{:S(2)}) collective-permute-start(bf16[160,2048]{1,0:T(8,128)(2,1)S(1)} %get-tuple-element.34.refs_4_), channel_id=1, source_target_pairs={{0,1},{1,0},{2,3},{3,2},{4,5},{5,4},{6,7},{7,6},{8,9},{9,8},{10,11... | collective-permute-start | bytes 1966088 | tf_op jit(solution)/shard_map/cond/branch_0_fun/ppermute | solution.py:378
  59.6 1.0 copy-start.9
  60.9 2.1 %collective-permute-start.3 = (bf16[160,2048]{1,0:T(8,128)(2,1)S(1)}, bf16[160,2048]{1,0:T(8,128)(2,1)S(1)}, u32[]{:S(2)}, u32[]{:S(2)}) collective-permute-start(bf16[160,2048]{1,0:T(8,128)(2,1)S(1)} %collective-permute-done.2.refs_6_), channel_id=1, source_target_pairs={{0,1},{1,0},{2,3},{3,2},{4,5},{5,4},{6,7},{7,6},{8,9},{9,8},{10,11... | collective-permute-start | bytes 1966088 | tf_op jit(solution)/shard_map/cond/branch_0_fun/ppermute | solution.py:378
  80.8 1.8 %collective-permute-start.5 = (bf16[160,1152]{1,0:T(8,128)(2,1)S(1)}, bf16[160,1152]{1,0:T(8,128)(2,1)S(1)}, u32[]{:S(2)}, u32[]{:S(2)}) collective-permute-start(bf16[160,1152]{1,0:T(8,128)(2,1)S(1)} %get-tuple-element.47), channel_id=1, source_target_pairs={{0,1},{1,0},{2,3},{3,2},{4,5},{5,4},{6,7},{7,6},{8,9},{9,8},{10,11... | collective-permute-start | bytes 1105928 | tf_op jit(solution)/shard_map/cond/branch_0_fun/ppermute | solution.py:378
  82.7 10.7 %collective-permute-start.6 = (bf16[160,1152]{1,0:T(8,128)(2,1)S(1)}, bf16[160,1152]{1,0:T(8,128)(2,1)S(1)}, u32[]{:S(2)}, u32[]{:S(2)}) collective-permute-start(bf16[160,1152]{1,0:T(8,128)(2,1)S(1)} %add_convert_fusion.1), channel_id=1, source_target_pairs={{0,2},{1,3},{2,0},{3,1},{4,6},{5,7},{6,4},{7,5},{8,10},{9,11},{10,... | collective-permute-start | bytes 1105928 | tf_op jit(solution)/shard_map/cond/branch_0_fun/ppermute | solution.py:378
  83.3 10.6 %collective-permute-start.4 = (bf16[160,1152]{1,0:T(8,128)(2,1)S(1)}, bf16[160,1152]{1,0:T(8,128)(2,1)S(1)}, u32[]{:S(2)}, u32[]{:S(2)}) collective-permute-start(bf16[160,1152]{1,0:T(8,128)(2,1)S(1)} %get-tuple-element.45), channel_id=1, source_target_pairs={{0,1},{1,0},{2,3},{3,2},{4,5},{5,4},{6,7},{7,6},{8,9},{9,8},{10,11... | collective-permute-start | bytes 1105928 | tf_op jit(solution)/shard_map/cond/branch_0_fun/ppermute | solution.py:378
  83.3 18.2 %copy-start.6 = (bf16[16,64,2048]{2,1,0:T(8,128)(2,1)S(1)}, bf16[16,64,2048]{2,1,0:T(8,128)(2,1)}, u32[]{:S(2)}) copy-start(bf16[16,64,2048]{2,1,0:T(8,128)(2,1)} %get-tuple-element.60.cs_ref) | copy-start | bytes 12582916 | tf_op jit(solution)/shard_map/cond
  93.4 14.5 %collective-permute-start.10 = (bf16[160,1024]{1,0:T(8,128)(2,1)S(1)}, bf16[160,1024]{1,0:T(8,128)(2,1)S(1)}, u32[]{:S(2)}, u32[]{:S(2)}) collective-permute-start(bf16[160,1024]{1,0:T(8,128)(2,1)S(1)} %get-tuple-element.55), channel_id=1, source_target_pairs={{0,1},{1,0},{2,3},{3,2},{4,5},{5,4},{6,7},{7,6},{8,9},{9,8},{10,11... | collective-permute-start | bytes 983048 | tf_op jit(solution)/shard_map/cond/branch_0_fun/ppermute | solution.py:378
  93.4 2.1 %collective-permute-start.11 = (bf16[160,1024]{1,0:T(8,128)(2,1)S(1)}, bf16[160,1024]{1,0:T(8,128)(2,1)S(1)}, u32[]{:S(2)}, u32[]{:S(2)}) collective-permute-start(bf16[160,1024]{1,0:T(8,128)(2,1)S(1)} %get-tuple-element.57), channel_id=1, source_target_pairs={{0,1},{1,0},{2,3},{3,2},{4,5},{5,4},{6,7},{7,6},{8,9},{9,8},{10,11... | collective-permute-start | bytes 983048 | tf_op jit(solution)/shard_map/cond/branch_0_fun/ppermute | solution.py:378
  95.6 12.3 %collective-permute-start.12 = (bf16[160,1024]{1,0:T(8,128)(2,1)S(1)}, bf16[160,1024]{1,0:T(8,128)(2,1)S(1)}, u32[]{:S(2)}, u32[]{:S(2)}) collective-permute-start(bf16[160,1024]{1,0:T(8,128)(2,1)S(1)} %add_convert_fusion.4), channel_id=1, source_target_pairs={{0,2},{1,3},{2,0},{3,1},{4,6},{5,7},{6,4},{7,5},{8,10},{9,11},{10,... | collective-permute-start | bytes 983048 | tf_op jit(solution)/shard_map/cond/branch_0_fun/ppermute | solution.py:378
  96.2 11.6 %collective-permute-start.9 = (bf16[40,1152]{1,0:T(8,128)(2,1)S(1)}, bf16[40,1152]{1,0:T(8,128)(2,1)S(1)}, u32[]{:S(2)}, u32[]{:S(2)}) collective-permute-start(bf16[40,1152]{1,0:T(8,128)(2,1)S(1)} %get-tuple-element.122), channel_id=1, source_target_pairs={{0,4},{4,8},{8,12},{12,0},{1,5},{5,9},{9,13},{13,1},{2,6},{6,10},{... | collective-permute-start | bytes 276488 | tf_op jit(solution)/shard_map/cond/branch_0_fun/ppermute | solution.py:373
  96.6 11.2 %collective-permute-start.8 = (bf16[40,1152]{1,0:T(8,128)(2,1)S(1)}, bf16[40,1152]{1,0:T(8,128)(2,1)S(1)}, u32[]{:S(2)}, u32[]{:S(2)}) collective-permute-start(bf16[40,1152]{1,0:T(8,128)(2,1)S(1)} %get-tuple-element.123), channel_id=1, source_target_pairs={{0,8},{4,12},{8,0},{12,4},{1,9},{5,13},{9,1},{13,5},{2,10},{6,14},... | collective-permute-start | bytes 276488 | tf_op jit(solution)/shard_map/cond/branch_0_fun/ppermute | solution.py:373
  98.6 9.2 %collective-permute-start.7 = (bf16[40,1152]{1,0:T(8,128)(2,1)S(1)}, bf16[40,1152]{1,0:T(8,128)(2,1)S(1)}, u32[]{:S(2)}, u32[]{:S(2)}) collective-permute-start(bf16[40,1152]{1,0:T(8,128)(2,1)S(1)} %get-tuple-element.124), channel_id=1, source_target_pairs={{0,12},{4,0},{8,4},{12,8},{1,13},{5,1},{9,5},{13,9},{2,14},{6,2},{... | collective-permute-start | bytes 276488 | tf_op jit(solution)/shard_map/cond/branch_0_fun/ppermute | solution.py:373
  108.1 7.0 %collective-permute-start.15 = (bf16[40,1024]{1,0:T(8,128)(2,1)S(1)}, bf16[40,1024]{1,0:T(8,128)(2,1)S(1)}, u32[]{:S(2)}, u32[]{:S(2)}) collective-permute-start(bf16[40,1024]{1,0:T(8,128)(2,1)S(1)} %get-tuple-element.126), channel_id=1, source_target_pairs={{0,4},{4,8},{8,12},{12,0},{1,5},{5,9},{9,13},{13,1},{2,6},{6,10},{... | collective-permute-start | bytes 245768 | tf_op jit(solution)/shard_map/cond/branch_0_fun/ppermute | solution.py:373
  108.4 8.5 %collective-permute-start.14 = (bf16[40,1024]{1,0:T(8,128)(2,1)S(1)}, bf16[40,1024]{1,0:T(8,128)(2,1)S(1)}, u32[]{:S(2)}, u32[]{:S(2)}) collective-permute-start(bf16[40,1024]{1,0:T(8,128)(2,1)S(1)} %get-tuple-element.127), channel_id=1, source_target_pairs={{0,8},{4,12},{8,0},{12,4},{1,9},{5,13},{9,1},{13,5},{2,10},{6,14},... | collective-permute-start | bytes 245768 | tf_op jit(solution)/shard_map/cond/branch_0_fun/ppermute | solution.py:373
  110.6 6.3 %collective-permute-start.13 = (bf16[40,1024]{1,0:T(8,128)(2,1)S(1)}, bf16[40,1024]{1,0:T(8,128)(2,1)S(1)}, u32[]{:S(2)}, u32[]{:S(2)}) collective-permute-start(bf16[40,1024]{1,0:T(8,128)(2,1)S(1)} %get-tuple-element.128), channel_id=1, source_target_pairs={{0,12},{4,0},{8,4},{12,8},{1,13},{5,1},{9,5},{13,9},{2,14},{6,2},{... | collective-permute-start | bytes 245768 | tf_op jit(solution)/shard_map/cond/branch_0_fun/ppermute | solution.py:373

commit v4 on v3

--- a/solution.py
+++ b/solution.py
@@ -12,7 +12,7 @@
 OVER = 2
 BF = jnp.bfloat16
 F32 = jnp.float32
-VMEM_BYTES = 48 * 1024 * 1024
+MIB = 1024 * 1024
 
 
 def dot_nn(a, b):
@@ -27,8 +27,12 @@
     return lax.dot_general(a, b, (((0,), (0,)), ((), ())), preferred_element_type=F32)
 
 
-def params():
-    return pltpu.CompilerParams(vmem_limit_bytes=VMEM_BYTES)
+def params(mib=18):
+    return pltpu.CompilerParams(vmem_limit_bytes=mib * MIB)
+
+
+def big_limit(rows):
+    return 20 + -(-8 * rows.shape[0] * rows.shape[1] * 2 // MIB)
 
 
 def cost(flops, moved):
@@ -173,7 +177,7 @@
         out_specs=[pl.BlockSpec((step, expert_rows, hidden), by_expert)] * 2,
         out_shape=[shape, shape],
         scratch_shapes=[pltpu.VMEM((experts, expert_rows, width), BF)],
-        compiler_params=params(),
+        compiler_params=params(big_limit(x_list[0])),
         cost_estimate=cost(2e9, 3e7),
         name="gate_up",
     )(*x_list, gate, up)
@@ -242,7 +246,7 @@
             pltpu.VMEM((experts, expert_rows, width), BF),
             pltpu.VMEM((experts, expert_rows, META), BF),
         ],
-        compiler_params=params(),
+        compiler_params=params(big_limit(c_list[0])),
         cost_estimate=cost(2e9, 2e7),
         name="hidden_grads",
     )(*x_list, *c_list, g, u, down)
@@ -305,29 +309,33 @@
     )(*args)
 
 
-def down_kernel(hw_ref, cs_ref, out_ref):
+def down_kernel(*refs):
+    hw_ref, cs_ref, out_ref = refs[0], refs[1], refs[-1]
     for i in range(hw_ref.shape[0]):
         out_ref[i] = dot_tn(hw_ref[i], cs_ref[i]).astype(BF)
 
 
-def down_layer(hw, cs):
+def down_layer(hw, cs, low, count, sofar=None):
     experts, rows, hidden = hw.shape
     width = cs.shape[2]
-    step = step_of(experts, 4)
-    by_expert = lambda e: (e, 0, 0)
+    step = step_of(count, 4)
+    by_expert = lambda e: (e + low // step, 0, 0)
+    more = [] if sofar is None else [sofar]
     return pl.pallas_call(
         down_kernel,
-        grid=(experts // step,),
+        grid=(count // step,),
         in_specs=[
             pl.BlockSpec((step, rows, hidden), by_expert),
             pl.BlockSpec((step, rows, width), by_expert),
-        ],
+        ]
+        + [pl.BlockSpec(memory_space=pl.ANY)] * len(more),
         out_specs=pl.BlockSpec((step, hidden, width), by_expert),
         out_shape=jax.ShapeDtypeStruct((experts, hidden, width), BF),
+        input_output_aliases={2: 0} if more else {},
         compiler_params=params(),
-        cost_estimate=cost(1e9, 1.8e7),
+        cost_estimate=cost(5e8, 9e6),
         name="down_grads",
-    )(hw, cs)
+    )(hw, cs, *more)
 
 
 def home_kernel(per_device, room, n_shards, n_half, n_blocks, ids_ref, *refs):
@@ -460,13 +468,15 @@
     come_1 = far_hop(go_1, n_dp)
     dg, du = lax.optimization_barrier((dg, du, go_1))[:2]
     second = third_layer(x_list, dg, du, gate, up, None, 1, 2, room, n_shards)
-    second = after(second, come_1)
+    early = per_device // 2
+    down_grad = down_layer(after(hw, second), cs, 0, early) if early else None
+    second = after(second, (come_1, down_grad))
     stay_2, go_2 = near_sums(second, n_dp)
     come_2 = far_hop(go_2, n_dp)
-    down_grad = down_layer(after(hw, go_2), cs)
     home_1 = from_shards(add_rows(stay_1, come_1), room, n_shards)
-    come_2 = after(come_2, (down_grad, home_1))
-    home_2 = from_shards(add_rows(stay_2, come_2), room, n_shards)
+    down_grad = down_layer(after(hw, go_2), cs, early, per_device - early, down_grad)
+    rows_2 = add_rows(stay_2, after(come_2, down_grad))
+    home_2 = from_shards(rows_2, room, n_shards)
     token_grad, route = home_rows(ids, [home_1, home_2], width, per_device, room, n_shards)
     return token_grad, route.reshape(-1, 1), down_grad
 

time: 119 us -> 114 us (0.958)
  Pallas kernels: 49.2 us -> 42.3 us
  waiting for transfers between devices: 39 us -> 40.9 us
    pallas_call x2, Pallas kernels: 14.8 us -> 9.43 us  [third_layer(): pl.pallas_call(functools.partial(third_kernel, n_dp, room, n_shards, rout...]
    pallas_call x1 -> x2, Pallas kernels: 6.38 us -> 4.05 us  [down_layer(): pl.pallas_call(down_kernel, grid=(count // step,), in_specs=[pl.BlockSpec...]
    ppermute x14, waiting for transfers between devices: 10.6 us -> 12.8 us  [swapped(): return lax.ppermute(value, axis, [(i, i ^ bit) for i in range(n)])]
    pallas_call x1, Pallas kernels: 13.6 us -> 15.3 us  [first_layer(): pl.pallas_call(functools.partial(first_kernel, n_dp, room, n_shards), gri...]
  transfers between devices with their start and end apart: 27 -> 27, of which waited for: 13 -> 13; matrix products, arithmetic and copies ran while one was open for 0% -> 1% of each run, Pallas kernels for 23% -> 21%
where the time goes in v4:
time: 114 us; the launch traced here: 113 us
  Pallas kernels  42.3 us (37%)
  waiting for transfers between devices  40.9 us (36%)
  starting transfers between devices  27.2 us (24%)
  between operations  1.42 us (1%)
    ppermute x13, waiting for transfers between devices, shifted(): return lax.ppermute(value, axis, [(i, (i + step) % n) for i in range(n)])  28.2 us
    ppermute x13, starting transfers between devices, shifted(): return lax.ppermute(value, axis, [(i, (i + step) % n) for i in range(n)])  22.1 us
    pallas_call x1, Pallas kernels, first_layer(): pl.pallas_call(functools.partial(first_kernel, n_dp, room, n_shards), gri...  15.3 us
    ppermute x14, waiting for transfers between devices, swapped(): return lax.ppermute(value, axis, [(i, i ^ bit) for i in range(n)])  12.8 us
    pallas_call x1, Pallas kernels, second_layer(): pl.pallas_call(functools.partial(second_kernel, n_dp, room, n_shards), gr...  9.66 us
    pallas_call x2, Pallas kernels, third_layer(): pl.pallas_call(functools.partial(third_kernel, n_dp, room, n_shards, rout...  9.43 us
    ppermute x14, starting transfers between devices, swapped(): return lax.ppermute(value, axis, [(i, i ^ bit) for i in range(n)])  5.12 us
    pallas_call x2, Pallas kernels, down_layer(): pl.pallas_call(down_kernel, grid=(count // step,), in_specs=[pl.BlockSpec...  4.05 us
  transfers between devices with their start and end apart: 27, of which 13 were waited for; matrix products, arithmetic and copies ran while one was open for 1% of the time, Pallas kernels for 21%

profile of v4, /device:TPU:0, one launch (start us, length us, event | category | flops | bytes accessed | tf_op | source)
XLA Modules:
  0.0 113.5 jit_solution(16148258447337821662)
XLA Ops:
  0.6 2.0 %pack_rows.3 = (bf16[160,2176]{1,0:T(8,128)(2,1)S(1)}, bf16[160,2048]{1,0:T(8,128)(2,1)S(1)}) custom-call(s32[1,128]{1,0:T(1,128)} %bitcast.17, bf16[128,2048]{1,0:T(8,128)(2,1)} %tok_ref.1, bf16[128,2048]{1,0:T(8,128)(2,1)} %cot_ref.1, bf16[1,128]{1,0:T(2,128)(2,1)} %bitcast.20), custom_call_target="tpu_custom_call" | custom-call | flops 400000000 | bytes 4000000 | tf_op jit(solution)/shard_map/pack_rows/pallas_call | solution.py:104
  2.7 5.1 %collective-permute-start.42 = (bf16[40,2176]{1,0:T(8,128)(2,1)S(1)}, bf16[40,2176]{1,0:T(8,128)(2,1)S(1)}, u32[]{:S(2)}, u32[]{:S(2)}) collective-permute-start(bf16[40,2176]{1,0:T(8,128)(2,1)S(1)} %get-tuple-element.149), channel_id=1, source_target_pairs={{0,12},{4,0},{8,4},{12,8},{1,13},{5,1},{9,5},{13,9},{2,14},{6,2},{... | collective-permute-start | bytes 522248 | tf_op jit(solution)/shard_map/ppermute | solution.py:381
  7.8 1.0 collective-permute-start.40
  8.8 3.9 %collective-permute-done.42 = bf16[40,2176]{1,0:T(8,128)(2,1)S(1)} collective-permute-done((bf16[40,2176]{1,0:T(8,128)(2,1)S(1)}, bf16[40,2176]{1,0:T(8,128)(2,1)S(1)}, u32[]{:S(2)}, u32[]{:S(2)}) %collective-permute-start.42) | collective-permute-done | bytes 174112 | tf_op jit(solution)/shard_map/ppermute | solution.py:381
  12.7 9.9 %collective-permute-done.41 = bf16[40,2176]{1,0:T(8,128)(2,1)S(1)} collective-permute-done((bf16[40,2176]{1,0:T(8,128)(2,1)S(1)}, bf16[40,2176]{1,0:T(8,128)(2,1)S(1)}, u32[]{:S(2)}, u32[]{:S(2)}) %collective-permute-start.41) | collective-permute-done | bytes 174112 | tf_op jit(solution)/shard_map/ppermute | solution.py:381
  22.7 0.1 collective-permute-start.47
  22.8 1.6 %collective-permute-start.43 = (bf16[160,2176]{1,0:T(8,128)(2,1)S(1)}, bf16[160,2176]{1,0:T(8,128)(2,1)S(1)}, u32[]{:S(2)}, u32[]{:S(2)}) collective-permute-start(bf16[160,2176]{1,0:T(8,128)(2,1)S(1)} %pad_maximum_fusion.2), channel_id=1, source_target_pairs={{0,2},{1,3},{2,0},{3,1},{4,6},{5,7},{6,4},{7,5},{8,10},{9,11},{10,... | collective-permute-start | bytes 2088968 | tf_op jit(solution)/shard_map/ppermute | solution.py:386
  24.4 0.9 collective-permute-start.46
  25.3 2.0 %collective-permute-start.45 = (bf16[40,2048]{1,0:T(8,128)(2,1)S(1)}, bf16[40,2048]{1,0:T(8,128)(2,1)S(1)}, u32[]{:S(2)}, u32[]{:S(2)}) collective-permute-start(bf16[40,2048]{1,0:T(8,128)(2,1)S(1)} %get-tuple-element.154), channel_id=1, source_target_pairs={{0,8},{4,12},{8,0},{12,4},{1,9},{5,13},{9,1},{13,5},{2,10},{6,14},... | collective-permute-start | bytes 491528 | tf_op jit(solution)/shard_map/ppermute | solution.py:381
  27.3 1.9 %collective-permute-start.44 = (bf16[40,2048]{1,0:T(8,128)(2,1)S(1)}, bf16[40,2048]{1,0:T(8,128)(2,1)S(1)}, u32[]{:S(2)}, u32[]{:S(2)}) collective-permute-start(bf16[40,2048]{1,0:T(8,128)(2,1)S(1)} %get-tuple-element.155), channel_id=1, source_target_pairs={{0,4},{4,8},{8,12},{12,0},{1,5},{5,9},{9,13},{13,1},{2,6},{6,10},{... | collective-permute-start | bytes 491528 | tf_op jit(solution)/shard_map/ppermute | solution.py:381
  29.3 1.6 %collective-permute-start.48 = (f32[8,128]{1,0:T(8,128)S(1)}, f32[8,128]{1,0:T(8,128)S(1)}, u32[]{:S(2)}, u32[]{:S(2)}) collective-permute-start(f32[8,128]{1,0:T(8,128)S(1)} %broadcast_in_dim.2), channel_id=1, source_target_pairs={{0,16},{16,0},{1,17},{17,1},{2,18},{18,2},{3,19},{19,3},{4,20},{20... | collective-permute-start | bytes 12296 | tf_op jit(solution)/shard_map/ppermute | solution.py:381
  30.9 2.1 %collective-permute-done.48 = f32[8,128]{1,0:T(8,128)S(1)} collective-permute-done((f32[8,128]{1,0:T(8,128)S(1)}, f32[8,128]{1,0:T(8,128)S(1)}, u32[]{:S(2)}, u32[]{:S(2)}) %collective-permute-start.48) | collective-permute-done | bytes 4128 | tf_op jit(solution)/shard_map/ppermute | solution.py:381
  33.0 1.2 %collective-permute-done.49 = f32[8,128]{1,0:T(8,128)S(1)} collective-permute-done((f32[8,128]{1,0:T(8,128)S(1)}, f32[8,128]{1,0:T(8,128)S(1)}, u32[]{:S(2)}, u32[]{:S(2)}) %collective-permute-start.49) | collective-permute-done | bytes 4128 | tf_op jit(solution)/shard_map/ppermute | solution.py:386
  34.2 0.5 collective-permute-start.50
  34.7 7.6 %collective-permute-done.45 = bf16[40,2048]{1,0:T(8,128)(2,1)S(1)} collective-permute-done((bf16[40,2048]{1,0:T(8,128)(2,1)S(1)}, bf16[40,2048]{1,0:T(8,128)(2,1)S(1)}, u32[]{:S(2)}, u32[]{:S(2)}) %collective-permute-start.45) | collective-permute-done | bytes 163872 | tf_op jit(solution)/shard_map/ppermute | solution.py:381
  42.4 0.6 slice.111
  43.7 69.8 %conditional.1 = (bf16[128,2048]{1,0:T(8,128)(2,1)}, bf16[128,1]{0,1:T(2,128)(2,1)}, bf16[16,192,2048]{2,1,0:T(8,128)(2,1)}) conditional(s32[]{:T(128)} %bitcast.4, (bf16[160,2176]{1,0:T(8,128)(2,1)S(1)}, bf16[160,2048]{1,0:T(8,128)(2,1)S(1)}, bf16[160,2176]{1,0:T(8,128)(2,1)S(1)}, bf16[160,2176]{1,0:T(8,128)(2,1)S(1)}, ...), branch_computations={%region_1.0_spmd, %region_2.0_spmd} | conditional | flops 7615335424 | bytes 259911136 | solution.py:526
  43.8 0.6 collective-permute-start.2
  44.3 0.2 collective-permute-start.1
  44.5 1.4 %collective-permute-done.refs_3_ = bf16[160,2176]{1,0:T(8,128)(2,1)S(1)} collective-permute-done((bf16[160,2176]{1,0:T(8,128)(2,1)S(1)}, bf16[160,2176]{1,0:T(8,128)(2,1)S(1)}, u32[]{:S(2)}, u32[]{:S(2)}) %collective-permute-start) | collective-permute-done | bytes 696352 | tf_op jit(solution)/shard_map/cond/branch_0_fun/ppermute | solution.py:386
  45.9 15.3 %gate_up.2 = (f32[16,64,192]{2,1,0:T(8,128)S(1)}, f32[16,64,192]{2,1,0:T(8,128)S(1)}) custom-call(bf16[160,2176]{1,0:T(8,128)(2,1)S(1)} %get-tuple-element.31.refs_0_, bf16[160,2176]{1,0:T(8,128)(2,1)S(1)} %get-tuple-element.32.refs_1_, bf16[160,2176]{1,0:T(8,128)(2,1)S(1)} %get-tuple-element.33.refs_2_, bf16[160,2176]{1,0:T(8,128)(2,1)S(1)} %collective-permute-done.refs_3_, ...), custom_call_target="tpu_custom_call" | custom-call | flops 2000000000 | bytes 30000000 | tf_op jit(solution)/shard_map/cond/branch_0_fun/gate_up/pallas_call | solution.py:172
  61.2 0.2 collective-permute-start.3
  61.4 2.0 %collective-permute-done.3.refs_7_ = bf16[160,2048]{1,0:T(8,128)(2,1)S(1)} collective-permute-done((bf16[160,2048]{1,0:T(8,128)(2,1)S(1)}, bf16[160,2048]{1,0:T(8,128)(2,1)S(1)}, u32[]{:S(2)}, u32[]{:S(2)}) %collective-permute-start.3) | collective-permute-done | bytes 655392 | tf_op jit(solution)/shard_map/cond/branch_0_fun/ppermute | solution.py:386
  63.4 9.7 %hidden_grads.2 = (bf16[16,64,192]{2,1,0:T(8,128)(2,1)S(1)}, bf16[16,64,192]{2,1,0:T(8,128)(2,1)S(1)}, bf16[16,64,192]{2,1,0:T(8,128)(2,1)S(1)}, bf16[16,64,2048...) custom-call(bf16[160,2176]{1,0:T(8,128)(2,1)S(1)} %get-tuple-element.31.refs_0_, ...), custom_call_target="tpu_custom_call" | custom-call | flops 2000000000 | bytes 20000000 | tf_op jit(solution)/shard_map/cond/branch_0_fun/hidden_grads/pallas_call | solution.py:228
  73.1 4.8 %input_grads.4 = (bf16[160,1152]{1,0:T(8,128)(2,1)S(1)}, bf16[160,1152]{1,0:T(8,128)(2,1)S(1)}, bf16[160,1152]{1,0:T(8,128)(2,1)S(1)}, bf16[160,1152]{1,0:T(8,128)(2,1)S(1)}) custom-call(bf16[160,2176]{1,0:T(8,128)(2,1)S(1)} %get-tuple-element.31.refs_0_, bf16[160,2176]{1,0:T(8,128)(2,1)S(1)} %get-tuple-element.32.refs_1_, ...), custom_call_target="tpu_custom_call" | custom-call | flops 1000000000 | bytes 15000000 | tf_op jit(solution)/shard_map/cond/branch_0_fun/input_grads/pallas_call | solution.py:299
  77.9 0.2 collective-permute-start.5
  78.1 1.5 %collective-permute-done.5 = bf16[160,1152]{1,0:T(8,128)(2,1)S(1)} collective-permute-done((bf16[160,1152]{1,0:T(8,128)(2,1)S(1)}, bf16[160,1152]{1,0:T(8,128)(2,1)S(1)}, u32[]{:S(2)}, u32[]{:S(2)}) %collective-permute-start.5) | collective-permute-done | bytes 368672 | tf_op jit(solution)/shard_map/cond/branch_0_fun/ppermute | solution.py:386
  79.6 0.1 add_convert_fusion.1
  79.7 0.6 collective-permute-start.6
  80.3 4.7 %input_grads.5 = (bf16[160,1024]{1,0:T(8,128)(2,1)S(1)}, bf16[160,1024]{1,0:T(8,128)(2,1)S(1)}, bf16[160,1024]{1,0:T(8,128)(2,1)S(1)}, bf16[160,1024]{1,0:T(8,128)(2,1)S(1)}) custom-call(bf16[160,2176]{1,0:T(8,128)(2,1)S(1)} %get-tuple-element.31.refs_0_, bf16[160,2176]{1,0:T(8,128)(2,1)S(1)} %get-tuple-element.32.refs_1_, ...), custom_call_target="tpu_custom_call" | custom-call | flops 1000000000 | bytes 15000000 | tf_op jit(solution)/shard_map/cond/branch_0_fun/input_grads/pallas_call | solution.py:299
  85.0 2.0 %down_grads.4.refs_2_ = bf16[16,192,2048]{2,1,0:T(8,128)(2,1)S(1)} custom-call(bf16[16,64,192]{2,1,0:T(8,128)(2,1)S(1)} %get-tuple-element.61.refs_0_, bf16[16,64,2048]{2,1,0:T(8,128)(2,1)S(1)} %get-tuple-element.56.refs_1_), custom_call_target="tpu_custom_call" | custom-call | flops 500000000 | bytes 9000000 | tf_op jit(solution)/shard_map/cond/branch_0_fun/down_grads/pallas_call | solution.py:324
  87.1 3.4 %collective-permute-done.6 = bf16[160,1152]{1,0:T(8,128)(2,1)S(1)} collective-permute-done((bf16[160,1152]{1,0:T(8,128)(2,1)S(1)}, bf16[160,1152]{1,0:T(8,128)(2,1)S(1)}, u32[]{:S(2)}, u32[]{:S(2)}) %collective-permute-start.6) | collective-permute-done | bytes 368672 | tf_op jit(solution)/shard_map/cond/branch_0_fun/ppermute | solution.py:386
  90.4 0.5 collective-permute-start.11
  91.0 0.1 add_convert_fusion
  91.1 1.4 %collective-permute-done.11 = bf16[160,1024]{1,0:T(8,128)(2,1)S(1)} collective-permute-done((bf16[160,1024]{1,0:T(8,128)(2,1)S(1)}, bf16[160,1024]{1,0:T(8,128)(2,1)S(1)}, u32[]{:S(2)}, u32[]{:S(2)}) %collective-permute-start.11) | collective-permute-done | bytes 327712 | tf_op jit(solution)/shard_map/cond/branch_0_fun/ppermute | solution.py:386
  92.5 0.1 add_convert_fusion.4
  92.6 0.6 collective-permute-start.12
  93.3 0.4 collective-permute-start.9
  93.7 2.0 %collective-permute-start.8 = (bf16[40,1152]{1,0:T(8,128)(2,1)S(1)}, bf16[40,1152]{1,0:T(8,128)(2,1)S(1)}, u32[]{:S(2)}, u32[]{:S(2)}) collective-permute-start(bf16[40,1152]{1,0:T(8,128)(2,1)S(1)} %get-tuple-element.125), channel_id=1, source_target_pairs={{0,8},{4,12},{8,0},{12,4},{1,9},{5,13},{9,1},{13,5},{2,10},{6,14},... | collective-permute-start | bytes 276488 | tf_op jit(solution)/shard_map/cond/branch_0_fun/ppermute | solution.py:381
  95.7 2.8 %collective-permute-start.7 = (bf16[40,1152]{1,0:T(8,128)(2,1)S(1)}, bf16[40,1152]{1,0:T(8,128)(2,1)S(1)}, u32[]{:S(2)}, u32[]{:S(2)}) collective-permute-start(bf16[40,1152]{1,0:T(8,128)(2,1)S(1)} %get-tuple-element.126), channel_id=1, source_target_pairs={{0,12},{4,0},{8,4},{12,8},{1,13},{5,1},{9,5},{13,9},{2,14},{6,2},{... | collective-permute-start | bytes 276488 | tf_op jit(solution)/shard_map/cond/branch_0_fun/ppermute | solution.py:381
  98.5 2.0 %down_grads.5 = bf16[16,192,2048]{2,1,0:T(8,128)(2,1)S(1)} custom-call(bf16[16,64,192]{2,1,0:T(8,128)(2,1)S(1)} %get-tuple-element.61.refs_0_, bf16[16,64,2048]{2,1,0:T(8,128)(2,1)S(1)} %get-tuple-element.56.refs_1_, bf16[16,192,2048]{2,1,0:T(8,128)(2,1)S(1)} %down_grads.4.refs_2_), custom_call_target="tpu_custom_call", output_to_operand_aliasing={{}: (2, {})} | custom-call | flops 500000000 | bytes 9000000 | tf_op jit(solution)/shard_map/cond/branch_0_fun/down_grads/pallas_call | solution.py:324
  100.6 1.9 %collective-permute-done.12 = bf16[160,1024]{1,0:T(8,128)(2,1)S(1)} collective-permute-done((bf16[160,1024]{1,0:T(8,128)(2,1)S(1)}, bf16[160,1024]{1,0:T(8,128)(2,1)S(1)}, u32[]{:S(2)}, u32[]{:S(2)}) %collective-permute-start.12) | collective-permute-done | bytes 327712 | tf_op jit(solution)/shard_map/cond/branch_0_fun/ppermute | solution.py:386
  102.5 0.2 add_convert_fusion.3
  102.7 1.4 %collective-permute-start.14 = (bf16[40,1024]{1,0:T(8,128)(2,1)S(1)}, bf16[40,1024]{1,0:T(8,128)(2,1)S(1)}, u32[]{:S(2)}, u32[]{:S(2)}) collective-permute-start(bf16[40,1024]{1,0:T(8,128)(2,1)S(1)} %get-tuple-element.129), channel_id=1, source_target_pairs={{0,8},{4,12},{8,0},{12,4},{1,9},{5,13},{9,1},{13,5},{2,10},{6,14},... | collective-permute-start | bytes 245768 | tf_op jit(solution)/shard_map/cond/branch_0_fun/ppermute | solution.py:381
  104.1 2.8 %collective-permute-start.13 = (bf16[40,1024]{1,0:T(8,128)(2,1)S(1)}, bf16[40,1024]{1,0:T(8,128)(2,1)S(1)}, u32[]{:S(2)}, u32[]{:S(2)}) collective-permute-start(bf16[40,1024]{1,0:T(8,128)(2,1)S(1)} %get-tuple-element.130), channel_id=1, source_target_pairs={{0,12},{4,0},{8,4},{12,8},{1,13},{5,1},{9,5},{13,9},{2,14},{6,2},{... | collective-permute-start | bytes 245768 | tf_op jit(solution)/shard_map/cond/branch_0_fun/ppermute | solution.py:381
  107.0 2.9 %collective-permute-done.15.refs_7_ = bf16[40,1024]{1,0:T(8,128)(2,1)S(1)} collective-permute-done((bf16[40,1024]{1,0:T(8,128)(2,1)S(1)}, bf16[40,1024]{1,0:T(8,128)(2,1)S(1)}, u32[]{:S(2)}, u32[]{:S(2)}) %collective-permute-start.15) | collective-permute-done | bytes 81952 | tf_op jit(solution)/shard_map/cond/branch_0_fun/ppermute | solution.py:381
  109.9 1.8 %collective-permute-done.14.refs_6_ = bf16[40,1024]{1,0:T(8,128)(2,1)S(1)} collective-permute-done((bf16[40,1024]{1,0:T(8,128)(2,1)S(1)}, bf16[40,1024]{1,0:T(8,128)(2,1)S(1)}, u32[]{:S(2)}, u32[]{:S(2)}) %collective-permute-start.14) | collective-permute-done | bytes 81952 | tf_op jit(solution)/shard_map/cond/branch_0_fun/ppermute | solution.py:381
  111.7 1.8 %home_rows.2 = (bf16[128,2048]{1,0:T(8,128)(2,1)}, bf16[1,128]{1,0:T(2,128)(2,1)}) custom-call(s32[1,128]{1,0:T(1,128)S(1)} %get-tuple-element.30.ids_ref, bf16[40,1152]{1,0:T(8,128)(2,1)S(1)} %get-tuple-element.127.refs_0_, bf16[40,1152]{1,0:T(8,128)(2,1)S(1)} %collective-permute-done.7.refs_1_, bf16[40,1152]{1,0:T(8,128)(2,1)S(1)} %collective-permute-done.8.refs_2_, ...), custom_call_target="tpu_custom_call" | custom-call | flops 200000000 | bytes 2000000 | tf_op jit(solution)/shard_map/cond/branch_0_fun/home_rows/pallas_call | solution.py:361
  (55 shorter events, 0.5 us)
Async XLA Ops:
  2.7 10.0 %collective-permute-start.42 = (bf16[40,2176]{1,0:T(8,128)(2,1)S(1)}, bf16[40,2176]{1,0:T(8,128)(2,1)S(1)}, u32[]{:S(2)}, u32[]{:S(2)}) collective-permute-start(bf16[40,2176]{1,0:T(8,128)(2,1)S(1)} %get-tuple-element.149), channel_id=1, source_target_pairs={{0,12},{4,0},{8,4},{12,8},{1,13},{5,1},{9,5},{13,9},{2,14},{6,2},{... | collective-permute-start | bytes 522248 | tf_op jit(solution)/shard_map/ppermute | solution.py:381
  7.8 14.8 %collective-permute-start.41 = (bf16[40,2176]{1,0:T(8,128)(2,1)S(1)}, bf16[40,2176]{1,0:T(8,128)(2,1)S(1)}, u32[]{:S(2)}, u32[]{:S(2)}) collective-permute-start(bf16[40,2176]{1,0:T(8,128)(2,1)S(1)} %get-tuple-element.150), channel_id=1, source_target_pairs={{0,8},{4,12},{8,0},{12,4},{1,9},{5,13},{9,1},{13,5},{2,10},{6,14},... | collective-permute-start | bytes 522248 | tf_op jit(solution)/shard_map/ppermute | solution.py:381
  7.8 14.8 %collective-permute-start.40 = (bf16[40,2176]{1,0:T(8,128)(2,1)S(1)}, bf16[40,2176]{1,0:T(8,128)(2,1)S(1)}, u32[]{:S(2)}, u32[]{:S(2)}) collective-permute-start(bf16[40,2176]{1,0:T(8,128)(2,1)S(1)} %get-tuple-element.151), channel_id=1, source_target_pairs={{0,4},{4,8},{8,12},{12,0},{1,5},{5,9},{9,13},{13,1},{2,6},{6,10},{... | collective-permute-start | bytes 522248 | tf_op jit(solution)/shard_map/ppermute | solution.py:381
  22.6 21.0 %copy-start.2 = (s32[128,1]{0,1:T(1,128)S(1)}, s32[128,1]{0,1:T(1,128)}, u32[]{:S(2)}) copy-start(s32[128,1]{0,1:T(1,128)} %param.12) | copy-start | bytes 1540
  22.7 21.0 %copy-start.3 = (bf16[128,2048]{1,0:T(8,128)(2,1)S(1)}, bf16[128,2048]{1,0:T(8,128)(2,1)}, u32[]{:S(2)}) copy-start(bf16[128,2048]{1,0:T(8,128)(2,1)} %tok_ref.1) | copy-start | bytes 1572868
  22.7 21.0 %copy-start.4 = (bf16[128,2048]{1,0:T(8,128)(2,1)S(1)}, bf16[128,2048]{1,0:T(8,128)(2,1)}, u32[]{:S(2)}) copy-start(bf16[128,2048]{1,0:T(8,128)(2,1)} %cot_ref.1) | copy-start | bytes 1572868
  22.7 21.0 %copy-start.5 = (bf16[128,1]{0,1:T(2,128)(2,1)S(1)}, bf16[128,1]{0,1:T(2,128)(2,1)}, u32[]{:S(2)}) copy-start(bf16[128,1]{0,1:T(2,128)(2,1)} %param.11) | copy-start | bytes 772
  22.7 6.6 %collective-permute-start.47 = (bf16[160,2176]{1,0:T(8,128)(2,1)S(1)}, bf16[160,2176]{1,0:T(8,128)(2,1)S(1)}, u32[]{:S(2)}, u32[]{:S(2)}) collective-permute-start(bf16[160,2176]{1,0:T(8,128)(2,1)S(1)} %pad_maximum_fusion.2), channel_id=1, source_target_pairs={{0,1},{1,0},{2,3},{3,2},{4,5},{5,4},{6,7},{7,6},{8,9},{9,8},{10,11... | collective-permute-start | bytes 2088968 | tf_op jit(solution)/shard_map/ppermute | solution.py:386
  22.8 19.6 %collective-permute-start.43 = (bf16[160,2176]{1,0:T(8,128)(2,1)S(1)}, bf16[160,2176]{1,0:T(8,128)(2,1)S(1)}, u32[]{:S(2)}, u32[]{:S(2)}) collective-permute-start(bf16[160,2176]{1,0:T(8,128)(2,1)S(1)} %pad_maximum_fusion.2), channel_id=1, source_target_pairs={{0,2},{1,3},{2,0},{3,1},{4,6},{5,7},{6,4},{7,5},{8,10},{9,11},{10,... | collective-permute-start | bytes 2088968 | tf_op jit(solution)/shard_map/ppermute | solution.py:386
  24.4 10.3 %collective-permute-start.46 = (bf16[40,2048]{1,0:T(8,128)(2,1)S(1)}, bf16[40,2048]{1,0:T(8,128)(2,1)S(1)}, u32[]{:S(2)}, u32[]{:S(2)}) collective-permute-start(bf16[40,2048]{1,0:T(8,128)(2,1)S(1)} %get-tuple-element.153), channel_id=1, source_target_pairs={{0,12},{4,0},{8,4},{12,8},{1,13},{5,1},{9,5},{13,9},{2,14},{6,2},{... | collective-permute-start | bytes 491528 | tf_op jit(solution)/shard_map/ppermute | solution.py:381
  25.3 17.0 %collective-permute-start.45 = (bf16[40,2048]{1,0:T(8,128)(2,1)S(1)}, bf16[40,2048]{1,0:T(8,128)(2,1)S(1)}, u32[]{:S(2)}, u32[]{:S(2)}) collective-permute-start(bf16[40,2048]{1,0:T(8,128)(2,1)S(1)} %get-tuple-element.154), channel_id=1, source_target_pairs={{0,8},{4,12},{8,0},{12,4},{1,9},{5,13},{9,1},{13,5},{2,10},{6,14},... | collective-permute-start | bytes 491528 | tf_op jit(solution)/shard_map/ppermute | solution.py:381
  27.3 15.0 %collective-permute-start.44 = (bf16[40,2048]{1,0:T(8,128)(2,1)S(1)}, bf16[40,2048]{1,0:T(8,128)(2,1)S(1)}, u32[]{:S(2)}, u32[]{:S(2)}) collective-permute-start(bf16[40,2048]{1,0:T(8,128)(2,1)S(1)} %get-tuple-element.155), channel_id=1, source_target_pairs={{0,4},{4,8},{8,12},{12,0},{1,5},{5,9},{9,13},{13,1},{2,6},{6,10},{... | collective-permute-start | bytes 491528 | tf_op jit(solution)/shard_map/ppermute | solution.py:381
  29.3 3.7 %collective-permute-start.48 = (f32[8,128]{1,0:T(8,128)S(1)}, f32[8,128]{1,0:T(8,128)S(1)}, u32[]{:S(2)}, u32[]{:S(2)}) collective-permute-start(f32[8,128]{1,0:T(8,128)S(1)} %broadcast_in_dim.2), channel_id=1, source_target_pairs={{0,16},{16,0},{1,17},{17,1},{2,18},{18,2},{3,19},{19,3},{4,20},{20... | collective-permute-start | bytes 12296 | tf_op jit(solution)/shard_map/ppermute | solution.py:381
  33.0 1.2 %collective-permute-start.49 = (f32[8,128]{1,0:T(8,128)S(1)}, f32[8,128]{1,0:T(8,128)S(1)}, u32[]{:S(2)}, u32[]{:S(2)}) collective-permute-start(f32[8,128]{1,0:T(8,128)S(1)} %max.9), channel_id=1, source_target_pairs={{0,1},{1,0},{2,3},{3,2},{4,5},{5,4},{6,7},{7,6},{8,9},{9,8},{10,11... | collective-permute-start | bytes 12296 | tf_op jit(solution)/shard_map/ppermute | solution.py:386
  34.2 8.2 %collective-permute-start.50 = (f32[8,128]{1,0:T(8,128)S(1)}, f32[8,128]{1,0:T(8,128)S(1)}, u32[]{:S(2)}, u32[]{:S(2)}) collective-permute-start(f32[8,128]{1,0:T(8,128)S(1)} %max.10), channel_id=1, source_target_pairs={{0,2},{1,3},{2,0},{3,1},{4,6},{5,7},{6,4},{7,5},{8,10},{9,11},{10,... | collective-permute-start | bytes 12296 | tf_op jit(solution)/shard_map/ppermute | solution.py:386
  43.7 2.2 %collective-permute-start = (bf16[160,2176]{1,0:T(8,128)(2,1)S(1)}, bf16[160,2176]{1,0:T(8,128)(2,1)S(1)}, u32[]{:S(2)}, u32[]{:S(2)}) collective-permute-start(bf16[160,2176]{1,0:T(8,128)(2,1)S(1)} %get-tuple-element.33.refs_2_), channel_id=1, source_target_pairs={{0,1},{1,0},{2,3},{3,2},{4,5},{5,4},{6,7},{7,6},{8,9},{9,8},{10,11... | collective-permute-start | bytes 2088968 | tf_op jit(solution)/shard_map/cond/branch_0_fun/ppermute | solution.py:386
  43.8 17.5 %collective-permute-start.2 = (bf16[160,2048]{1,0:T(8,128)(2,1)S(1)}, bf16[160,2048]{1,0:T(8,128)(2,1)S(1)}, u32[]{:S(2)}, u32[]{:S(2)}) collective-permute-start(bf16[160,2048]{1,0:T(8,128)(2,1)S(1)} %get-tuple-element.34.refs_4_), channel_id=1, source_target_pairs={{0,2},{1,3},{2,0},{3,1},{4,6},{5,7},{6,4},{7,5},{8,10},{9,11},{10,... | collective-permute-start | bytes 1966088 | tf_op jit(solution)/shard_map/cond/branch_0_fun/ppermute | solution.py:386
  44.3 17.1 %collective-permute-start.1 = (bf16[160,2048]{1,0:T(8,128)(2,1)S(1)}, bf16[160,2048]{1,0:T(8,128)(2,1)S(1)}, u32[]{:S(2)}, u32[]{:S(2)}) collective-permute-start(bf16[160,2048]{1,0:T(8,128)(2,1)S(1)} %get-tuple-element.34.refs_4_), channel_id=1, source_target_pairs={{0,1},{1,0},{2,3},{3,2},{4,5},{5,4},{6,7},{7,6},{8,9},{9,8},{10,11... | collective-permute-start | bytes 1966088 | tf_op jit(solution)/shard_map/cond/branch_0_fun/ppermute | solution.py:386
  45.9 27.2 %slice-start = ((s8[12582912]{0:T(1024)(128)(4,1)}), s8[4194304]{0:T(1024)(128)(4,1)S(1)}, s32[]{:S(2)}) async-start(s8[12582912]{0:T(1024)(128)(4,1)} %bitcast.9), calls=%async_computation | async-start | bytes 8388608 | tf_op jit(solution)/shard_map/cond
  45.9 27.2 %slice-start.1 = ((s8[12582912]{0:T(1024)(128)(4,1)}), s8[4194304]{0:T(1024)(128)(4,1)S(1)}, s32[]{:S(2)}) async-start(s8[12582912]{0:T(1024)(128)(4,1)} %bitcast.9), calls=%async_computation.1 | async-start | bytes 8388608 | tf_op jit(solution)/shard_map/cond
  45.9 27.2 %slice-start.6 = ((s8[12582912]{0:T(1024)(128)(4,1)}), s8[4194304]{0:T(1024)(128)(4,1)S(1)}, s32[]{:S(2)}) async-start(s8[12582912]{0:T(1024)(128)(4,1)} %bitcast.15), calls=%async_computation.6 | async-start | bytes 8388608 | tf_op jit(solution)/shard_map/cond
  45.9 27.2 %slice-start.7 = ((s8[12582912]{0:T(1024)(128)(4,1)}), s8[4194304]{0:T(1024)(128)(4,1)S(1)}, s32[]{:S(2)}) async-start(s8[12582912]{0:T(1024)(128)(4,1)} %bitcast.15), calls=%async_computation.7 | async-start | bytes 8388608 | tf_op jit(solution)/shard_map/cond
  61.2 2.2 %collective-permute-start.3 = (bf16[160,2048]{1,0:T(8,128)(2,1)S(1)}, bf16[160,2048]{1,0:T(8,128)(2,1)S(1)}, u32[]{:S(2)}, u32[]{:S(2)}) collective-permute-start(bf16[160,2048]{1,0:T(8,128)(2,1)S(1)} %collective-permute-done.2.refs_6_), channel_id=1, source_target_pairs={{0,1},{1,0},{2,3},{3,2},{4,5},{5,4},{6,7},{7,6},{8,9},{9,8},{10,11... | collective-permute-start | bytes 1966088 | tf_op jit(solution)/shard_map/cond/branch_0_fun/ppermute | solution.py:386
  63.4 9.7 %slice-start.2 = ((s8[12582912]{0:T(1024)(128)(4,1)}), s8[4194304]{0:T(1024)(128)(4,1)S(1)}, s32[]{:S(2)}) async-start(s8[12582912]{0:T(1024)(128)(4,1)} %bitcast.9), calls=%async_computation.2 | async-start | bytes 8388608 | tf_op jit(solution)/shard_map/cond
  63.4 9.7 %slice-start.8 = ((s8[12582912]{0:T(1024)(128)(4,1)}), s8[4194304]{0:T(1024)(128)(4,1)S(1)}, s32[]{:S(2)}) async-start(s8[12582912]{0:T(1024)(128)(4,1)} %bitcast.15), calls=%async_computation.8 | async-start | bytes 8388608 | tf_op jit(solution)/shard_map/cond
  77.9 1.8 %collective-permute-start.5 = (bf16[160,1152]{1,0:T(8,128)(2,1)S(1)}, bf16[160,1152]{1,0:T(8,128)(2,1)S(1)}, u32[]{:S(2)}, u32[]{:S(2)}) collective-permute-start(bf16[160,1152]{1,0:T(8,128)(2,1)S(1)} %get-tuple-element.47), channel_id=1, source_target_pairs={{0,1},{1,0},{2,3},{3,2},{4,5},{5,4},{6,7},{7,6},{8,9},{9,8},{10,11... | collective-permute-start | bytes 1105928 | tf_op jit(solution)/shard_map/cond/branch_0_fun/ppermute | solution.py:386
  79.7 10.7 %collective-permute-start.6 = (bf16[160,1152]{1,0:T(8,128)(2,1)S(1)}, bf16[160,1152]{1,0:T(8,128)(2,1)S(1)}, u32[]{:S(2)}, u32[]{:S(2)}) collective-permute-start(bf16[160,1152]{1,0:T(8,128)(2,1)S(1)} %add_convert_fusion.1), channel_id=1, source_target_pairs={{0,2},{1,3},{2,0},{3,1},{4,6},{5,7},{6,4},{7,5},{8,10},{9,11},{10,... | collective-permute-start | bytes 1105928 | tf_op jit(solution)/shard_map/cond/branch_0_fun/ppermute | solution.py:386
  80.3 10.6 %collective-permute-start.4 = (bf16[160,1152]{1,0:T(8,128)(2,1)S(1)}, bf16[160,1152]{1,0:T(8,128)(2,1)S(1)}, u32[]{:S(2)}, u32[]{:S(2)}) collective-permute-start(bf16[160,1152]{1,0:T(8,128)(2,1)S(1)} %get-tuple-element.45), channel_id=1, source_target_pairs={{0,1},{1,0},{2,3},{3,2},{4,5},{5,4},{6,7},{7,6},{8,9},{9,8},{10,11... | collective-permute-start | bytes 1105928 | tf_op jit(solution)/shard_map/cond/branch_0_fun/ppermute | solution.py:386
  90.4 12.0 %collective-permute-start.10 = (bf16[160,1024]{1,0:T(8,128)(2,1)S(1)}, bf16[160,1024]{1,0:T(8,128)(2,1)S(1)}, u32[]{:S(2)}, u32[]{:S(2)}) collective-permute-start(bf16[160,1024]{1,0:T(8,128)(2,1)S(1)} %get-tuple-element.58), channel_id=1, source_target_pairs={{0,1},{1,0},{2,3},{3,2},{4,5},{5,4},{6,7},{7,6},{8,9},{9,8},{10,11... | collective-permute-start | bytes 983048 | tf_op jit(solution)/shard_map/cond/branch_0_fun/ppermute | solution.py:386
  90.4 2.1 %collective-permute-start.11 = (bf16[160,1024]{1,0:T(8,128)(2,1)S(1)}, bf16[160,1024]{1,0:T(8,128)(2,1)S(1)}, u32[]{:S(2)}, u32[]{:S(2)}) collective-permute-start(bf16[160,1024]{1,0:T(8,128)(2,1)S(1)} %get-tuple-element.60), channel_id=1, source_target_pairs={{0,1},{1,0},{2,3},{3,2},{4,5},{5,4},{6,7},{7,6},{8,9},{9,8},{10,11... | collective-permute-start | bytes 983048 | tf_op jit(solution)/shard_map/cond/branch_0_fun/ppermute | solution.py:386
  92.6 9.8 %collective-permute-start.12 = (bf16[160,1024]{1,0:T(8,128)(2,1)S(1)}, bf16[160,1024]{1,0:T(8,128)(2,1)S(1)}, u32[]{:S(2)}, u32[]{:S(2)}) collective-permute-start(bf16[160,1024]{1,0:T(8,128)(2,1)S(1)} %add_convert_fusion.4), channel_id=1, source_target_pairs={{0,2},{1,3},{2,0},{3,1},{4,6},{5,7},{6,4},{7,5},{8,10},{9,11},{10,... | collective-permute-start | bytes 983048 | tf_op jit(solution)/shard_map/cond/branch_0_fun/ppermute | solution.py:386
  93.3 10.8 %collective-permute-start.9 = (bf16[40,1152]{1,0:T(8,128)(2,1)S(1)}, bf16[40,1152]{1,0:T(8,128)(2,1)S(1)}, u32[]{:S(2)}, u32[]{:S(2)}) collective-permute-start(bf16[40,1152]{1,0:T(8,128)(2,1)S(1)} %get-tuple-element.124), channel_id=1, source_target_pairs={{0,4},{4,8},{8,12},{12,0},{1,5},{5,9},{9,13},{13,1},{2,6},{6,10},{... | collective-permute-start | bytes 276488 | tf_op jit(solution)/shard_map/cond/branch_0_fun/ppermute | solution.py:381
  93.7 13.3 %collective-permute-start.8 = (bf16[40,1152]{1,0:T(8,128)(2,1)S(1)}, bf16[40,1152]{1,0:T(8,128)(2,1)S(1)}, u32[]{:S(2)}, u32[]{:S(2)}) collective-permute-start(bf16[40,1152]{1,0:T(8,128)(2,1)S(1)} %get-tuple-element.125), channel_id=1, source_target_pairs={{0,8},{4,12},{8,0},{12,4},{1,9},{5,13},{9,1},{13,5},{2,10},{6,14},... | collective-permute-start | bytes 276488 | tf_op jit(solution)/shard_map/cond/branch_0_fun/ppermute | solution.py:381
  95.7 11.3 %collective-permute-start.7 = (bf16[40,1152]{1,0:T(8,128)(2,1)S(1)}, bf16[40,1152]{1,0:T(8,128)(2,1)S(1)}, u32[]{:S(2)}, u32[]{:S(2)}) collective-permute-start(bf16[40,1152]{1,0:T(8,128)(2,1)S(1)} %get-tuple-element.126), channel_id=1, source_target_pairs={{0,12},{4,0},{8,4},{12,8},{1,13},{5,1},{9,5},{13,9},{2,14},{6,2},{... | collective-permute-start | bytes 276488 | tf_op jit(solution)/shard_map/cond/branch_0_fun/ppermute | solution.py:381
  100.6 12.9 %copy-start = (bf16[16,192,2048]{2,1,0:T(8,128)(2,1)}, bf16[16,192,2048]{2,1,0:T(8,128)(2,1)S(1)}, u32[]{:S(2)}) copy-start(bf16[16,192,2048]{2,1,0:T(8,128)(2,1)S(1)} %down_grads.5) | copy-start | bytes 37748740 | tf_op jit(solution)/shard_map/cond
  102.7 7.2 %collective-permute-start.15 = (bf16[40,1024]{1,0:T(8,128)(2,1)S(1)}, bf16[40,1024]{1,0:T(8,128)(2,1)S(1)}, u32[]{:S(2)}, u32[]{:S(2)}) collective-permute-start(bf16[40,1024]{1,0:T(8,128)(2,1)S(1)} %get-tuple-element.128), channel_id=1, source_target_pairs={{0,4},{4,8},{8,12},{12,0},{1,5},{5,9},{9,13},{13,1},{2,6},{6,10},{... | collective-permute-start | bytes 245768 | tf_op jit(solution)/shard_map/cond/branch_0_fun/ppermute | solution.py:381
  102.7 9.0 %collective-permute-start.14 = (bf16[40,1024]{1,0:T(8,128)(2,1)S(1)}, bf16[40,1024]{1,0:T(8,128)(2,1)S(1)}, u32[]{:S(2)}, u32[]{:S(2)}) collective-permute-start(bf16[40,1024]{1,0:T(8,128)(2,1)S(1)} %get-tuple-element.129), channel_id=1, source_target_pairs={{0,8},{4,12},{8,0},{12,4},{1,9},{5,13},{9,1},{13,5},{2,10},{6,14},... | collective-permute-start | bytes 245768 | tf_op jit(solution)/shard_map/cond/branch_0_fun/ppermute | solution.py:381
  104.1 7.6 %collective-permute-start.13 = (bf16[40,1024]{1,0:T(8,128)(2,1)S(1)}, bf16[40,1024]{1,0:T(8,128)(2,1)S(1)}, u32[]{:S(2)}, u32[]{:S(2)}) collective-permute-start(bf16[40,1024]{1,0:T(8,128)(2,1)S(1)} %get-tuple-element.130), channel_id=1, source_target_pairs={{0,12},{4,0},{8,4},{12,8},{1,13},{5,1},{9,5},{13,9},{2,14},{6,2},{... | collective-permute-start | bytes 245768 | tf_op jit(solution)/shard_map/cond/branch_0_fun/ppermute | solution.py:381

commit v5 on v4

--- a/solution.py
+++ b/solution.py
@@ -465,14 +465,17 @@
     dg, du, hw, cs, router = second_layer(x_list, c_list, g, u, down, room, n_shards)
     first = third_layer(x_list, dg, du, gate, up, router, 0, 2, room, n_shards)
     stay_1, go_1 = near_sums(first, n_dp)
-    come_1 = far_hop(go_1, n_dp)
+    cut = go_1.shape[0] // 2
+    come_1 = far_hop(go_1[:cut], n_dp)
+    come_1b = far_hop(go_1[cut:], n_dp)
     dg, du = lax.optimization_barrier((dg, du, go_1))[:2]
     second = third_layer(x_list, dg, du, gate, up, None, 1, 2, room, n_shards)
+    second = after(second, come_1)
+    stay_2, go_2 = near_sums(second, n_dp)
     early = per_device // 2
-    down_grad = down_layer(after(hw, second), cs, 0, early) if early else None
-    second = after(second, (come_1, down_grad))
-    stay_2, go_2 = near_sums(second, n_dp)
-    come_2 = far_hop(go_2, n_dp)
+    down_grad = down_layer(after(hw, go_2), cs, 0, early) if early else None
+    come_2 = far_hop(after(go_2, (come_1b, down_grad)), n_dp)
+    come_1 = jnp.concatenate([come_1, come_1b])
     home_1 = from_shards(add_rows(stay_1, come_1), room, n_shards)
     down_grad = down_layer(after(hw, go_2), cs, early, per_device - early, down_grad)
     rows_2 = add_rows(stay_2, after(come_2, down_grad))

time: 114 us -> 112 us (0.982)
  waiting for transfers between devices: 40.9 us -> 37.5 us
  starting transfers between devices: 27.2 us -> 29.1 us
    ppermute x14 -> x15, waiting for transfers between devices: 12.8 us -> 10.2 us  [swapped(): return lax.ppermute(value, axis, [(i, i ^ bit) for i in range(n)])]
    ppermute x14 -> x15, starting transfers between devices: 5.12 us -> 6.98 us  [swapped(): return lax.ppermute(value, axis, [(i, i ^ bit) for i in range(n)])]
  transfers between devices with their start and end apart: 27 -> 28, of which waited for: 13 -> 13; matrix products, arithmetic and copies ran while one was open for 1% -> 1% of each run, Pallas kernels for 21% -> 21%
where the time goes in v5:
time: 112 us
  Pallas kernels  42 us (38%)
  waiting for transfers between devices  37.5 us (33%)
  starting transfers between devices  29.1 us (26%)
  between operations  1.42 us (1%)
    ppermute x13, waiting for transfers between devices, shifted(): return lax.ppermute(value, axis, [(i, (i + step) % n) for i in range(n)])  27.3 us
    ppermute x13, starting transfers between devices, shifted(): return lax.ppermute(value, axis, [(i, (i + step) % n) for i in range(n)])  22.1 us
    pallas_call x1, Pallas kernels, first_layer(): pl.pallas_call(functools.partial(first_kernel, n_dp, room, n_shards), gri...  15.2 us
    ppermute x15, waiting for transfers between devices, swapped(): return lax.ppermute(value, axis, [(i, i ^ bit) for i in range(n)])  10.2 us
    pallas_call x1, Pallas kernels, second_layer(): pl.pallas_call(functools.partial(second_kernel, n_dp, room, n_shards), gr...  9.59 us
    pallas_call x2, Pallas kernels, third_layer(): pl.pallas_call(functools.partial(third_kernel, n_dp, room, n_shards, rout...  9.35 us
    ppermute x15, starting transfers between devices, swapped(): return lax.ppermute(value, axis, [(i, i ^ bit) for i in range(n)])  6.98 us
    pallas_call x2, Pallas kernels, down_layer(): pl.pallas_call(down_kernel, grid=(count // step,), in_specs=[pl.BlockSpec...  4.04 us
  transfers between devices with their start and end apart: 28, of which 13 were waited for; matrix products, arithmetic and copies ran while one was open for 1% of the time, Pallas kernels for 21%

profile of v5, /device:TPU:0, one launch (start us, length us, event | category | flops | bytes accessed | tf_op | source)
XLA Modules:
  0.0 111.8 jit_solution(4277099393852865571)
XLA Ops:
  0.6 2.0 %pack_rows.3 = (bf16[160,2176]{1,0:T(8,128)(2,1)S(1)}, bf16[160,2048]{1,0:T(8,128)(2,1)S(1)}) custom-call(s32[1,128]{1,0:T(1,128)} %bitcast.17, bf16[128,2048]{1,0:T(8,128)(2,1)} %tok_ref.1, bf16[128,2048]{1,0:T(8,128)(2,1)} %cot_ref.1, bf16[1,128]{1,0:T(2,128)(2,1)} %bitcast.20), custom_call_target="tpu_custom_call" | custom-call | flops 400000000 | bytes 4000000 | tf_op jit(solution)/shard_map/pack_rows/pallas_call | solution.py:104
  2.7 5.1 %collective-permute-start.44 = (bf16[40,2176]{1,0:T(8,128)(2,1)S(1)}, bf16[40,2176]{1,0:T(8,128)(2,1)S(1)}, u32[]{:S(2)}, u32[]{:S(2)}) collective-permute-start(bf16[40,2176]{1,0:T(8,128)(2,1)S(1)} %get-tuple-element.153), channel_id=1, source_target_pairs={{0,12},{4,0},{8,4},{12,8},{1,13},{5,1},{9,5},{13,9},{2,14},{6,2},{... | collective-permute-start | bytes 522248 | tf_op jit(solution)/shard_map/ppermute | solution.py:381
  7.8 1.0 collective-permute-start.42
  8.8 3.9 %collective-permute-done.44 = bf16[40,2176]{1,0:T(8,128)(2,1)S(1)} collective-permute-done((bf16[40,2176]{1,0:T(8,128)(2,1)S(1)}, bf16[40,2176]{1,0:T(8,128)(2,1)S(1)}, u32[]{:S(2)}, u32[]{:S(2)}) %collective-permute-start.44) | collective-permute-done | bytes 174112 | tf_op jit(solution)/shard_map/ppermute | solution.py:381
  12.7 9.9 %collective-permute-done.43 = bf16[40,2176]{1,0:T(8,128)(2,1)S(1)} collective-permute-done((bf16[40,2176]{1,0:T(8,128)(2,1)S(1)}, bf16[40,2176]{1,0:T(8,128)(2,1)S(1)}, u32[]{:S(2)}, u32[]{:S(2)}) %collective-permute-start.43) | collective-permute-done | bytes 174112 | tf_op jit(solution)/shard_map/ppermute | solution.py:381
  22.8 1.6 %collective-permute-start.45 = (bf16[160,2176]{1,0:T(8,128)(2,1)S(1)}, bf16[160,2176]{1,0:T(8,128)(2,1)S(1)}, u32[]{:S(2)}, u32[]{:S(2)}) collective-permute-start(bf16[160,2176]{1,0:T(8,128)(2,1)S(1)} %pad_maximum_fusion.2), channel_id=1, source_target_pairs={{0,2},{1,3},{2,0},{3,1},{4,6},{5,7},{6,4},{7,5},{8,10},{9,11},{10,... | collective-permute-start | bytes 2088968 | tf_op jit(solution)/shard_map/ppermute | solution.py:386
  24.4 0.9 collective-permute-start.48
  25.3 2.0 %collective-permute-start.47 = (bf16[40,2048]{1,0:T(8,128)(2,1)S(1)}, bf16[40,2048]{1,0:T(8,128)(2,1)S(1)}, u32[]{:S(2)}, u32[]{:S(2)}) collective-permute-start(bf16[40,2048]{1,0:T(8,128)(2,1)S(1)} %get-tuple-element.158), channel_id=1, source_target_pairs={{0,8},{4,12},{8,0},{12,4},{1,9},{5,13},{9,1},{13,5},{2,10},{6,14},... | collective-permute-start | bytes 491528 | tf_op jit(solution)/shard_map/ppermute | solution.py:381
  27.3 1.9 %collective-permute-start.46 = (bf16[40,2048]{1,0:T(8,128)(2,1)S(1)}, bf16[40,2048]{1,0:T(8,128)(2,1)S(1)}, u32[]{:S(2)}, u32[]{:S(2)}) collective-permute-start(bf16[40,2048]{1,0:T(8,128)(2,1)S(1)} %get-tuple-element.159), channel_id=1, source_target_pairs={{0,4},{4,8},{8,12},{12,0},{1,5},{5,9},{9,13},{13,1},{2,6},{6,10},{... | collective-permute-start | bytes 491528 | tf_op jit(solution)/shard_map/ppermute | solution.py:381
  29.3 1.6 %collective-permute-start.50 = (f32[8,128]{1,0:T(8,128)S(1)}, f32[8,128]{1,0:T(8,128)S(1)}, u32[]{:S(2)}, u32[]{:S(2)}) collective-permute-start(f32[8,128]{1,0:T(8,128)S(1)} %broadcast_in_dim.2), channel_id=1, source_target_pairs={{0,16},{16,0},{1,17},{17,1},{2,18},{18,2},{3,19},{19,3},{4,20},{20... | collective-permute-start | bytes 12296 | tf_op jit(solution)/shard_map/ppermute | solution.py:381
  30.9 2.1 %collective-permute-done.50 = f32[8,128]{1,0:T(8,128)S(1)} collective-permute-done((f32[8,128]{1,0:T(8,128)S(1)}, f32[8,128]{1,0:T(8,128)S(1)}, u32[]{:S(2)}, u32[]{:S(2)}) %collective-permute-start.50) | collective-permute-done | bytes 4128 | tf_op jit(solution)/shard_map/ppermute | solution.py:381
  33.0 1.2 %collective-permute-done.51 = f32[8,128]{1,0:T(8,128)S(1)} collective-permute-done((f32[8,128]{1,0:T(8,128)S(1)}, f32[8,128]{1,0:T(8,128)S(1)}, u32[]{:S(2)}, u32[]{:S(2)}) %collective-permute-start.51) | collective-permute-done | bytes 4128 | tf_op jit(solution)/shard_map/ppermute | solution.py:386
  34.2 0.5 collective-permute-start.52
  34.7 7.6 %collective-permute-done.47 = bf16[40,2048]{1,0:T(8,128)(2,1)S(1)} collective-permute-done((bf16[40,2048]{1,0:T(8,128)(2,1)S(1)}, bf16[40,2048]{1,0:T(8,128)(2,1)S(1)}, u32[]{:S(2)}, u32[]{:S(2)}) %collective-permute-start.47) | collective-permute-done | bytes 163872 | tf_op jit(solution)/shard_map/ppermute | solution.py:381
  42.4 0.6 slice.123
  43.7 68.1 %conditional.1 = (bf16[128,2048]{1,0:T(8,128)(2,1)}, bf16[128,1]{0,1:T(2,128)(2,1)}, bf16[16,192,2048]{2,1,0:T(8,128)(2,1)}) conditional(s32[]{:T(128)} %bitcast.4, (bf16[160,2176]{1,0:T(8,128)(2,1)S(1)}, bf16[160,2048]{1,0:T(8,128)(2,1)S(1)}, bf16[160,2176]{1,0:T(8,128)(2,1)S(1)}, bf16[160,2176]{1,0:T(8,128)(2,1)S(1)}, ...), branch_computations={%region_1.0_spmd, %region_2.0_spmd} | conditional | flops 7616220160 | bytes 261090816 | solution.py:529
  43.7 0.6 collective-permute-start.2
  44.3 0.2 collective-permute-start.1
  44.5 1.4 %collective-permute-done.refs_3_ = bf16[160,2176]{1,0:T(8,128)(2,1)S(1)} collective-permute-done((bf16[160,2176]{1,0:T(8,128)(2,1)S(1)}, bf16[160,2176]{1,0:T(8,128)(2,1)S(1)}, u32[]{:S(2)}, u32[]{:S(2)}) %collective-permute-start) | collective-permute-done | bytes 696352 | tf_op jit(solution)/shard_map/cond/branch_0_fun/ppermute | solution.py:386
  45.9 15.2 %gate_up.2 = (f32[16,64,192]{2,1,0:T(8,128)S(1)}, f32[16,64,192]{2,1,0:T(8,128)S(1)}) custom-call(bf16[160,2176]{1,0:T(8,128)(2,1)S(1)} %get-tuple-element.31.refs_0_, bf16[160,2176]{1,0:T(8,128)(2,1)S(1)} %get-tuple-element.32.refs_1_, bf16[160,2176]{1,0:T(8,128)(2,1)S(1)} %get-tuple-element.33.refs_2_, bf16[160,2176]{1,0:T(8,128)(2,1)S(1)} %collective-permute-done.refs_3_, ...), custom_call_target="tpu_custom_call" | custom-call | flops 2000000000 | bytes 30000000 | tf_op jit(solution)/shard_map/cond/branch_0_fun/gate_up/pallas_call | solution.py:172
  61.1 0.2 collective-permute-start.3
  61.3 2.0 %collective-permute-done.3.refs_7_ = bf16[160,2048]{1,0:T(8,128)(2,1)S(1)} collective-permute-done((bf16[160,2048]{1,0:T(8,128)(2,1)S(1)}, bf16[160,2048]{1,0:T(8,128)(2,1)S(1)}, u32[]{:S(2)}, u32[]{:S(2)}) %collective-permute-start.3) | collective-permute-done | bytes 655392 | tf_op jit(solution)/shard_map/cond/branch_0_fun/ppermute | solution.py:386
  63.3 9.6 %hidden_grads.2 = (bf16[16,64,192]{2,1,0:T(8,128)(2,1)S(1)}, bf16[16,64,192]{2,1,0:T(8,128)(2,1)S(1)}, bf16[16,64,192]{2,1,0:T(8,128)(2,1)S(1)}, bf16[16,64,2048...) custom-call(bf16[160,2176]{1,0:T(8,128)(2,1)S(1)} %get-tuple-element.31.refs_0_, ...), custom_call_target="tpu_custom_call" | custom-call | flops 2000000000 | bytes 20000000 | tf_op jit(solution)/shard_map/cond/branch_0_fun/hidden_grads/pallas_call | solution.py:228
  73.0 4.7 %input_grads.4 = (bf16[160,1152]{1,0:T(8,128)(2,1)S(1)}, bf16[160,1152]{1,0:T(8,128)(2,1)S(1)}, bf16[160,1152]{1,0:T(8,128)(2,1)S(1)}, bf16[160,1152]{1,0:T(8,128)(2,1)S(1)}) custom-call(bf16[160,2176]{1,0:T(8,128)(2,1)S(1)} %get-tuple-element.31.refs_0_, bf16[160,2176]{1,0:T(8,128)(2,1)S(1)} %get-tuple-element.32.refs_1_, ...), custom_call_target="tpu_custom_call" | custom-call | flops 1000000000 | bytes 15000000 | tf_op jit(solution)/shard_map/cond/branch_0_fun/input_grads/pallas_call | solution.py:299
  77.7 0.2 collective-permute-start.5
  77.9 0.4 collective-permute-start.4
  78.3 1.2 %collective-permute-done.5 = bf16[160,1152]{1,0:T(8,128)(2,1)S(1)} collective-permute-done((bf16[160,1152]{1,0:T(8,128)(2,1)S(1)}, bf16[160,1152]{1,0:T(8,128)(2,1)S(1)}, u32[]{:S(2)}, u32[]{:S(2)}) %collective-permute-start.5) | collective-permute-done | bytes 368672 | tf_op jit(solution)/shard_map/cond/branch_0_fun/ppermute | solution.py:386
  79.6 0.6 collective-permute-start.6
  80.2 1.5 %collective-permute-start.7 = (bf16[80,1152]{1,0:T(8,128)(2,1)S(1)}, bf16[80,1152]{1,0:T(8,128)(2,1)S(1)}, u32[]{:S(2)}, u32[]{:S(2)}) collective-permute-start(bf16[80,1152]{1,0:T(8,128)(2,1)S(1)} %get-tuple-element.129), channel_id=1, source_target_pairs={{0,2},{1,3},{2,0},{3,1},{4,6},{5,7},{6,4},{7,5},{8,10},{9,11},{10,... | collective-permute-start | bytes 552968 | tf_op jit(solution)/shard_map/cond/branch_0_fun/ppermute | solution.py:386
  81.7 4.6 %input_grads.5 = (bf16[160,1024]{1,0:T(8,128)(2,1)S(1)}, bf16[160,1024]{1,0:T(8,128)(2,1)S(1)}, bf16[160,1024]{1,0:T(8,128)(2,1)S(1)}, bf16[160,1024]{1,0:T(8,128)(2,1)S(1)}) custom-call(bf16[160,2176]{1,0:T(8,128)(2,1)S(1)} %get-tuple-element.31.refs_0_, bf16[160,2176]{1,0:T(8,128)(2,1)S(1)} %get-tuple-element.32.refs_1_, ...), custom_call_target="tpu_custom_call" | custom-call | flops 1000000000 | bytes 15000000 | tf_op jit(solution)/shard_map/cond/branch_0_fun/input_grads/pallas_call | solution.py:299
  86.3 0.8 collective-permute-done.6
  87.2 0.5 collective-permute-start.12
  87.7 2.6 %collective-permute-done.7 = bf16[80,1152]{1,0:T(8,128)(2,1)S(1)} collective-permute-done((bf16[80,1152]{1,0:T(8,128)(2,1)S(1)}, bf16[80,1152]{1,0:T(8,128)(2,1)S(1)}, u32[]{:S(2)}, u32[]{:S(2)}) %collective-permute-start.7) | collective-permute-done | bytes 184352 | tf_op jit(solution)/shard_map/cond/branch_0_fun/ppermute | solution.py:386
  90.3 0.1 add_convert_fusion
  90.5 0.1 add_convert_fusion.4
  90.6 2.0 %down_grads.4.refs_2_ = bf16[16,192,2048]{2,1,0:T(8,128)(2,1)S(1)} custom-call(bf16[16,64,192]{2,1,0:T(8,128)(2,1)S(1)} %get-tuple-element.59.refs_0_, bf16[16,64,2048]{2,1,0:T(8,128)(2,1)S(1)} %get-tuple-element.60.refs_1_), custom_call_target="tpu_custom_call" | custom-call | flops 500000000 | bytes 9000000 | tf_op jit(solution)/shard_map/cond/branch_0_fun/down_grads/pallas_call | solution.py:324
  92.6 0.6 collective-permute-start.13
  93.2 0.4 collective-permute-start.10
  93.6 2.0 %collective-permute-start.9 = (bf16[40,1152]{1,0:T(8,128)(2,1)S(1)}, bf16[40,1152]{1,0:T(8,128)(2,1)S(1)}, u32[]{:S(2)}, u32[]{:S(2)}) collective-permute-start(bf16[40,1152]{1,0:T(8,128)(2,1)S(1)} %get-tuple-element.125), channel_id=1, source_target_pairs={{0,8},{4,12},{8,0},{12,4},{1,9},{5,13},{9,1},{13,5},{2,10},{6,14},... | collective-permute-start | bytes 276488 | tf_op jit(solution)/shard_map/cond/branch_0_fun/ppermute | solution.py:381
  95.7 2.8 %collective-permute-start.8 = (bf16[40,1152]{1,0:T(8,128)(2,1)S(1)}, bf16[40,1152]{1,0:T(8,128)(2,1)S(1)}, u32[]{:S(2)}, u32[]{:S(2)}) collective-permute-start(bf16[40,1152]{1,0:T(8,128)(2,1)S(1)} %get-tuple-element.126), channel_id=1, source_target_pairs={{0,12},{4,0},{8,4},{12,8},{1,13},{5,1},{9,5},{13,9},{2,14},{6,2},{... | collective-permute-start | bytes 276488 | tf_op jit(solution)/shard_map/cond/branch_0_fun/ppermute | solution.py:381
  98.5 2.0 %down_grads.5 = bf16[16,192,2048]{2,1,0:T(8,128)(2,1)S(1)} custom-call(bf16[16,64,192]{2,1,0:T(8,128)(2,1)S(1)} %get-tuple-element.59.refs_0_, bf16[16,64,2048]{2,1,0:T(8,128)(2,1)S(1)} %get-tuple-element.60.refs_1_, bf16[16,192,2048]{2,1,0:T(8,128)(2,1)S(1)} %down_grads.4.refs_2_), custom_call_target="tpu_custom_call", output_to_operand_aliasing={{}: (2, {})} | custom-call | flops 500000000 | bytes 9000000 | tf_op jit(solution)/shard_map/cond/branch_0_fun/down_grads/pallas_call | solution.py:324
  100.5 1.1 collective-permute-done.13
  101.6 0.2 add_convert_fusion.3
  101.9 1.4 %collective-permute-start.15 = (bf16[40,1024]{1,0:T(8,128)(2,1)S(1)}, bf16[40,1024]{1,0:T(8,128)(2,1)S(1)}, u32[]{:S(2)}, u32[]{:S(2)}) collective-permute-start(bf16[40,1024]{1,0:T(8,128)(2,1)S(1)} %get-tuple-element.131), channel_id=1, source_target_pairs={{0,8},{4,12},{8,0},{12,4},{1,9},{5,13},{9,1},{13,5},{2,10},{6,14},... | collective-permute-start | bytes 245768 | tf_op jit(solution)/shard_map/cond/branch_0_fun/ppermute | solution.py:381
  103.3 2.8 %collective-permute-start.14 = (bf16[40,1024]{1,0:T(8,128)(2,1)S(1)}, bf16[40,1024]{1,0:T(8,128)(2,1)S(1)}, u32[]{:S(2)}, u32[]{:S(2)}) collective-permute-start(bf16[40,1024]{1,0:T(8,128)(2,1)S(1)} %get-tuple-element.132), channel_id=1, source_target_pairs={{0,12},{4,0},{8,4},{12,8},{1,13},{5,1},{9,5},{13,9},{2,14},{6,2},{... | collective-permute-start | bytes 245768 | tf_op jit(solution)/shard_map/cond/branch_0_fun/ppermute | solution.py:381
  106.1 2.2 %collective-permute-done.16.refs_7_ = bf16[40,1024]{1,0:T(8,128)(2,1)S(1)} collective-permute-done((bf16[40,1024]{1,0:T(8,128)(2,1)S(1)}, bf16[40,1024]{1,0:T(8,128)(2,1)S(1)}, u32[]{:S(2)}, u32[]{:S(2)}) %collective-permute-start.16) | collective-permute-done | bytes 81952 | tf_op jit(solution)/shard_map/cond/branch_0_fun/ppermute | solution.py:381
  108.3 1.7 %collective-permute-done.15.refs_6_ = bf16[40,1024]{1,0:T(8,128)(2,1)S(1)} collective-permute-done((bf16[40,1024]{1,0:T(8,128)(2,1)S(1)}, bf16[40,1024]{1,0:T(8,128)(2,1)S(1)}, u32[]{:S(2)}, u32[]{:S(2)}) %collective-permute-start.15) | collective-permute-done | bytes 81952 | tf_op jit(solution)/shard_map/cond/branch_0_fun/ppermute | solution.py:381
  110.0 1.8 %home_rows.2 = (bf16[128,2048]{1,0:T(8,128)(2,1)}, bf16[1,128]{1,0:T(2,128)(2,1)}) custom-call(s32[1,128]{1,0:T(1,128)S(1)} %get-tuple-element.30.ids_ref, bf16[40,1152]{1,0:T(8,128)(2,1)S(1)} %get-tuple-element.127.refs_0_, bf16[40,1152]{1,0:T(8,128)(2,1)S(1)} %collective-permute-done.8.refs_1_, bf16[40,1152]{1,0:T(8,128)(2,1)S(1)} %collective-permute-done.9.refs_2_, ...), custom_call_target="tpu_custom_call" | custom-call | flops 200000000 | bytes 2000000 | tf_op jit(solution)/shard_map/cond/branch_0_fun/home_rows/pallas_call | solution.py:361
  (58 shorter events, 0.7 us)
Async XLA Ops:
  2.7 10.0 %collective-permute-start.44 = (bf16[40,2176]{1,0:T(8,128)(2,1)S(1)}, bf16[40,2176]{1,0:T(8,128)(2,1)S(1)}, u32[]{:S(2)}, u32[]{:S(2)}) collective-permute-start(bf16[40,2176]{1,0:T(8,128)(2,1)S(1)} %get-tuple-element.153), channel_id=1, source_target_pairs={{0,12},{4,0},{8,4},{12,8},{1,13},{5,1},{9,5},{13,9},{2,14},{6,2},{... | collective-permute-start | bytes 522248 | tf_op jit(solution)/shard_map/ppermute | solution.py:381
  7.8 14.8 %collective-permute-start.43 = (bf16[40,2176]{1,0:T(8,128)(2,1)S(1)}, bf16[40,2176]{1,0:T(8,128)(2,1)S(1)}, u32[]{:S(2)}, u32[]{:S(2)}) collective-permute-start(bf16[40,2176]{1,0:T(8,128)(2,1)S(1)} %get-tuple-element.154), channel_id=1, source_target_pairs={{0,8},{4,12},{8,0},{12,4},{1,9},{5,13},{9,1},{13,5},{2,10},{6,14},... | collective-permute-start | bytes 522248 | tf_op jit(solution)/shard_map/ppermute | solution.py:381
  7.8 14.8 %collective-permute-start.42 = (bf16[40,2176]{1,0:T(8,128)(2,1)S(1)}, bf16[40,2176]{1,0:T(8,128)(2,1)S(1)}, u32[]{:S(2)}, u32[]{:S(2)}) collective-permute-start(bf16[40,2176]{1,0:T(8,128)(2,1)S(1)} %get-tuple-element.155), channel_id=1, source_target_pairs={{0,4},{4,8},{8,12},{12,0},{1,5},{5,9},{9,13},{13,1},{2,6},{6,10},{... | collective-permute-start | bytes 522248 | tf_op jit(solution)/shard_map/ppermute | solution.py:381
  22.6 21.0 %copy-start.2 = (s32[128,1]{0,1:T(1,128)S(1)}, s32[128,1]{0,1:T(1,128)}, u32[]{:S(2)}) copy-start(s32[128,1]{0,1:T(1,128)} %param.12) | copy-start | bytes 1540
  22.7 21.0 %copy-start.3 = (bf16[128,2048]{1,0:T(8,128)(2,1)S(1)}, bf16[128,2048]{1,0:T(8,128)(2,1)}, u32[]{:S(2)}) copy-start(bf16[128,2048]{1,0:T(8,128)(2,1)} %tok_ref.1) | copy-start | bytes 1572868
  22.7 21.0 %copy-start.4 = (bf16[128,2048]{1,0:T(8,128)(2,1)S(1)}, bf16[128,2048]{1,0:T(8,128)(2,1)}, u32[]{:S(2)}) copy-start(bf16[128,2048]{1,0:T(8,128)(2,1)} %cot_ref.1) | copy-start | bytes 1572868
  22.7 21.0 %copy-start.5 = (bf16[128,1]{0,1:T(2,128)(2,1)S(1)}, bf16[128,1]{0,1:T(2,128)(2,1)}, u32[]{:S(2)}) copy-start(bf16[128,1]{0,1:T(2,128)(2,1)} %param.11) | copy-start | bytes 772
  22.7 6.6 %collective-permute-start.49 = (bf16[160,2176]{1,0:T(8,128)(2,1)S(1)}, bf16[160,2176]{1,0:T(8,128)(2,1)S(1)}, u32[]{:S(2)}, u32[]{:S(2)}) collective-permute-start(bf16[160,2176]{1,0:T(8,128)(2,1)S(1)} %pad_maximum_fusion.2), channel_id=1, source_target_pairs={{0,1},{1,0},{2,3},{3,2},{4,5},{5,4},{6,7},{7,6},{8,9},{9,8},{10,11... | collective-permute-start | bytes 2088968 | tf_op jit(solution)/shard_map/ppermute | solution.py:386
  22.8 19.6 %collective-permute-start.45 = (bf16[160,2176]{1,0:T(8,128)(2,1)S(1)}, bf16[160,2176]{1,0:T(8,128)(2,1)S(1)}, u32[]{:S(2)}, u32[]{:S(2)}) collective-permute-start(bf16[160,2176]{1,0:T(8,128)(2,1)S(1)} %pad_maximum_fusion.2), channel_id=1, source_target_pairs={{0,2},{1,3},{2,0},{3,1},{4,6},{5,7},{6,4},{7,5},{8,10},{9,11},{10,... | collective-permute-start | bytes 2088968 | tf_op jit(solution)/shard_map/ppermute | solution.py:386
  24.4 10.3 %collective-permute-start.48 = (bf16[40,2048]{1,0:T(8,128)(2,1)S(1)}, bf16[40,2048]{1,0:T(8,128)(2,1)S(1)}, u32[]{:S(2)}, u32[]{:S(2)}) collective-permute-start(bf16[40,2048]{1,0:T(8,128)(2,1)S(1)} %get-tuple-element.157), channel_id=1, source_target_pairs={{0,12},{4,0},{8,4},{12,8},{1,13},{5,1},{9,5},{13,9},{2,14},{6,2},{... | collective-permute-start | bytes 491528 | tf_op jit(solution)/shard_map/ppermute | solution.py:381
  25.3 17.0 %collective-permute-start.47 = (bf16[40,2048]{1,0:T(8,128)(2,1)S(1)}, bf16[40,2048]{1,0:T(8,128)(2,1)S(1)}, u32[]{:S(2)}, u32[]{:S(2)}) collective-permute-start(bf16[40,2048]{1,0:T(8,128)(2,1)S(1)} %get-tuple-element.158), channel_id=1, source_target_pairs={{0,8},{4,12},{8,0},{12,4},{1,9},{5,13},{9,1},{13,5},{2,10},{6,14},... | collective-permute-start | bytes 491528 | tf_op jit(solution)/shard_map/ppermute | solution.py:381
  27.3 15.0 %collective-permute-start.46 = (bf16[40,2048]{1,0:T(8,128)(2,1)S(1)}, bf16[40,2048]{1,0:T(8,128)(2,1)S(1)}, u32[]{:S(2)}, u32[]{:S(2)}) collective-permute-start(bf16[40,2048]{1,0:T(8,128)(2,1)S(1)} %get-tuple-element.159), channel_id=1, source_target_pairs={{0,4},{4,8},{8,12},{12,0},{1,5},{5,9},{9,13},{13,1},{2,6},{6,10},{... | collective-permute-start | bytes 491528 | tf_op jit(solution)/shard_map/ppermute | solution.py:381
  29.3 3.7 %collective-permute-start.50 = (f32[8,128]{1,0:T(8,128)S(1)}, f32[8,128]{1,0:T(8,128)S(1)}, u32[]{:S(2)}, u32[]{:S(2)}) collective-permute-start(f32[8,128]{1,0:T(8,128)S(1)} %broadcast_in_dim.2), channel_id=1, source_target_pairs={{0,16},{16,0},{1,17},{17,1},{2,18},{18,2},{3,19},{19,3},{4,20},{20... | collective-permute-start | bytes 12296 | tf_op jit(solution)/shard_map/ppermute | solution.py:381
  33.0 1.2 %collective-permute-start.51 = (f32[8,128]{1,0:T(8,128)S(1)}, f32[8,128]{1,0:T(8,128)S(1)}, u32[]{:S(2)}, u32[]{:S(2)}) collective-permute-start(f32[8,128]{1,0:T(8,128)S(1)} %max.9), channel_id=1, source_target_pairs={{0,1},{1,0},{2,3},{3,2},{4,5},{5,4},{6,7},{7,6},{8,9},{9,8},{10,11... | collective-permute-start | bytes 12296 | tf_op jit(solution)/shard_map/ppermute | solution.py:386
  34.2 8.2 %collective-permute-start.52 = (f32[8,128]{1,0:T(8,128)S(1)}, f32[8,128]{1,0:T(8,128)S(1)}, u32[]{:S(2)}, u32[]{:S(2)}) collective-permute-start(f32[8,128]{1,0:T(8,128)S(1)} %max.10), channel_id=1, source_target_pairs={{0,2},{1,3},{2,0},{3,1},{4,6},{5,7},{6,4},{7,5},{8,10},{9,11},{10,... | collective-permute-start | bytes 12296 | tf_op jit(solution)/shard_map/ppermute | solution.py:386
  43.7 2.2 %collective-permute-start = (bf16[160,2176]{1,0:T(8,128)(2,1)S(1)}, bf16[160,2176]{1,0:T(8,128)(2,1)S(1)}, u32[]{:S(2)}, u32[]{:S(2)}) collective-permute-start(bf16[160,2176]{1,0:T(8,128)(2,1)S(1)} %get-tuple-element.33.refs_2_), channel_id=1, source_target_pairs={{0,1},{1,0},{2,3},{3,2},{4,5},{5,4},{6,7},{7,6},{8,9},{9,8},{10,11... | collective-permute-start | bytes 2088968 | tf_op jit(solution)/shard_map/cond/branch_0_fun/ppermute | solution.py:386
  43.7 17.4 %collective-permute-start.2 = (bf16[160,2048]{1,0:T(8,128)(2,1)S(1)}, bf16[160,2048]{1,0:T(8,128)(2,1)S(1)}, u32[]{:S(2)}, u32[]{:S(2)}) collective-permute-start(bf16[160,2048]{1,0:T(8,128)(2,1)S(1)} %get-tuple-element.34.refs_4_), channel_id=1, source_target_pairs={{0,2},{1,3},{2,0},{3,1},{4,6},{5,7},{6,4},{7,5},{8,10},{9,11},{10,... | collective-permute-start | bytes 1966088 | tf_op jit(solution)/shard_map/cond/branch_0_fun/ppermute | solution.py:386
  44.3 17.0 %collective-permute-start.1 = (bf16[160,2048]{1,0:T(8,128)(2,1)S(1)}, bf16[160,2048]{1,0:T(8,128)(2,1)S(1)}, u32[]{:S(2)}, u32[]{:S(2)}) collective-permute-start(bf16[160,2048]{1,0:T(8,128)(2,1)S(1)} %get-tuple-element.34.refs_4_), channel_id=1, source_target_pairs={{0,1},{1,0},{2,3},{3,2},{4,5},{5,4},{6,7},{7,6},{8,9},{9,8},{10,11... | collective-permute-start | bytes 1966088 | tf_op jit(solution)/shard_map/cond/branch_0_fun/ppermute | solution.py:386
  45.9 27.0 %slice-start = ((s8[12582912]{0:T(1024)(128)(4,1)}), s8[4194304]{0:T(1024)(128)(4,1)S(1)}, s32[]{:S(2)}) async-start(s8[12582912]{0:T(1024)(128)(4,1)} %bitcast.9), calls=%async_computation | async-start | bytes 8388608 | tf_op jit(solution)/shard_map/cond
  45.9 27.0 %slice-start.1 = ((s8[12582912]{0:T(1024)(128)(4,1)}), s8[4194304]{0:T(1024)(128)(4,1)S(1)}, s32[]{:S(2)}) async-start(s8[12582912]{0:T(1024)(128)(4,1)} %bitcast.9), calls=%async_computation.1 | async-start | bytes 8388608 | tf_op jit(solution)/shard_map/cond
  45.9 27.0 %slice-start.6 = ((s8[12582912]{0:T(1024)(128)(4,1)}), s8[4194304]{0:T(1024)(128)(4,1)S(1)}, s32[]{:S(2)}) async-start(s8[12582912]{0:T(1024)(128)(4,1)} %bitcast.15), calls=%async_computation.6 | async-start | bytes 8388608 | tf_op jit(solution)/shard_map/cond
  45.9 27.1 %slice-start.7 = ((s8[12582912]{0:T(1024)(128)(4,1)}), s8[4194304]{0:T(1024)(128)(4,1)S(1)}, s32[]{:S(2)}) async-start(s8[12582912]{0:T(1024)(128)(4,1)} %bitcast.15), calls=%async_computation.7 | async-start | bytes 8388608 | tf_op jit(solution)/shard_map/cond
  61.1 2.2 %collective-permute-start.3 = (bf16[160,2048]{1,0:T(8,128)(2,1)S(1)}, bf16[160,2048]{1,0:T(8,128)(2,1)S(1)}, u32[]{:S(2)}, u32[]{:S(2)}) collective-permute-start(bf16[160,2048]{1,0:T(8,128)(2,1)S(1)} %collective-permute-done.2.refs_6_), channel_id=1, source_target_pairs={{0,1},{1,0},{2,3},{3,2},{4,5},{5,4},{6,7},{7,6},{8,9},{9,8},{10,11... | collective-permute-start | bytes 1966088 | tf_op jit(solution)/shard_map/cond/branch_0_fun/ppermute | solution.py:386
  63.3 9.6 %slice-start.2 = ((s8[12582912]{0:T(1024)(128)(4,1)}), s8[4194304]{0:T(1024)(128)(4,1)S(1)}, s32[]{:S(2)}) async-start(s8[12582912]{0:T(1024)(128)(4,1)} %bitcast.9), calls=%async_computation.2 | async-start | bytes 8388608 | tf_op jit(solution)/shard_map/cond
  63.3 9.7 %slice-start.8 = ((s8[12582912]{0:T(1024)(128)(4,1)}), s8[4194304]{0:T(1024)(128)(4,1)S(1)}, s32[]{:S(2)}) async-start(s8[12582912]{0:T(1024)(128)(4,1)} %bitcast.15), calls=%async_computation.8 | async-start | bytes 8388608 | tf_op jit(solution)/shard_map/cond
  77.7 1.8 %collective-permute-start.5 = (bf16[160,1152]{1,0:T(8,128)(2,1)S(1)}, bf16[160,1152]{1,0:T(8,128)(2,1)S(1)}, u32[]{:S(2)}, u32[]{:S(2)}) collective-permute-start(bf16[160,1152]{1,0:T(8,128)(2,1)S(1)} %get-tuple-element.47), channel_id=1, source_target_pairs={{0,1},{1,0},{2,3},{3,2},{4,5},{5,4},{6,7},{7,6},{8,9},{9,8},{10,11... | collective-permute-start | bytes 1105928 | tf_op jit(solution)/shard_map/cond/branch_0_fun/ppermute | solution.py:386
  77.9 9.7 %collective-permute-start.4 = (bf16[160,1152]{1,0:T(8,128)(2,1)S(1)}, bf16[160,1152]{1,0:T(8,128)(2,1)S(1)}, u32[]{:S(2)}, u32[]{:S(2)}) collective-permute-start(bf16[160,1152]{1,0:T(8,128)(2,1)S(1)} %get-tuple-element.45), channel_id=1, source_target_pairs={{0,1},{1,0},{2,3},{3,2},{4,5},{5,4},{6,7},{7,6},{8,9},{9,8},{10,11... | collective-permute-start | bytes 1105928 | tf_op jit(solution)/shard_map/cond/branch_0_fun/ppermute | solution.py:386
  79.6 7.5 %collective-permute-start.6 = (bf16[80,1152]{1,0:T(8,128)(2,1)S(1)}, bf16[80,1152]{1,0:T(8,128)(2,1)S(1)}, u32[]{:S(2)}, u32[]{:S(2)}) collective-permute-start(bf16[80,1152]{1,0:T(8,128)(2,1)S(1)} %get-tuple-element.128), channel_id=1, source_target_pairs={{0,2},{1,3},{2,0},{3,1},{4,6},{5,7},{6,4},{7,5},{8,10},{9,11},{10,... | collective-permute-start | bytes 552968 | tf_op jit(solution)/shard_map/cond/branch_0_fun/ppermute | solution.py:386
  80.2 10.1 %collective-permute-start.7 = (bf16[80,1152]{1,0:T(8,128)(2,1)S(1)}, bf16[80,1152]{1,0:T(8,128)(2,1)S(1)}, u32[]{:S(2)}, u32[]{:S(2)}) collective-permute-start(bf16[80,1152]{1,0:T(8,128)(2,1)S(1)} %get-tuple-element.129), channel_id=1, source_target_pairs={{0,2},{1,3},{2,0},{3,1},{4,6},{5,7},{6,4},{7,5},{8,10},{9,11},{10,... | collective-permute-start | bytes 552968 | tf_op jit(solution)/shard_map/cond/branch_0_fun/ppermute | solution.py:386
  87.2 14.4 %collective-permute-start.11 = (bf16[160,1024]{1,0:T(8,128)(2,1)S(1)}, bf16[160,1024]{1,0:T(8,128)(2,1)S(1)}, u32[]{:S(2)}, u32[]{:S(2)}) collective-permute-start(bf16[160,1024]{1,0:T(8,128)(2,1)S(1)} %get-tuple-element.55), channel_id=1, source_target_pairs={{0,1},{1,0},{2,3},{3,2},{4,5},{5,4},{6,7},{7,6},{8,9},{9,8},{10,11... | collective-permute-start | bytes 983048 | tf_op jit(solution)/shard_map/cond/branch_0_fun/ppermute | solution.py:386
  87.2 3.3 %collective-permute-start.12 = (bf16[160,1024]{1,0:T(8,128)(2,1)S(1)}, bf16[160,1024]{1,0:T(8,128)(2,1)S(1)}, u32[]{:S(2)}, u32[]{:S(2)}) collective-permute-start(bf16[160,1024]{1,0:T(8,128)(2,1)S(1)} %get-tuple-element.57), channel_id=1, source_target_pairs={{0,1},{1,0},{2,3},{3,2},{4,5},{5,4},{6,7},{7,6},{8,9},{9,8},{10,11... | collective-permute-start | bytes 983048 | tf_op jit(solution)/shard_map/cond/branch_0_fun/ppermute | solution.py:386
  92.6 9.0 %collective-permute-start.13 = (bf16[160,1024]{1,0:T(8,128)(2,1)S(1)}, bf16[160,1024]{1,0:T(8,128)(2,1)S(1)}, u32[]{:S(2)}, u32[]{:S(2)}) collective-permute-start(bf16[160,1024]{1,0:T(8,128)(2,1)S(1)} %add_convert_fusion.4), channel_id=1, source_target_pairs={{0,2},{1,3},{2,0},{3,1},{4,6},{5,7},{6,4},{7,5},{8,10},{9,11},{10,... | collective-permute-start | bytes 983048 | tf_op jit(solution)/shard_map/cond/branch_0_fun/ppermute | solution.py:386
  93.2 10.0 %collective-permute-start.10 = (bf16[40,1152]{1,0:T(8,128)(2,1)S(1)}, bf16[40,1152]{1,0:T(8,128)(2,1)S(1)}, u32[]{:S(2)}, u32[]{:S(2)}) collective-permute-start(bf16[40,1152]{1,0:T(8,128)(2,1)S(1)} %get-tuple-element.124), channel_id=1, source_target_pairs={{0,4},{4,8},{8,12},{12,0},{1,5},{5,9},{9,13},{13,1},{2,6},{6,10},{... | collective-permute-start | bytes 276488 | tf_op jit(solution)/shard_map/cond/branch_0_fun/ppermute | solution.py:381
  93.6 12.5 %collective-permute-start.9 = (bf16[40,1152]{1,0:T(8,128)(2,1)S(1)}, bf16[40,1152]{1,0:T(8,128)(2,1)S(1)}, u32[]{:S(2)}, u32[]{:S(2)}) collective-permute-start(bf16[40,1152]{1,0:T(8,128)(2,1)S(1)} %get-tuple-element.125), channel_id=1, source_target_pairs={{0,8},{4,12},{8,0},{12,4},{1,9},{5,13},{9,1},{13,5},{2,10},{6,14},... | collective-permute-start | bytes 276488 | tf_op jit(solution)/shard_map/cond/branch_0_fun/ppermute | solution.py:381
  95.7 10.5 %collective-permute-start.8 = (bf16[40,1152]{1,0:T(8,128)(2,1)S(1)}, bf16[40,1152]{1,0:T(8,128)(2,1)S(1)}, u32[]{:S(2)}, u32[]{:S(2)}) collective-permute-start(bf16[40,1152]{1,0:T(8,128)(2,1)S(1)} %get-tuple-element.126), channel_id=1, source_target_pairs={{0,12},{4,0},{8,4},{12,8},{1,13},{5,1},{9,5},{13,9},{2,14},{6,2},{... | collective-permute-start | bytes 276488 | tf_op jit(solution)/shard_map/cond/branch_0_fun/ppermute | solution.py:381
  100.5 11.2 %copy-start = (bf16[16,192,2048]{2,1,0:T(8,128)(2,1)}, bf16[16,192,2048]{2,1,0:T(8,128)(2,1)S(1)}, u32[]{:S(2)}) copy-start(bf16[16,192,2048]{2,1,0:T(8,128)(2,1)S(1)} %down_grads.5) | copy-start | bytes 37748740 | tf_op jit(solution)/shard_map/cond
  101.8 6.5 %collective-permute-start.16 = (bf16[40,1024]{1,0:T(8,128)(2,1)S(1)}, bf16[40,1024]{1,0:T(8,128)(2,1)S(1)}, u32[]{:S(2)}, u32[]{:S(2)}) collective-permute-start(bf16[40,1024]{1,0:T(8,128)(2,1)S(1)} %get-tuple-element.130), channel_id=1, source_target_pairs={{0,4},{4,8},{8,12},{12,0},{1,5},{5,9},{9,13},{13,1},{2,6},{6,10},{... | collective-permute-start | bytes 245768 | tf_op jit(solution)/shard_map/cond/branch_0_fun/ppermute | solution.py:381
  101.9 8.1 %collective-permute-start.15 = (bf16[40,1024]{1,0:T(8,128)(2,1)S(1)}, bf16[40,1024]{1,0:T(8,128)(2,1)S(1)}, u32[]{:S(2)}, u32[]{:S(2)}) collective-permute-start(bf16[40,1024]{1,0:T(8,128)(2,1)S(1)} %get-tuple-element.131), channel_id=1, source_target_pairs={{0,8},{4,12},{8,0},{12,4},{1,9},{5,13},{9,1},{13,5},{2,10},{6,14},... | collective-permute-start | bytes 245768 | tf_op jit(solution)/shard_map/cond/branch_0_fun/ppermute | solution.py:381
  103.3 6.7 %collective-permute-start.14 = (bf16[40,1024]{1,0:T(8,128)(2,1)S(1)}, bf16[40,1024]{1,0:T(8,128)(2,1)S(1)}, u32[]{:S(2)}, u32[]{:S(2)}) collective-permute-start(bf16[40,1024]{1,0:T(8,128)(2,1)S(1)} %get-tuple-element.132), channel_id=1, source_target_pairs={{0,12},{4,0},{8,4},{12,8},{1,13},{5,1},{9,5},{13,9},{2,14},{6,2},{... | collective-permute-start | bytes 245768 | tf_op jit(solution)/shard_map/cond/branch_0_fun/ppermute | solution.py:381

commit v6 on v5

--- a/solution.py
+++ b/solution.py
@@ -474,7 +474,7 @@
     stay_2, go_2 = near_sums(second, n_dp)
     early = per_device // 2
     down_grad = down_layer(after(hw, go_2), cs, 0, early) if early else None
-    come_2 = far_hop(after(go_2, (come_1b, down_grad)), n_dp)
+    come_2 = far_hop(after(go_2, down_grad), n_dp)
     come_1 = jnp.concatenate([come_1, come_1b])
     home_1 = from_shards(add_rows(stay_1, come_1), room, n_shards)
     down_grad = down_layer(after(hw, go_2), cs, early, per_device - early, down_grad)

time: 112 us -> 112 us (level)
  no operation moved by 1% of the time
where the time goes in v6:
time: 112 us
  Pallas kernels  42 us (38%)
  waiting for transfers between devices  37.5 us (33%)
  starting transfers between devices  29.1 us (26%)
  between operations  1.42 us (1%)
    ppermute x13, waiting for transfers between devices, shifted(): return lax.ppermute(value, axis, [(i, (i + step) % n) for i in range(n)])  27.3 us
    ppermute x13, starting transfers between devices, shifted(): return lax.ppermute(value, axis, [(i, (i + step) % n) for i in range(n)])  22.1 us
    pallas_call x1, Pallas kernels, first_layer(): pl.pallas_call(functools.partial(first_kernel, n_dp, room, n_shards), gri...  15.2 us
    ppermute x15, waiting for transfers between devices, swapped(): return lax.ppermute(value, axis, [(i, i ^ bit) for i in range(n)])  10.2 us
    pallas_call x1, Pallas kernels, second_layer(): pl.pallas_call(functools.partial(second_kernel, n_dp, room, n_shards), gr...  9.59 us
    pallas_call x2, Pallas kernels, third_layer(): pl.pallas_call(functools.partial(third_kernel, n_dp, room, n_shards, rout...  9.35 us
    ppermute x15, starting transfers between devices, swapped(): return lax.ppermute(value, axis, [(i, i ^ bit) for i in range(n)])  6.98 us
    pallas_call x2, Pallas kernels, down_layer(): pl.pallas_call(down_kernel, grid=(count // step,), in_specs=[pl.BlockSpec...  4.04 us
  transfers between devices with their start and end apart: 28, of which 13 were waited for; matrix products, arithmetic and copies ran while one was open for 1% of the time, Pallas kernels for 21%

profile of v6, /device:TPU:0, one launch (start us, length us, event | category | flops | bytes accessed | tf_op | source)
XLA Modules:
  0.0 111.8 jit_solution(4277099393852865571)
XLA Ops:
  0.6 2.0 %pack_rows.3 = (bf16[160,2176]{1,0:T(8,128)(2,1)S(1)}, bf16[160,2048]{1,0:T(8,128)(2,1)S(1)}) custom-call(s32[1,128]{1,0:T(1,128)} %bitcast.17, bf16[128,2048]{1,0:T(8,128)(2,1)} %tok_ref.1, bf16[128,2048]{1,0:T(8,128)(2,1)} %cot_ref.1, bf16[1,128]{1,0:T(2,128)(2,1)} %bitcast.20), custom_call_target="tpu_custom_call" | custom-call | flops 400000000 | bytes 4000000 | tf_op jit(solution)/shard_map/pack_rows/pallas_call | solution.py:104
  2.7 5.1 %collective-permute-start.44 = (bf16[40,2176]{1,0:T(8,128)(2,1)S(1)}, bf16[40,2176]{1,0:T(8,128)(2,1)S(1)}, u32[]{:S(2)}, u32[]{:S(2)}) collective-permute-start(bf16[40,2176]{1,0:T(8,128)(2,1)S(1)} %get-tuple-element.153), channel_id=1, source_target_pairs={{0,12},{4,0},{8,4},{12,8},{1,13},{5,1},{9,5},{13,9},{2,14},{6,2},{... | collective-permute-start | bytes 522248 | tf_op jit(solution)/shard_map/ppermute | solution.py:381
  7.8 1.0 collective-permute-start.42
  8.8 3.9 %collective-permute-done.44 = bf16[40,2176]{1,0:T(8,128)(2,1)S(1)} collective-permute-done((bf16[40,2176]{1,0:T(8,128)(2,1)S(1)}, bf16[40,2176]{1,0:T(8,128)(2,1)S(1)}, u32[]{:S(2)}, u32[]{:S(2)}) %collective-permute-start.44) | collective-permute-done | bytes 174112 | tf_op jit(solution)/shard_map/ppermute | solution.py:381
  12.7 9.9 %collective-permute-done.43 = bf16[40,2176]{1,0:T(8,128)(2,1)S(1)} collective-permute-done((bf16[40,2176]{1,0:T(8,128)(2,1)S(1)}, bf16[40,2176]{1,0:T(8,128)(2,1)S(1)}, u32[]{:S(2)}, u32[]{:S(2)}) %collective-permute-start.43) | collective-permute-done | bytes 174112 | tf_op jit(solution)/shard_map/ppermute | solution.py:381
  22.8 1.6 %collective-permute-start.45 = (bf16[160,2176]{1,0:T(8,128)(2,1)S(1)}, bf16[160,2176]{1,0:T(8,128)(2,1)S(1)}, u32[]{:S(2)}, u32[]{:S(2)}) collective-permute-start(bf16[160,2176]{1,0:T(8,128)(2,1)S(1)} %pad_maximum_fusion.2), channel_id=1, source_target_pairs={{0,2},{1,3},{2,0},{3,1},{4,6},{5,7},{6,4},{7,5},{8,10},{9,11},{10,... | collective-permute-start | bytes 2088968 | tf_op jit(solution)/shard_map/ppermute | solution.py:386
  24.4 0.9 collective-permute-start.48
  25.3 2.0 %collective-permute-start.47 = (bf16[40,2048]{1,0:T(8,128)(2,1)S(1)}, bf16[40,2048]{1,0:T(8,128)(2,1)S(1)}, u32[]{:S(2)}, u32[]{:S(2)}) collective-permute-start(bf16[40,2048]{1,0:T(8,128)(2,1)S(1)} %get-tuple-element.158), channel_id=1, source_target_pairs={{0,8},{4,12},{8,0},{12,4},{1,9},{5,13},{9,1},{13,5},{2,10},{6,14},... | collective-permute-start | bytes 491528 | tf_op jit(solution)/shard_map/ppermute | solution.py:381
  27.3 1.9 %collective-permute-start.46 = (bf16[40,2048]{1,0:T(8,128)(2,1)S(1)}, bf16[40,2048]{1,0:T(8,128)(2,1)S(1)}, u32[]{:S(2)}, u32[]{:S(2)}) collective-permute-start(bf16[40,2048]{1,0:T(8,128)(2,1)S(1)} %get-tuple-element.159), channel_id=1, source_target_pairs={{0,4},{4,8},{8,12},{12,0},{1,5},{5,9},{9,13},{13,1},{2,6},{6,10},{... | collective-permute-start | bytes 491528 | tf_op jit(solution)/shard_map/ppermute | solution.py:381
  29.3 1.6 %collective-permute-start.50 = (f32[8,128]{1,0:T(8,128)S(1)}, f32[8,128]{1,0:T(8,128)S(1)}, u32[]{:S(2)}, u32[]{:S(2)}) collective-permute-start(f32[8,128]{1,0:T(8,128)S(1)} %broadcast_in_dim.2), channel_id=1, source_target_pairs={{0,16},{16,0},{1,17},{17,1},{2,18},{18,2},{3,19},{19,3},{4,20},{20... | collective-permute-start | bytes 12296 | tf_op jit(solution)/shard_map/ppermute | solution.py:381
  30.9 2.1 %collective-permute-done.50 = f32[8,128]{1,0:T(8,128)S(1)} collective-permute-done((f32[8,128]{1,0:T(8,128)S(1)}, f32[8,128]{1,0:T(8,128)S(1)}, u32[]{:S(2)}, u32[]{:S(2)}) %collective-permute-start.50) | collective-permute-done | bytes 4128 | tf_op jit(solution)/shard_map/ppermute | solution.py:381
  33.0 1.2 %collective-permute-done.51 = f32[8,128]{1,0:T(8,128)S(1)} collective-permute-done((f32[8,128]{1,0:T(8,128)S(1)}, f32[8,128]{1,0:T(8,128)S(1)}, u32[]{:S(2)}, u32[]{:S(2)}) %collective-permute-start.51) | collective-permute-done | bytes 4128 | tf_op jit(solution)/shard_map/ppermute | solution.py:386
  34.2 0.5 collective-permute-start.52
  34.7 7.6 %collective-permute-done.47 = bf16[40,2048]{1,0:T(8,128)(2,1)S(1)} collective-permute-done((bf16[40,2048]{1,0:T(8,128)(2,1)S(1)}, bf16[40,2048]{1,0:T(8,128)(2,1)S(1)}, u32[]{:S(2)}, u32[]{:S(2)}) %collective-permute-start.47) | collective-permute-done | bytes 163872 | tf_op jit(solution)/shard_map/ppermute | solution.py:381
  42.4 0.6 slice.123
  43.7 68.1 %conditional.1 = (bf16[128,2048]{1,0:T(8,128)(2,1)}, bf16[128,1]{0,1:T(2,128)(2,1)}, bf16[16,192,2048]{2,1,0:T(8,128)(2,1)}) conditional(s32[]{:T(128)} %bitcast.4, (bf16[160,2176]{1,0:T(8,128)(2,1)S(1)}, bf16[160,2048]{1,0:T(8,128)(2,1)S(1)}, bf16[160,2176]{1,0:T(8,128)(2,1)S(1)}, bf16[160,2176]{1,0:T(8,128)(2,1)S(1)}, ...), branch_computations={%region_1.0_spmd, %region_2.0_spmd} | conditional | flops 7616220160 | bytes 261090816 | solution.py:529
  43.7 0.6 collective-permute-start.2
  44.3 0.2 collective-permute-start.1
  44.5 1.4 %collective-permute-done.refs_3_ = bf16[160,2176]{1,0:T(8,128)(2,1)S(1)} collective-permute-done((bf16[160,2176]{1,0:T(8,128)(2,1)S(1)}, bf16[160,2176]{1,0:T(8,128)(2,1)S(1)}, u32[]{:S(2)}, u32[]{:S(2)}) %collective-permute-start) | collective-permute-done | bytes 696352 | tf_op jit(solution)/shard_map/cond/branch_0_fun/ppermute | solution.py:386
  45.9 15.2 %gate_up.2 = (f32[16,64,192]{2,1,0:T(8,128)S(1)}, f32[16,64,192]{2,1,0:T(8,128)S(1)}) custom-call(bf16[160,2176]{1,0:T(8,128)(2,1)S(1)} %get-tuple-element.31.refs_0_, bf16[160,2176]{1,0:T(8,128)(2,1)S(1)} %get-tuple-element.32.refs_1_, bf16[160,2176]{1,0:T(8,128)(2,1)S(1)} %get-tuple-element.33.refs_2_, bf16[160,2176]{1,0:T(8,128)(2,1)S(1)} %collective-permute-done.refs_3_, ...), custom_call_target="tpu_custom_call" | custom-call | flops 2000000000 | bytes 30000000 | tf_op jit(solution)/shard_map/cond/branch_0_fun/gate_up/pallas_call | solution.py:172
  61.1 0.2 collective-permute-start.3
  61.3 2.0 %collective-permute-done.3.refs_7_ = bf16[160,2048]{1,0:T(8,128)(2,1)S(1)} collective-permute-done((bf16[160,2048]{1,0:T(8,128)(2,1)S(1)}, bf16[160,2048]{1,0:T(8,128)(2,1)S(1)}, u32[]{:S(2)}, u32[]{:S(2)}) %collective-permute-start.3) | collective-permute-done | bytes 655392 | tf_op jit(solution)/shard_map/cond/branch_0_fun/ppermute | solution.py:386
  63.3 9.6 %hidden_grads.2 = (bf16[16,64,192]{2,1,0:T(8,128)(2,1)S(1)}, bf16[16,64,192]{2,1,0:T(8,128)(2,1)S(1)}, bf16[16,64,192]{2,1,0:T(8,128)(2,1)S(1)}, bf16[16,64,2048...) custom-call(bf16[160,2176]{1,0:T(8,128)(2,1)S(1)} %get-tuple-element.31.refs_0_, ...), custom_call_target="tpu_custom_call" | custom-call | flops 2000000000 | bytes 20000000 | tf_op jit(solution)/shard_map/cond/branch_0_fun/hidden_grads/pallas_call | solution.py:228
  73.0 4.7 %input_grads.4 = (bf16[160,1152]{1,0:T(8,128)(2,1)S(1)}, bf16[160,1152]{1,0:T(8,128)(2,1)S(1)}, bf16[160,1152]{1,0:T(8,128)(2,1)S(1)}, bf16[160,1152]{1,0:T(8,128)(2,1)S(1)}) custom-call(bf16[160,2176]{1,0:T(8,128)(2,1)S(1)} %get-tuple-element.31.refs_0_, bf16[160,2176]{1,0:T(8,128)(2,1)S(1)} %get-tuple-element.32.refs_1_, ...), custom_call_target="tpu_custom_call" | custom-call | flops 1000000000 | bytes 15000000 | tf_op jit(solution)/shard_map/cond/branch_0_fun/input_grads/pallas_call | solution.py:299
  77.7 0.2 collective-permute-start.5
  77.9 0.4 collective-permute-start.4
  78.3 1.2 %collective-permute-done.5 = bf16[160,1152]{1,0:T(8,128)(2,1)S(1)} collective-permute-done((bf16[160,1152]{1,0:T(8,128)(2,1)S(1)}, bf16[160,1152]{1,0:T(8,128)(2,1)S(1)}, u32[]{:S(2)}, u32[]{:S(2)}) %collective-permute-start.5) | collective-permute-done | bytes 368672 | tf_op jit(solution)/shard_map/cond/branch_0_fun/ppermute | solution.py:386
  79.6 0.6 collective-permute-start.6
  80.2 1.5 %collective-permute-start.7 = (bf16[80,1152]{1,0:T(8,128)(2,1)S(1)}, bf16[80,1152]{1,0:T(8,128)(2,1)S(1)}, u32[]{:S(2)}, u32[]{:S(2)}) collective-permute-start(bf16[80,1152]{1,0:T(8,128)(2,1)S(1)} %get-tuple-element.129), channel_id=1, source_target_pairs={{0,2},{1,3},{2,0},{3,1},{4,6},{5,7},{6,4},{7,5},{8,10},{9,11},{10,... | collective-permute-start | bytes 552968 | tf_op jit(solution)/shard_map/cond/branch_0_fun/ppermute | solution.py:386
  81.7 4.6 %input_grads.5 = (bf16[160,1024]{1,0:T(8,128)(2,1)S(1)}, bf16[160,1024]{1,0:T(8,128)(2,1)S(1)}, bf16[160,1024]{1,0:T(8,128)(2,1)S(1)}, bf16[160,1024]{1,0:T(8,128)(2,1)S(1)}) custom-call(bf16[160,2176]{1,0:T(8,128)(2,1)S(1)} %get-tuple-element.31.refs_0_, bf16[160,2176]{1,0:T(8,128)(2,1)S(1)} %get-tuple-element.32.refs_1_, ...), custom_call_target="tpu_custom_call" | custom-call | flops 1000000000 | bytes 15000000 | tf_op jit(solution)/shard_map/cond/branch_0_fun/input_grads/pallas_call | solution.py:299
  86.3 0.8 collective-permute-done.6
  87.2 0.5 collective-permute-start.12
  87.7 2.6 %collective-permute-done.7 = bf16[80,1152]{1,0:T(8,128)(2,1)S(1)} collective-permute-done((bf16[80,1152]{1,0:T(8,128)(2,1)S(1)}, bf16[80,1152]{1,0:T(8,128)(2,1)S(1)}, u32[]{:S(2)}, u32[]{:S(2)}) %collective-permute-start.7) | collective-permute-done | bytes 184352 | tf_op jit(solution)/shard_map/cond/branch_0_fun/ppermute | solution.py:386
  90.3 0.1 add_convert_fusion
  90.5 0.1 add_convert_fusion.4
  90.6 2.0 %down_grads.4.refs_2_ = bf16[16,192,2048]{2,1,0:T(8,128)(2,1)S(1)} custom-call(bf16[16,64,192]{2,1,0:T(8,128)(2,1)S(1)} %get-tuple-element.59.refs_0_, bf16[16,64,2048]{2,1,0:T(8,128)(2,1)S(1)} %get-tuple-element.60.refs_1_), custom_call_target="tpu_custom_call" | custom-call | flops 500000000 | bytes 9000000 | tf_op jit(solution)/shard_map/cond/branch_0_fun/down_grads/pallas_call | solution.py:324
  92.6 0.6 collective-permute-start.13
  93.2 0.4 collective-permute-start.10
  93.6 2.0 %collective-permute-start.9 = (bf16[40,1152]{1,0:T(8,128)(2,1)S(1)}, bf16[40,1152]{1,0:T(8,128)(2,1)S(1)}, u32[]{:S(2)}, u32[]{:S(2)}) collective-permute-start(bf16[40,1152]{1,0:T(8,128)(2,1)S(1)} %get-tuple-element.125), channel_id=1, source_target_pairs={{0,8},{4,12},{8,0},{12,4},{1,9},{5,13},{9,1},{13,5},{2,10},{6,14},... | collective-permute-start | bytes 276488 | tf_op jit(solution)/shard_map/cond/branch_0_fun/ppermute | solution.py:381
  95.7 2.8 %collective-permute-start.8 = (bf16[40,1152]{1,0:T(8,128)(2,1)S(1)}, bf16[40,1152]{1,0:T(8,128)(2,1)S(1)}, u32[]{:S(2)}, u32[]{:S(2)}) collective-permute-start(bf16[40,1152]{1,0:T(8,128)(2,1)S(1)} %get-tuple-element.126), channel_id=1, source_target_pairs={{0,12},{4,0},{8,4},{12,8},{1,13},{5,1},{9,5},{13,9},{2,14},{6,2},{... | collective-permute-start | bytes 276488 | tf_op jit(solution)/shard_map/cond/branch_0_fun/ppermute | solution.py:381
  98.5 2.0 %down_grads.5 = bf16[16,192,2048]{2,1,0:T(8,128)(2,1)S(1)} custom-call(bf16[16,64,192]{2,1,0:T(8,128)(2,1)S(1)} %get-tuple-element.59.refs_0_, bf16[16,64,2048]{2,1,0:T(8,128)(2,1)S(1)} %get-tuple-element.60.refs_1_, bf16[16,192,2048]{2,1,0:T(8,128)(2,1)S(1)} %down_grads.4.refs_2_), custom_call_target="tpu_custom_call", output_to_operand_aliasing={{}: (2, {})} | custom-call | flops 500000000 | bytes 9000000 | tf_op jit(solution)/shard_map/cond/branch_0_fun/down_grads/pallas_call | solution.py:324
  100.5 1.1 collective-permute-done.13
  101.6 0.2 add_convert_fusion.3
  101.9 1.4 %collective-permute-start.15 = (bf16[40,1024]{1,0:T(8,128)(2,1)S(1)}, bf16[40,1024]{1,0:T(8,128)(2,1)S(1)}, u32[]{:S(2)}, u32[]{:S(2)}) collective-permute-start(bf16[40,1024]{1,0:T(8,128)(2,1)S(1)} %get-tuple-element.131), channel_id=1, source_target_pairs={{0,8},{4,12},{8,0},{12,4},{1,9},{5,13},{9,1},{13,5},{2,10},{6,14},... | collective-permute-start | bytes 245768 | tf_op jit(solution)/shard_map/cond/branch_0_fun/ppermute | solution.py:381
  103.3 2.8 %collective-permute-start.14 = (bf16[40,1024]{1,0:T(8,128)(2,1)S(1)}, bf16[40,1024]{1,0:T(8,128)(2,1)S(1)}, u32[]{:S(2)}, u32[]{:S(2)}) collective-permute-start(bf16[40,1024]{1,0:T(8,128)(2,1)S(1)} %get-tuple-element.132), channel_id=1, source_target_pairs={{0,12},{4,0},{8,4},{12,8},{1,13},{5,1},{9,5},{13,9},{2,14},{6,2},{... | collective-permute-start | bytes 245768 | tf_op jit(solution)/shard_map/cond/branch_0_fun/ppermute | solution.py:381
  106.1 2.2 %collective-permute-done.16.refs_7_ = bf16[40,1024]{1,0:T(8,128)(2,1)S(1)} collective-permute-done((bf16[40,1024]{1,0:T(8,128)(2,1)S(1)}, bf16[40,1024]{1,0:T(8,128)(2,1)S(1)}, u32[]{:S(2)}, u32[]{:S(2)}) %collective-permute-start.16) | collective-permute-done | bytes 81952 | tf_op jit(solution)/shard_map/cond/branch_0_fun/ppermute | solution.py:381
  108.3 1.7 %collective-permute-done.15.refs_6_ = bf16[40,1024]{1,0:T(8,128)(2,1)S(1)} collective-permute-done((bf16[40,1024]{1,0:T(8,128)(2,1)S(1)}, bf16[40,1024]{1,0:T(8,128)(2,1)S(1)}, u32[]{:S(2)}, u32[]{:S(2)}) %collective-permute-start.15) | collective-permute-done | bytes 81952 | tf_op jit(solution)/shard_map/cond/branch_0_fun/ppermute | solution.py:381
  110.0 1.8 %home_rows.2 = (bf16[128,2048]{1,0:T(8,128)(2,1)}, bf16[1,128]{1,0:T(2,128)(2,1)}) custom-call(s32[1,128]{1,0:T(1,128)S(1)} %get-tuple-element.30.ids_ref, bf16[40,1152]{1,0:T(8,128)(2,1)S(1)} %get-tuple-element.127.refs_0_, bf16[40,1152]{1,0:T(8,128)(2,1)S(1)} %collective-permute-done.8.refs_1_, bf16[40,1152]{1,0:T(8,128)(2,1)S(1)} %collective-permute-done.9.refs_2_, ...), custom_call_target="tpu_custom_call" | custom-call | flops 200000000 | bytes 2000000 | tf_op jit(solution)/shard_map/cond/branch_0_fun/home_rows/pallas_call | solution.py:361
  (58 shorter events, 0.7 us)
Async XLA Ops:
  2.7 10.0 %collective-permute-start.44 = (bf16[40,2176]{1,0:T(8,128)(2,1)S(1)}, bf16[40,2176]{1,0:T(8,128)(2,1)S(1)}, u32[]{:S(2)}, u32[]{:S(2)}) collective-permute-start(bf16[40,2176]{1,0:T(8,128)(2,1)S(1)} %get-tuple-element.153), channel_id=1, source_target_pairs={{0,12},{4,0},{8,4},{12,8},{1,13},{5,1},{9,5},{13,9},{2,14},{6,2},{... | collective-permute-start | bytes 522248 | tf_op jit(solution)/shard_map/ppermute | solution.py:381
  7.8 14.8 %collective-permute-start.43 = (bf16[40,2176]{1,0:T(8,128)(2,1)S(1)}, bf16[40,2176]{1,0:T(8,128)(2,1)S(1)}, u32[]{:S(2)}, u32[]{:S(2)}) collective-permute-start(bf16[40,2176]{1,0:T(8,128)(2,1)S(1)} %get-tuple-element.154), channel_id=1, source_target_pairs={{0,8},{4,12},{8,0},{12,4},{1,9},{5,13},{9,1},{13,5},{2,10},{6,14},... | collective-permute-start | bytes 522248 | tf_op jit(solution)/shard_map/ppermute | solution.py:381
  7.8 14.8 %collective-permute-start.42 = (bf16[40,2176]{1,0:T(8,128)(2,1)S(1)}, bf16[40,2176]{1,0:T(8,128)(2,1)S(1)}, u32[]{:S(2)}, u32[]{:S(2)}) collective-permute-start(bf16[40,2176]{1,0:T(8,128)(2,1)S(1)} %get-tuple-element.155), channel_id=1, source_target_pairs={{0,4},{4,8},{8,12},{12,0},{1,5},{5,9},{9,13},{13,1},{2,6},{6,10},{... | collective-permute-start | bytes 522248 | tf_op jit(solution)/shard_map/ppermute | solution.py:381
  22.6 21.0 %copy-start.2 = (s32[128,1]{0,1:T(1,128)S(1)}, s32[128,1]{0,1:T(1,128)}, u32[]{:S(2)}) copy-start(s32[128,1]{0,1:T(1,128)} %param.12) | copy-start | bytes 1540
  22.7 21.0 %copy-start.3 = (bf16[128,2048]{1,0:T(8,128)(2,1)S(1)}, bf16[128,2048]{1,0:T(8,128)(2,1)}, u32[]{:S(2)}) copy-start(bf16[128,2048]{1,0:T(8,128)(2,1)} %tok_ref.1) | copy-start | bytes 1572868
  22.7 21.0 %copy-start.4 = (bf16[128,2048]{1,0:T(8,128)(2,1)S(1)}, bf16[128,2048]{1,0:T(8,128)(2,1)}, u32[]{:S(2)}) copy-start(bf16[128,2048]{1,0:T(8,128)(2,1)} %cot_ref.1) | copy-start | bytes 1572868
  22.7 21.0 %copy-start.5 = (bf16[128,1]{0,1:T(2,128)(2,1)S(1)}, bf16[128,1]{0,1:T(2,128)(2,1)}, u32[]{:S(2)}) copy-start(bf16[128,1]{0,1:T(2,128)(2,1)} %param.11) | copy-start | bytes 772
  22.7 6.6 %collective-permute-start.49 = (bf16[160,2176]{1,0:T(8,128)(2,1)S(1)}, bf16[160,2176]{1,0:T(8,128)(2,1)S(1)}, u32[]{:S(2)}, u32[]{:S(2)}) collective-permute-start(bf16[160,2176]{1,0:T(8,128)(2,1)S(1)} %pad_maximum_fusion.2), channel_id=1, source_target_pairs={{0,1},{1,0},{2,3},{3,2},{4,5},{5,4},{6,7},{7,6},{8,9},{9,8},{10,11... | collective-permute-start | bytes 2088968 | tf_op jit(solution)/shard_map/ppermute | solution.py:386
  22.8 19.6 %collective-permute-start.45 = (bf16[160,2176]{1,0:T(8,128)(2,1)S(1)}, bf16[160,2176]{1,0:T(8,128)(2,1)S(1)}, u32[]{:S(2)}, u32[]{:S(2)}) collective-permute-start(bf16[160,2176]{1,0:T(8,128)(2,1)S(1)} %pad_maximum_fusion.2), channel_id=1, source_target_pairs={{0,2},{1,3},{2,0},{3,1},{4,6},{5,7},{6,4},{7,5},{8,10},{9,11},{10,... | collective-permute-start | bytes 2088968 | tf_op jit(solution)/shard_map/ppermute | solution.py:386
  24.4 10.3 %collective-permute-start.48 = (bf16[40,2048]{1,0:T(8,128)(2,1)S(1)}, bf16[40,2048]{1,0:T(8,128)(2,1)S(1)}, u32[]{:S(2)}, u32[]{:S(2)}) collective-permute-start(bf16[40,2048]{1,0:T(8,128)(2,1)S(1)} %get-tuple-element.157), channel_id=1, source_target_pairs={{0,12},{4,0},{8,4},{12,8},{1,13},{5,1},{9,5},{13,9},{2,14},{6,2},{... | collective-permute-start | bytes 491528 | tf_op jit(solution)/shard_map/ppermute | solution.py:381
  25.3 17.0 %collective-permute-start.47 = (bf16[40,2048]{1,0:T(8,128)(2,1)S(1)}, bf16[40,2048]{1,0:T(8,128)(2,1)S(1)}, u32[]{:S(2)}, u32[]{:S(2)}) collective-permute-start(bf16[40,2048]{1,0:T(8,128)(2,1)S(1)} %get-tuple-element.158), channel_id=1, source_target_pairs={{0,8},{4,12},{8,0},{12,4},{1,9},{5,13},{9,1},{13,5},{2,10},{6,14},... | collective-permute-start | bytes 491528 | tf_op jit(solution)/shard_map/ppermute | solution.py:381
  27.3 15.0 %collective-permute-start.46 = (bf16[40,2048]{1,0:T(8,128)(2,1)S(1)}, bf16[40,2048]{1,0:T(8,128)(2,1)S(1)}, u32[]{:S(2)}, u32[]{:S(2)}) collective-permute-start(bf16[40,2048]{1,0:T(8,128)(2,1)S(1)} %get-tuple-element.159), channel_id=1, source_target_pairs={{0,4},{4,8},{8,12},{12,0},{1,5},{5,9},{9,13},{13,1},{2,6},{6,10},{... | collective-permute-start | bytes 491528 | tf_op jit(solution)/shard_map/ppermute | solution.py:381
  29.3 3.7 %collective-permute-start.50 = (f32[8,128]{1,0:T(8,128)S(1)}, f32[8,128]{1,0:T(8,128)S(1)}, u32[]{:S(2)}, u32[]{:S(2)}) collective-permute-start(f32[8,128]{1,0:T(8,128)S(1)} %broadcast_in_dim.2), channel_id=1, source_target_pairs={{0,16},{16,0},{1,17},{17,1},{2,18},{18,2},{3,19},{19,3},{4,20},{20... | collective-permute-start | bytes 12296 | tf_op jit(solution)/shard_map/ppermute | solution.py:381
  33.0 1.2 %collective-permute-start.51 = (f32[8,128]{1,0:T(8,128)S(1)}, f32[8,128]{1,0:T(8,128)S(1)}, u32[]{:S(2)}, u32[]{:S(2)}) collective-permute-start(f32[8,128]{1,0:T(8,128)S(1)} %max.9), channel_id=1, source_target_pairs={{0,1},{1,0},{2,3},{3,2},{4,5},{5,4},{6,7},{7,6},{8,9},{9,8},{10,11... | collective-permute-start | bytes 12296 | tf_op jit(solution)/shard_map/ppermute | solution.py:386
  34.2 8.2 %collective-permute-start.52 = (f32[8,128]{1,0:T(8,128)S(1)}, f32[8,128]{1,0:T(8,128)S(1)}, u32[]{:S(2)}, u32[]{:S(2)}) collective-permute-start(f32[8,128]{1,0:T(8,128)S(1)} %max.10), channel_id=1, source_target_pairs={{0,2},{1,3},{2,0},{3,1},{4,6},{5,7},{6,4},{7,5},{8,10},{9,11},{10,... | collective-permute-start | bytes 12296 | tf_op jit(solution)/shard_map/ppermute | solution.py:386
  43.7 2.2 %collective-permute-start = (bf16[160,2176]{1,0:T(8,128)(2,1)S(1)}, bf16[160,2176]{1,0:T(8,128)(2,1)S(1)}, u32[]{:S(2)}, u32[]{:S(2)}) collective-permute-start(bf16[160,2176]{1,0:T(8,128)(2,1)S(1)} %get-tuple-element.33.refs_2_), channel_id=1, source_target_pairs={{0,1},{1,0},{2,3},{3,2},{4,5},{5,4},{6,7},{7,6},{8,9},{9,8},{10,11... | collective-permute-start | bytes 2088968 | tf_op jit(solution)/shard_map/cond/branch_0_fun/ppermute | solution.py:386
  43.7 17.4 %collective-permute-start.2 = (bf16[160,2048]{1,0:T(8,128)(2,1)S(1)}, bf16[160,2048]{1,0:T(8,128)(2,1)S(1)}, u32[]{:S(2)}, u32[]{:S(2)}) collective-permute-start(bf16[160,2048]{1,0:T(8,128)(2,1)S(1)} %get-tuple-element.34.refs_4_), channel_id=1, source_target_pairs={{0,2},{1,3},{2,0},{3,1},{4,6},{5,7},{6,4},{7,5},{8,10},{9,11},{10,... | collective-permute-start | bytes 1966088 | tf_op jit(solution)/shard_map/cond/branch_0_fun/ppermute | solution.py:386
  44.3 17.0 %collective-permute-start.1 = (bf16[160,2048]{1,0:T(8,128)(2,1)S(1)}, bf16[160,2048]{1,0:T(8,128)(2,1)S(1)}, u32[]{:S(2)}, u32[]{:S(2)}) collective-permute-start(bf16[160,2048]{1,0:T(8,128)(2,1)S(1)} %get-tuple-element.34.refs_4_), channel_id=1, source_target_pairs={{0,1},{1,0},{2,3},{3,2},{4,5},{5,4},{6,7},{7,6},{8,9},{9,8},{10,11... | collective-permute-start | bytes 1966088 | tf_op jit(solution)/shard_map/cond/branch_0_fun/ppermute | solution.py:386
  45.9 27.0 %slice-start = ((s8[12582912]{0:T(1024)(128)(4,1)}), s8[4194304]{0:T(1024)(128)(4,1)S(1)}, s32[]{:S(2)}) async-start(s8[12582912]{0:T(1024)(128)(4,1)} %bitcast.9), calls=%async_computation | async-start | bytes 8388608 | tf_op jit(solution)/shard_map/cond
  45.9 27.0 %slice-start.1 = ((s8[12582912]{0:T(1024)(128)(4,1)}), s8[4194304]{0:T(1024)(128)(4,1)S(1)}, s32[]{:S(2)}) async-start(s8[12582912]{0:T(1024)(128)(4,1)} %bitcast.9), calls=%async_computation.1 | async-start | bytes 8388608 | tf_op jit(solution)/shard_map/cond
  45.9 27.0 %slice-start.6 = ((s8[12582912]{0:T(1024)(128)(4,1)}), s8[4194304]{0:T(1024)(128)(4,1)S(1)}, s32[]{:S(2)}) async-start(s8[12582912]{0:T(1024)(128)(4,1)} %bitcast.15), calls=%async_computation.6 | async-start | bytes 8388608 | tf_op jit(solution)/shard_map/cond
  45.9 27.1 %slice-start.7 = ((s8[12582912]{0:T(1024)(128)(4,1)}), s8[4194304]{0:T(1024)(128)(4,1)S(1)}, s32[]{:S(2)}) async-start(s8[12582912]{0:T(1024)(128)(4,1)} %bitcast.15), calls=%async_computation.7 | async-start | bytes 8388608 | tf_op jit(solution)/shard_map/cond
  61.1 2.2 %collective-permute-start.3 = (bf16[160,2048]{1,0:T(8,128)(2,1)S(1)}, bf16[160,2048]{1,0:T(8,128)(2,1)S(1)}, u32[]{:S(2)}, u32[]{:S(2)}) collective-permute-start(bf16[160,2048]{1,0:T(8,128)(2,1)S(1)} %collective-permute-done.2.refs_6_), channel_id=1, source_target_pairs={{0,1},{1,0},{2,3},{3,2},{4,5},{5,4},{6,7},{7,6},{8,9},{9,8},{10,11... | collective-permute-start | bytes 1966088 | tf_op jit(solution)/shard_map/cond/branch_0_fun/ppermute | solution.py:386
  63.3 9.6 %slice-start.2 = ((s8[12582912]{0:T(1024)(128)(4,1)}), s8[4194304]{0:T(1024)(128)(4,1)S(1)}, s32[]{:S(2)}) async-start(s8[12582912]{0:T(1024)(128)(4,1)} %bitcast.9), calls=%async_computation.2 | async-start | bytes 8388608 | tf_op jit(solution)/shard_map/cond
  63.3 9.7 %slice-start.8 = ((s8[12582912]{0:T(1024)(128)(4,1)}), s8[4194304]{0:T(1024)(128)(4,1)S(1)}, s32[]{:S(2)}) async-start(s8[12582912]{0:T(1024)(128)(4,1)} %bitcast.15), calls=%async_computation.8 | async-start | bytes 8388608 | tf_op jit(solution)/shard_map/cond
  77.7 1.8 %collective-permute-start.5 = (bf16[160,1152]{1,0:T(8,128)(2,1)S(1)}, bf16[160,1152]{1,0:T(8,128)(2,1)S(1)}, u32[]{:S(2)}, u32[]{:S(2)}) collective-permute-start(bf16[160,1152]{1,0:T(8,128)(2,1)S(1)} %get-tuple-element.47), channel_id=1, source_target_pairs={{0,1},{1,0},{2,3},{3,2},{4,5},{5,4},{6,7},{7,6},{8,9},{9,8},{10,11... | collective-permute-start | bytes 1105928 | tf_op jit(solution)/shard_map/cond/branch_0_fun/ppermute | solution.py:386
  77.9 9.7 %collective-permute-start.4 = (bf16[160,1152]{1,0:T(8,128)(2,1)S(1)}, bf16[160,1152]{1,0:T(8,128)(2,1)S(1)}, u32[]{:S(2)}, u32[]{:S(2)}) collective-permute-start(bf16[160,1152]{1,0:T(8,128)(2,1)S(1)} %get-tuple-element.45), channel_id=1, source_target_pairs={{0,1},{1,0},{2,3},{3,2},{4,5},{5,4},{6,7},{7,6},{8,9},{9,8},{10,11... | collective-permute-start | bytes 1105928 | tf_op jit(solution)/shard_map/cond/branch_0_fun/ppermute | solution.py:386
  79.6 7.5 %collective-permute-start.6 = (bf16[80,1152]{1,0:T(8,128)(2,1)S(1)}, bf16[80,1152]{1,0:T(8,128)(2,1)S(1)}, u32[]{:S(2)}, u32[]{:S(2)}) collective-permute-start(bf16[80,1152]{1,0:T(8,128)(2,1)S(1)} %get-tuple-element.128), channel_id=1, source_target_pairs={{0,2},{1,3},{2,0},{3,1},{4,6},{5,7},{6,4},{7,5},{8,10},{9,11},{10,... | collective-permute-start | bytes 552968 | tf_op jit(solution)/shard_map/cond/branch_0_fun/ppermute | solution.py:386
  80.2 10.1 %collective-permute-start.7 = (bf16[80,1152]{1,0:T(8,128)(2,1)S(1)}, bf16[80,1152]{1,0:T(8,128)(2,1)S(1)}, u32[]{:S(2)}, u32[]{:S(2)}) collective-permute-start(bf16[80,1152]{1,0:T(8,128)(2,1)S(1)} %get-tuple-element.129), channel_id=1, source_target_pairs={{0,2},{1,3},{2,0},{3,1},{4,6},{5,7},{6,4},{7,5},{8,10},{9,11},{10,... | collective-permute-start | bytes 552968 | tf_op jit(solution)/shard_map/cond/branch_0_fun/ppermute | solution.py:386
  87.2 14.4 %collective-permute-start.11 = (bf16[160,1024]{1,0:T(8,128)(2,1)S(1)}, bf16[160,1024]{1,0:T(8,128)(2,1)S(1)}, u32[]{:S(2)}, u32[]{:S(2)}) collective-permute-start(bf16[160,1024]{1,0:T(8,128)(2,1)S(1)} %get-tuple-element.55), channel_id=1, source_target_pairs={{0,1},{1,0},{2,3},{3,2},{4,5},{5,4},{6,7},{7,6},{8,9},{9,8},{10,11... | collective-permute-start | bytes 983048 | tf_op jit(solution)/shard_map/cond/branch_0_fun/ppermute | solution.py:386
  87.2 3.3 %collective-permute-start.12 = (bf16[160,1024]{1,0:T(8,128)(2,1)S(1)}, bf16[160,1024]{1,0:T(8,128)(2,1)S(1)}, u32[]{:S(2)}, u32[]{:S(2)}) collective-permute-start(bf16[160,1024]{1,0:T(8,128)(2,1)S(1)} %get-tuple-element.57), channel_id=1, source_target_pairs={{0,1},{1,0},{2,3},{3,2},{4,5},{5,4},{6,7},{7,6},{8,9},{9,8},{10,11... | collective-permute-start | bytes 983048 | tf_op jit(solution)/shard_map/cond/branch_0_fun/ppermute | solution.py:386
  92.6 9.0 %collective-permute-start.13 = (bf16[160,1024]{1,0:T(8,128)(2,1)S(1)}, bf16[160,1024]{1,0:T(8,128)(2,1)S(1)}, u32[]{:S(2)}, u32[]{:S(2)}) collective-permute-start(bf16[160,1024]{1,0:T(8,128)(2,1)S(1)} %add_convert_fusion.4), channel_id=1, source_target_pairs={{0,2},{1,3},{2,0},{3,1},{4,6},{5,7},{6,4},{7,5},{8,10},{9,11},{10,... | collective-permute-start | bytes 983048 | tf_op jit(solution)/shard_map/cond/branch_0_fun/ppermute | solution.py:386
  93.2 10.0 %collective-permute-start.10 = (bf16[40,1152]{1,0:T(8,128)(2,1)S(1)}, bf16[40,1152]{1,0:T(8,128)(2,1)S(1)}, u32[]{:S(2)}, u32[]{:S(2)}) collective-permute-start(bf16[40,1152]{1,0:T(8,128)(2,1)S(1)} %get-tuple-element.124), channel_id=1, source_target_pairs={{0,4},{4,8},{8,12},{12,0},{1,5},{5,9},{9,13},{13,1},{2,6},{6,10},{... | collective-permute-start | bytes 276488 | tf_op jit(solution)/shard_map/cond/branch_0_fun/ppermute | solution.py:381
  93.6 12.5 %collective-permute-start.9 = (bf16[40,1152]{1,0:T(8,128)(2,1)S(1)}, bf16[40,1152]{1,0:T(8,128)(2,1)S(1)}, u32[]{:S(2)}, u32[]{:S(2)}) collective-permute-start(bf16[40,1152]{1,0:T(8,128)(2,1)S(1)} %get-tuple-element.125), channel_id=1, source_target_pairs={{0,8},{4,12},{8,0},{12,4},{1,9},{5,13},{9,1},{13,5},{2,10},{6,14},... | collective-permute-start | bytes 276488 | tf_op jit(solution)/shard_map/cond/branch_0_fun/ppermute | solution.py:381
  95.7 10.5 %collective-permute-start.8 = (bf16[40,1152]{1,0:T(8,128)(2,1)S(1)}, bf16[40,1152]{1,0:T(8,128)(2,1)S(1)}, u32[]{:S(2)}, u32[]{:S(2)}) collective-permute-start(bf16[40,1152]{1,0:T(8,128)(2,1)S(1)} %get-tuple-element.126), channel_id=1, source_target_pairs={{0,12},{4,0},{8,4},{12,8},{1,13},{5,1},{9,5},{13,9},{2,14},{6,2},{... | collective-permute-start | bytes 276488 | tf_op jit(solution)/shard_map/cond/branch_0_fun/ppermute | solution.py:381
  100.5 11.2 %copy-start = (bf16[16,192,2048]{2,1,0:T(8,128)(2,1)}, bf16[16,192,2048]{2,1,0:T(8,128)(2,1)S(1)}, u32[]{:S(2)}) copy-start(bf16[16,192,2048]{2,1,0:T(8,128)(2,1)S(1)} %down_grads.5) | copy-start | bytes 37748740 | tf_op jit(solution)/shard_map/cond
  101.8 6.5 %collective-permute-start.16 = (bf16[40,1024]{1,0:T(8,128)(2,1)S(1)}, bf16[40,1024]{1,0:T(8,128)(2,1)S(1)}, u32[]{:S(2)}, u32[]{:S(2)}) collective-permute-start(bf16[40,1024]{1,0:T(8,128)(2,1)S(1)} %get-tuple-element.130), channel_id=1, source_target_pairs={{0,4},{4,8},{8,12},{12,0},{1,5},{5,9},{9,13},{13,1},{2,6},{6,10},{... | collective-permute-start | bytes 245768 | tf_op jit(solution)/shard_map/cond/branch_0_fun/ppermute | solution.py:381
  101.9 8.1 %collective-permute-start.15 = (bf16[40,1024]{1,0:T(8,128)(2,1)S(1)}, bf16[40,1024]{1,0:T(8,128)(2,1)S(1)}, u32[]{:S(2)}, u32[]{:S(2)}) collective-permute-start(bf16[40,1024]{1,0:T(8,128)(2,1)S(1)} %get-tuple-element.131), channel_id=1, source_target_pairs={{0,8},{4,12},{8,0},{12,4},{1,9},{5,13},{9,1},{13,5},{2,10},{6,14},... | collective-permute-start | bytes 245768 | tf_op jit(solution)/shard_map/cond/branch_0_fun/ppermute | solution.py:381
  103.3 6.7 %collective-permute-start.14 = (bf16[40,1024]{1,0:T(8,128)(2,1)S(1)}, bf16[40,1024]{1,0:T(8,128)(2,1)S(1)}, u32[]{:S(2)}, u32[]{:S(2)}) collective-permute-start(bf16[40,1024]{1,0:T(8,128)(2,1)S(1)} %get-tuple-element.132), channel_id=1, source_target_pairs={{0,12},{4,0},{8,4},{12,8},{1,13},{5,1},{9,5},{13,9},{2,14},{6,2},{... | collective-permute-start | bytes 245768 | tf_op jit(solution)/shard_map/cond/branch_0_fun/ppermute | solution.py:381
